TPU v7x, 128 devices: a whole 4x4x4 slice. The times are simulated.
128 devices in a mesh: gx: 8 (over z, core), gy: 16 (over y, x).
Axes of the slice: x: 4, y: 4, z: 4, core: 2. Of those that a mesh axis runs over, the one named last changes fastest.
Arguments:
- tokens: bfloat16 [2, 512, 18432], P(None, 'gy', 'gx'), may hold values from -250 to 250
- norm_gain: float32 [18432], P('gx'), may hold values from 0.25 to 1.75
- w_query: bfloat16 [18432, 12288], P('gx', 'gy'), may hold values from -0.046875 to 0.046875
- w_kv: bfloat16 [18432, 512], P('gx'), may hold values from -0.046875 to 0.046875
- w_out: bfloat16 [12288, 18432], P('gy', 'gx'), may hold values from -0.0546875 to 0.0546875
- cache_keys: bfloat16 [512, 2048, 256], P(('gx', 'gy')), may hold values from -1000 to 1000
- cache_values: bfloat16 [512, 2048, 256], P(('gx', 'gy')), may hold values from -6 to 6
- lengths: int32 [512], P(('gx', 'gy')), may hold values from 1024 to 2048, as said below
Outputs:
- attn_branch: bfloat16 [2, 512, 18432], P(None, 'gy', 'gx')
Inputs may be any that keep to these rules, and one draw needn't show every extreme that they name: `lengths`: each row's valid cache length; some row holds exactly 2048 and some exactly 1024.
All inputs are finite; a program needn't handle non-finite values.
Results may differ from a plain program's by a relative error of at most 0.02.
The roundings to bfloat16 on the way count: a program that leaves them out, or rounds other values in their place, can miss the bound.
Values may be sent and summed in bfloat16 or wider, within the bound.
No kernel may reach another device: no remote copies, remote signals or barrier semaphores. Data moves between devices by JAX's collectives and lax.ppermute only.
A program may use at most 128 MiB of HBM per device.

v0:
```python
import jax
import jax.numpy as jnp
from jax import lax
from jax.sharding import PartitionSpec as P

D = 18432
HEADS = 48
HEAD_DIM = 256


def attend(query, keys_all, values_all, lens_here, new_keys, new_values):
    factor = query.shape[-1] ** (-0.5)
    scores_c = (
        jnp.einsum("rhd,rld->rhl", query, keys_all, preferred_element_type=jnp.float32) * factor
    )
    position = jnp.arange(keys_all.shape[1], dtype=jnp.int32)
    usable = position[None, None, :] < lens_here[:, None, None]
    scores_c = jnp.where(usable, scores_c, -1e30)
    scores_n = (
        jnp.einsum("rhd,rsd->rhs", query, new_keys, preferred_element_type=jnp.float32) * factor
    )
    highest = jnp.maximum(jnp.max(scores_c, axis=-1), jnp.max(scores_n, axis=-1))[..., None]
    exp_c = jnp.exp(scores_c - highest)
    exp_n = jnp.exp(scores_n - highest)
    totals = jnp.sum(exp_c, axis=-1, keepdims=True) + jnp.sum(exp_n, axis=-1, keepdims=True)
    weight_c = (exp_c / totals).astype(jnp.bfloat16)
    weight_n = (exp_n / totals).astype(jnp.bfloat16)
    result = jnp.einsum("rhl,rld->rhd", weight_c, values_all, preferred_element_type=jnp.float32)
    result = result + jnp.einsum(
        "rhs,rsd->rhd", weight_n, new_values, preferred_element_type=jnp.float32
    )
    return result.reshape(result.shape[0], -1).astype(jnp.bfloat16)


def per_device(tokens, norm_gain, w_query, w_kv, w_out, cache_keys, cache_values, lengths):
    local_rows = cache_keys.shape[0]
    kept_keys = []
    kept_values = []
    results = []
    for section in range(2):
        values_f = tokens[section : section + 1].astype(jnp.float32)
        feat_sums, feat_squares = lax.psum(
            (jnp.sum(values_f, axis=-1), jnp.sum(values_f * values_f, axis=-1)), "gx"
        )
        average = feat_sums / D
        spread = feat_squares / D - average * average
        scaled = (values_f - average[..., None]) * lax.rsqrt(spread[..., None] + 1e-05)
        normed = (scaled * norm_gain[None, None, :]).astype(jnp.bfloat16)
        gathered = lax.all_gather(normed, "gy", axis=1, tiled=True)
        query_part = jnp.einsum(
            "sbd,dc->sbc", gathered, w_query, preferred_element_type=jnp.float32
        )
        kv_part = jnp.einsum("sbd,dc->sbc", gathered, w_kv, preferred_element_type=jnp.float32)
        query_sum = lax.psum_scatter(query_part, "gx", scatter_dimension=1, tiled=True)
        kv_sum = lax.psum_scatter(kv_part, "gx", scatter_dimension=1, tiled=True)
        kv_sum = lax.dynamic_slice_in_dim(kv_sum, lax.axis_index("gy") * local_rows, local_rows, 1)
        key_value = kv_sum.astype(jnp.bfloat16)
        project_query_rows = lax.all_to_all(
            query_sum.astype(jnp.bfloat16), "gy", split_axis=1, concat_axis=2, tiled=True
        )
        fresh_keys = key_value[..., :HEAD_DIM]
        fresh_values = key_value[..., HEAD_DIM:]
        kept_keys.append(fresh_keys[0])
        kept_values.append(fresh_values[0])
        heads_query_rows = project_query_rows[0]
        mixed = attend(
            heads_query_rows.reshape(local_rows, HEADS, HEAD_DIM),
            cache_keys,
            cache_values,
            lengths,
            jnp.stack(kept_keys, axis=1),
            jnp.stack(kept_values, axis=1),
        )
        finish_mixed = mixed[None]
        head_cols = lax.all_to_all(finish_mixed, "gy", split_axis=2, concat_axis=1, tiled=True)
        partial_out = jnp.einsum(
            "sbc,cd->sbd",
            lax.all_gather(head_cols, "gx", axis=1, tiled=True),
            w_out,
            preferred_element_type=jnp.float32,
        )
        results.append(
            lax.psum_scatter(
                partial_out.astype(jnp.bfloat16), "gy", scatter_dimension=1, tiled=True
            )
        )
    return jnp.concatenate(results, axis=0)


def solution(mesh):
    in_specs = (
        P(None, "gy", "gx"),
        P("gx"),
        P("gx", "gy"),
        P("gx", None),
        P("gy", "gx"),
        P(("gx", "gy"), None, None),
        P(("gx", "gy"), None, None),
        P(("gx", "gy")),
    )
    out_specs = P(None, "gy", "gx")
    return jax.shard_map(
        per_device, mesh=mesh, in_specs=in_specs, out_specs=out_specs, check_vma=False
    )
```

profile of v0, /device:TPU:24, one launch (start us, length us, event | category | flops | bytes accessed | tf_op | source)
XLA Modules:
  0.0 661.5 jit_solution(10260797901266585309)
XLA Ops:
  6.5 1.3 convert_reduce_fusion.1
  7.9 16.5 %all-reduce = (f32[1,32]{1,0:T(1,128)}, f32[1,32]{1,0:T(1,128)}, f32[1,32]{1,0:T(1,128)}, f32[1,32]{1,0:T(1,128)}) all-reduce(f32[1,32]{1,0:T(1,128)S(1)} %bitcast.132, f32[1,32]{1,0:T(1,128)S(1)} %bitcast.133, f32[1,32]{1,0:T(1,128)S(1)} %bitcast.131, f32[1,32]{1,0:T(1,128)S(1)} %bitcast.130), channel_id=1, replica_groups=mesh['gx'=8,'gy'=16] {'gx'}, use_global_device_ids=true, to_apply=%region_12.13 | all-reduce | flops 128 | bytes 1024 | tf_op jit(solution)/shard_map/psum | solution.py:42
  25.1 1.9 fusion.36
  27.8 43.2 %all-gather.5.cloned.1.call-done = bf16[1,512,2304]{2,1,0:T(8,128)(2,1)} async-done(((bf16[1,32,2304]{2,1,0:T(8,128)(2,1)}), bf16[1,512,2304]{2,1,0:T(8,128)(2,1)}) %all-gather.5.cloned.1.call-update) | async-done | bytes 2359312 | tf_op jit(solution)/shard_map/all_gather | solution.py:49
  70.9 4.7 fusion.23
  75.8 42.3 %all-gather.3.cloned.1.call-done = bf16[1,512,2304]{2,1,0:T(8,128)(2,1)} async-done(((bf16[1,32,2304]{2,1,0:T(8,128)(2,1)}), bf16[1,512,2304]{2,1,0:T(8,128)(2,1)}) %all-gather.3.cloned.1.call-update) | async-done | bytes 2359312 | tf_op jit(solution)/shard_map/all_gather | solution.py:49
  118.0 4.8 fusion.20
  122.9 5.9 fusion.15
  128.9 6.0 fusion.12
  134.9 17.4 %reduce-scatter.15.cloned.1.call-done = f32[1,64,512]{2,1,0:T(8,128)} async-done(((f32[1,512,512]{2,1,0:T(8,128)}), f32[1,64,512]{2,1,0:T(8,128)}) %reduce-scatter.15.cloned.1.call-update) | async-done | bytes 131088 | tf_op jit(solution)/shard_map/reduce_scatter | solution.py:55
  153.6 31.8 %reduce-scatter.9.cloned.1.call-done = f32[1,64,512]{2,1,0:T(8,128)} async-done(((f32[1,512,512]{2,1,0:T(8,128)}), f32[1,64,512]{2,1,0:T(8,128)}) %reduce-scatter.9.cloned.1.call-update) | async-done | bytes 131088 | tf_op jit(solution)/shard_map/reduce_scatter | solution.py:55
  186.7 1.3 pad_maximum_fusion.1
  188.0 31.3 %reduce-scatter.13.cloned.1.call-done = f32[1,64,768]{2,1,0:T(8,128)} async-done(((f32[1,512,768]{2,1,0:T(8,128)}), f32[1,64,768]{2,1,0:T(8,128)}) %reduce-scatter.13.cloned.1.call-update) | async-done | bytes 196624 | tf_op jit(solution)/shard_map/reduce_scatter | solution.py:54
  219.3 0.9 convert_element_type.87
  220.3 0.8 copy.59
  221.6 2.6 reduce.8
  224.2 1.6 reshape.163
  225.8 7.2 %all-to-all-start.2 = ((bf16[16,2,1536]{2,1,0:T(2,128)(2,1)}), bf16[16,2,1536]{2,1,0:T(2,128)(2,1)}, u32[]{:S(2)}, u32[]{:S(2)}) async-start(bf16[16,2,1536]{2,1,0:T(2,128)(2,1)} %reshape.163), calls=%async_computation.6 | async-start | bytes 196608 | tf_op jit(solution)/shard_map/all_to_all | solution.py:58
  233.7 5.1 all-to-all-done.2
  238.8 1.6 reshape.164
  240.4 2.1 bitcast_reduce_fusion.1
  242.5 1.6 all_to_all.56
  244.1 1.5 copy.33
  245.6 1.6 reshape_squeeze.7
  247.2 1.0 fusion.53
  248.3 3.9 fusion.52
  252.8 1.5 fusion.27
  254.3 1.6 convert_element_type.92
  255.9 12.3 %copy.36 = bf16[1,4,12288]{1,0,2:T(2,128)(2,1)} copy(bf16[1,4,12288]{2,1,0:T(4,128)(2,1)} %convert_element_type.92) | data formatting | bytes 196608 | tf_op jit(solution)/shard_map/convert_element_type | solution.py:32
  268.2 68.6 %reduce.9 = bf16[12288,4]{1,0:T(8,128)(2,1)} reduce(bf16[12288,1,4]{2,1,0:T(2,128)(2,1)} %bitcast.117, bf16[]{:T(256)} %broadcast.63), dimensions={1}, to_apply=%bitcast.86.reduce_sub_computation | reduce | bytes 196610
  336.8 7.3 %reshape.165 = bf16[16,2,1536]{2,1,0:T(2,128)(2,1)} reshape(bf16[12288,4]{1,0:T(8,128)(2,1)} %reduce.9) | data formatting | bytes 196608
  344.0 11.9 %all_to_all.66 = bf16[16,2,1536]{2,1,0:T(2,128)(2,1)} all-to-all(bf16[16,2,1536]{2,1,0:T(2,128)(2,1)} %reshape.165), channel_id=1, replica_groups=mesh['gx'=8,'gy'=16] {'gy'}, dimensions={0} | all-to-all | bytes 196608 | tf_op jit(solution)/shard_map/all_to_all | solution.py:75
  356.0 11.6 %reshape.166 = bf16[12288,1,4]{2,1,0:T(2,128)(2,1)} reshape(bf16[16,2,1536]{2,1,0:T(2,128)(2,1)} %all_to_all.66) | data formatting | bytes 196608
  367.5 12.7 %copy.37 = bf16[1,4,12288]{2,1,0:T(4,128)(2,1)} copy(bf16[1,4,12288]{1,0,2:T(2,128)(2,1)} %bitcast.118) | data formatting | bytes 196608 | tf_op jit(solution)/shard_map/all_to_all | solution.py:75
  380.3 0.9 copy.57
  381.9 1.5 all_to_all.61
  383.4 13.8 %all_gather.15 = bf16[1,512,768]{2,1,0:T(8,128)(2,1)S(1)} all-gather(bf16[1,64,768]{2,1,0:T(8,128)(2,1)} %all_to_all.61), channel_id=1, replica_groups=mesh['gx'=8,'gy'=16] {'gx'}, dimensions={1}, use_global_device_ids=true | all-gather | bytes 884736 | tf_op jit(solution)/shard_map/all_gather | solution.py:78
  397.3 3.4 fusion.1
  400.8 0.9 convert_element_type.77
  401.7 0.8 copy.60
  402.6 2.6 reduce.10
  405.2 1.6 reshape.167
  406.8 12.1 %all_to_all.67 = bf16[16,2,1536]{2,1,0:T(2,128)(2,1)} all-to-all(bf16[16,2,1536]{2,1,0:T(2,128)(2,1)} %reshape.167), channel_id=1, replica_groups=mesh['gx'=8,'gy'=16] {'gy'}, dimensions={0} | all-to-all | bytes 196608 | tf_op jit(solution)/shard_map/all_to_all | solution.py:58
  418.9 1.6 reshape.168
  420.5 2.1 bitcast_reduce_fusion
  422.6 1.6 all_to_all.49
  424.2 1.5 copy.28
  425.7 1.6 reshape_squeeze.6
  427.3 1.0 fusion.42
  428.3 4.0 fusion.54
  432.7 1.5 fusion.26
  434.2 1.6 convert_element_type.82
  435.8 11.8 %copy.29 = bf16[1,4,12288]{1,0,2:T(2,128)(2,1)} copy(bf16[1,4,12288]{2,1,0:T(4,128)(2,1)} %convert_element_type.82) | data formatting | bytes 196608 | tf_op jit(solution)/shard_map/convert_element_type | solution.py:32
  447.6 68.6 %reduce.11 = bf16[12288,4]{1,0:T(8,128)(2,1)} reduce(bf16[12288,1,4]{2,1,0:T(2,128)(2,1)} %bitcast.116, bf16[]{:T(256)} %broadcast.63), dimensions={1}, to_apply=%bitcast.90.reduce_sub_computation | reduce | bytes 196610
  516.2 7.5 %reshape.169 = bf16[16,2,1536]{2,1,0:T(2,128)(2,1)} reshape(bf16[12288,4]{1,0:T(8,128)(2,1)} %reduce.11) | data formatting | bytes 196608
  523.7 12.0 %all_to_all.68 = bf16[16,2,1536]{2,1,0:T(2,128)(2,1)} all-to-all(bf16[16,2,1536]{2,1,0:T(2,128)(2,1)} %reshape.169), channel_id=1, replica_groups=mesh['gx'=8,'gy'=16] {'gy'}, dimensions={0} | all-to-all | bytes 196608 | tf_op jit(solution)/shard_map/all_to_all | solution.py:75
  535.7 11.6 %reshape.170 = bf16[12288,1,4]{2,1,0:T(2,128)(2,1)} reshape(bf16[16,2,1536]{2,1,0:T(2,128)(2,1)} %all_to_all.68) | data formatting | bytes 196608
  547.2 12.7 %copy.30 = bf16[1,4,12288]{2,1,0:T(4,128)(2,1)} copy(bf16[1,4,12288]{1,0,2:T(2,128)(2,1)} %bitcast.119) | data formatting | bytes 196608 | tf_op jit(solution)/shard_map/all_to_all | solution.py:75
  560.0 0.9 copy.58
  561.6 1.5 all_to_all.54
  563.1 13.7 %all_gather.13 = bf16[1,512,768]{2,1,0:T(8,128)(2,1)S(1)} all-gather(bf16[1,64,768]{2,1,0:T(8,128)(2,1)} %all_to_all.54), channel_id=1, replica_groups=mesh['gx'=8,'gy'=16] {'gx'}, dimensions={1}, use_global_device_ids=true | all-gather | bytes 884736 | tf_op jit(solution)/shard_map/all_gather | solution.py:78
  576.8 3.4 fusion
  580.3 72.4 %reduce-scatter.11.cloned.1.call-done = bf16[1,32,2304]{2,1,0:T(8,128)(2,1)} async-done(((bf16[1,512,2304]{2,1,0:T(8,128)(2,1)}), bf16[1,32,2304]{2,1,0:T(8,128)(2,1)}) %reduce-scatter.11.cloned.1.call-update) | async-done | bytes 147472 | tf_op jit(solution)/shard_map/reduce_scatter | solution.py:83
  652.7 1.7 pad_maximum_fusion
  (48 shorter events, 8.1 us)
Async XLA Ops:
  6.5 390.7 %copy-start = (bf16[768,2304]{1,0:T(8,128)(2,1)S(1)}, bf16[768,2304]{1,0:T(8,128)(2,1)}, u32[]{:S(2)}) copy-start(bf16[768,2304]{1,0:T(8,128)(2,1)} %param.12) | copy-start | bytes 10616836
  6.5 64.4 %all-gather.5.cloned.1.call-start = ((), (), s32[]{:S(2)}) async-start(), calls=%async_computation.14 | async-start | bytes 2506752 | tf_op jit(solution)/shard_map/all_gather | solution.py:49
  27.0 91.1 %all-gather.3.cloned.1.call-start = ((), (), s32[]{:S(2)}) async-start(), calls=%async_computation.10 | async-start | bytes 2506752 | tf_op jit(solution)/shard_map/all_gather | solution.py:49
  27.7 124.6 %reduce-scatter.15.cloned.1.call-start = ((), (), s32[]{:S(2)}) async-start(), calls=%async_computation.16 | async-start | bytes 1179648 | tf_op jit(solution)/shard_map/reduce_scatter | solution.py:55
  75.7 109.7 %reduce-scatter.9.cloned.1.call-start = ((), (), s32[]{:S(2)}) async-start(), calls=%async_computation.12 | async-start | bytes 1179648 | tf_op jit(solution)/shard_map/reduce_scatter | solution.py:55
  122.8 6.0 copy-start.3
  122.8 96.5 %reduce-scatter.13.cloned.1.call-start = ((), (), s32[]{:S(2)}) async-start(), calls=%async_computation.15 | async-start | bytes 1769472 | tf_op jit(solution)/shard_map/reduce_scatter | solution.py:54
  128.8 272.0 %reduce-scatter.7.cloned.1.call-start = ((), (), s32[]{:S(2)}) async-start(), calls=%async_computation.11 | async-start | bytes 1769472 | tf_op jit(solution)/shard_map/reduce_scatter | solution.py:54
  225.8 13.0 %all-to-all-start.2 = ((bf16[16,2,1536]{2,1,0:T(2,128)(2,1)}), bf16[16,2,1536]{2,1,0:T(2,128)(2,1)}, u32[]{:S(2)}, u32[]{:S(2)}) async-start(bf16[16,2,1536]{2,1,0:T(2,128)(2,1)} %reshape.163), calls=%async_computation.6 | async-start | bytes 196608 | tf_op jit(solution)/shard_map/all_to_all | solution.py:58
  233.0 347.3 %reduce-scatter.17.cloned.1.call-start = ((), (), s32[]{:S(2)}) async-start(), calls=%async_computation.17 | async-start | bytes 2506752 | tf_op jit(solution)/shard_map/reduce_scatter | solution.py:83
  248.3 4.5 copy-start.4
  400.7 26.6 %copy-start.2 = (bf16[4,256,1]{1,0,2:T(4,128)(2,1)S(1)}, bf16[4,256,1]{1,0,2:T(4,128)(2,1)}, u32[]{:S(2)}) copy-start(bf16[4,256,1]{1,0,2:T(4,128)(2,1)} %get-tuple-element.20) | copy-start | bytes 6148
  400.7 252.0 %reduce-scatter.11.cloned.1.call-start = ((), (), s32[]{:S(2)}) async-start(), calls=%async_computation.13 | async-start | bytes 2506752 | tf_op jit(solution)/shard_map/reduce_scatter | solution.py:83
  428.3 4.4 copy-start.1
  428.3 4.4 copy-start.5
Sparse Core Ops, SparseCore 0:
  27.1 43.7 all-gather.4
  73.1 44.9 all-gather.2
  120.4 31.8 reduce-scatter.14
  154.6 30.7 reduce-scatter.8
  187.7 31.5 reduce-scatter.12
  221.6 31.9 reduce-scatter.6
  400.8 72.4 reduce-scatter.16
  580.4 72.2 reduce-scatter.10
where the time goes:
time: 674 us; the launch traced here: 661 us
  waiting for transfers between devices  244 us (36%)
  other arithmetic  153 us (23%)
  local copies, waits for them, and re-layouts  121 us (18%)
  blocking collectives  79.9 us (12%)
  matrix products  41.3 us (6%)
  between operations  13.9 us (2%)
  starting transfers between devices  7.51 us (1%)
    unnamed x4, other arithmetic  142 us
    all_gather x2, waiting for transfers between devices, per_device(): gathered = lax.all_gather(normed, 'gy', axis=1, tiled=True)  85.5 us
    reduce_scatter x2, waiting for transfers between devices, per_device(): lax.psum_scatter(partial_out.astype(jnp.bfloat16), 'gy', scatter_dimensio...  72.4 us
    reduce_scatter x2, waiting for transfers between devices, per_device(): kv_sum = lax.psum_scatter(kv_part, 'gx', scatter_dimension=1, tiled=True)  49.2 us
    unnamed x23, local copies, waits for them, and re-layouts  46.7 us
    reduce_scatter x2, waiting for transfers between devices, per_device(): lax.psum_scatter(query_part, 'gx', scatter_dimension=1, tiled=True)  31.3 us
    all_to_all x6, local copies, waits for them, and re-layouts, per_device(): lax.all_to_all(finish_mixed, 'gy', split_axis=2, concat_axis=1, tiled=True)  30 us
    all_gather x2, blocking collectives, per_device(): lax.all_gather(head_cols, 'gx', axis=1, tiled=True)  27.5 us
  transfers between devices with their start and end apart: 9, of which 7 were waited for; matrix products, arithmetic and copies ran while one was open for 46% of the time, Pallas kernels for 0%

commit v1 on v0

v1 whole, which is shorter than its diff:
```python
import jax
import jax.numpy as jnp
from jax import lax
from jax.experimental import pallas as pl
from jax.experimental.pallas import tpu as pltpu
from jax.sharding import PartitionSpec as P

HEADS = 48
BF = jnp.bfloat16
F32 = jnp.float32
VMEM_LIMIT = 48 * 1024 * 1024


def flat_perm(place):
    pairs = []
    for gx in range(8):
        for gy in range(16):
            z, c, y, x = gx // 2, gx % 2, gy // 4, gy % 4
            z2, c2, y2, x2 = place(z, c, y, x)
            pairs.append((gx * 16 + gy, ((z2 % 4) * 2 + c2) * 16 + (y2 % 4) * 4 + x2 % 4))
    return pairs


def send(value, place):
    return lax.ppermute(value, ("gx", "gy"), flat_perm(place))


def along_x(z, c, y, x, d):
    return (z, c, y, x + d)


def along_y(z, c, y, x, d):
    return (z, c, y + d, x)


def first_axis(d):
    return lambda z, c, y, x: (z, c, y, x + d) if c == 0 else (z, c, y + d, x)


def second_axis(d):
    return lambda z, c, y, x: (z, c, y + d, x) if c == 0 else (z, c, y, x + d)


def z_axis(d):
    return lambda z, c, y, x: (z + d, c, y, x)


def other_core(z, c, y, x):
    return (z, 1 - c, y, x)


def whole(shape):
    return pl.BlockSpec(shape, lambda *_: (0,) * len(shape))


def kernel_call(body, grid, in_specs, out_specs, out_shape, scratch, flops, nbytes, name):
    return pl.pallas_call(
        body,
        grid_spec=pltpu.PrefetchScalarGridSpec(
            num_scalar_prefetch=1,
            grid=grid,
            in_specs=in_specs,
            out_specs=out_specs,
            scratch_shapes=scratch,
        ),
        out_shape=out_shape,
        compiler_params=pltpu.CompilerParams(vmem_limit_bytes=VMEM_LIMIT),
        cost_estimate=pl.CostEstimate(flops=flops, bytes_accessed=nbytes, transcendentals=0),
        name=name,
    )


def one_hot(rows, cols, source):
    row = lax.broadcasted_iota(jnp.int32, (rows, cols), 0)
    col = lax.broadcasted_iota(jnp.int32, (rows, cols), 1)
    return jnp.where(col == source(row), 1.0, 0.0).astype(BF)


def project_body(place, own, plus, minus, half_a, half_b, stat, gain, wq, wkv, out, raw, normed, sems):
    x, y, c, part = place[0], place[1], place[3], place[4]
    width_q = wq.shape[1]
    blocks = [(own, k, 0, k) for k in range(4)]
    blocks += [(plus, k, 1, k) for k in range(4)]
    blocks += [(minus, k, 3, k) for k in range(4)]
    blocks += [(half_a, k, 2, k) for k in range(2)]
    blocks += [(half_b, k, 2, k + 2) for k in range(2)]
    for ref, k, d1, d2 in blocks:
        bx = (x + jnp.where(c == 0, d2, d1)) & 3
        by = (y + jnp.where(c == 0, d1, d2)) & 3

        @pl.when((bx >> 1) == part)
        def _(ref=ref, k=k, bx=bx, by=by):
            slot = by * 2 + (bx & 1)
            pltpu.make_async_copy(ref.at[pl.ds(k * 64, 64)], raw.at[slot], sems.at[slot]).start()

    for slot in range(8):
        pltpu.make_async_copy(own.at[pl.ds(0, 64)], raw.at[slot], sems.at[slot]).wait()
        st = stat[(slot // 2) * 4 + 2 * part + slot % 2]
        value = raw[slot].astype(F32)
        normed[slot] = ((value - st[:, 0:1]) * st[:, 1:2] * gain[...]).astype(BF)
    for m in range(2):
        left = normed[4 * m : 4 * m + 4].reshape(256, normed.shape[-1])
        q = jnp.dot(left, wq[...], preferred_element_type=F32)
        kv = jnp.dot(left, wkv[...], preferred_element_type=F32)
        out[2 * m : 2 * m + 2, :, :width_q] = q.reshape(2, 128, width_q)
        out[2 * m : 2 * m + 2, :, width_q:] = kv.reshape(2, 128, kv.shape[1])


def project(place, pieces, stat, gain, wq, wkv):
    width, nq = wq.shape
    n = nq + wkv.shape[1]
    any_spec = pl.BlockSpec(memory_space=pl.ANY)
    return kernel_call(
        project_body,
        (1,),
        [any_spec] * 5 + [whole(stat.shape), whole(gain.shape), whole(wq.shape), whole(wkv.shape)],
        whole((4, 128, n)),
        jax.ShapeDtypeStruct((4, 128, n), F32),
        [
            pltpu.VMEM((8, 64, width), BF),
            pltpu.VMEM((8, 64, width), BF),
            pltpu.SemaphoreType.DMA((8,)),
        ],
        2 * 512 * width * n,
        512 * width * 2 + width * n * 2 + 512 * n * 4,
        "project",
    )(place, *pieces, stat, gain, wq, wkv)


def pair_sum_body(place, keep, got, own, s1, s2, s3):
    value = keep[0] + got[0]
    step = pl.program_id(0)

    @pl.when(step == 0)
    def _():
        own[...] = value

    for d, ref in ((1, s1), (2, s2), (3, s3)):

        @pl.when(step == d)
        def _(ref=ref):
            ref[...] = value.astype(BF)


def pair_sum(place, keep, got):
    n = keep.shape[-1]
    block = pl.BlockSpec((1, 128, n), lambda d, p: ((p[2] + d) & 3, 0, 0))
    return kernel_call(
        pair_sum_body,
        (4,),
        [block, block],
        [whole((128, n))] * 4,
        [jax.ShapeDtypeStruct((128, n), F32)] + [jax.ShapeDtypeStruct((128, n), BF)] * 3,
        [],
        512 * n,
        2 * 512 * n * 4,
        "pair_sum",
    )(place, keep, got)


def finish_query_body(place, own, r1, r2, r3, out):
    total = own[...] + r1[...].astype(F32) + r2[...].astype(F32) + r3[...].astype(F32)
    order = one_hot(
        128, 128, lambda i: (i & 64) + ((i >> 2) & 1) * 32 + ((i >> 3) & 7) * 4 + (i & 3)
    )
    moved = jnp.dot(order, total.astype(BF), preferred_element_type=F32)
    out[...] = moved.reshape(16, 8, moved.shape[-1]).astype(BF)


def finish_query(place, own, got):
    n = own.shape[-1]
    return kernel_call(
        finish_query_body,
        (1,),
        [whole((128, n))] * 4,
        whole((16, 8, n)),
        jax.ShapeDtypeStruct((16, 8, n), BF),
        [],
        2 * 128 * 128 * n,
        128 * n * 12,
        "finish_query",
    )(place, own, *got)


def attend_body(lens, x, keys, values, out, acc):
    row = pl.program_id(0)
    nq = out.shape[-1]
    dim = keys.shape[-1]
    length = keys.shape[1]
    piece = x.shape[-1] - nq
    factor = dim ** (-0.5)
    flat = x[...].astype(F32).reshape(128, x.shape[-1]).astype(BF)
    pick = one_hot(32, 128, lambda i: (i >> 1) * 8 + (i & 1) * 4 + row)
    mine = jnp.dot(pick, flat[:, :nq], preferred_element_type=F32).astype(BF)
    heads = nq // dim
    query = jnp.concatenate([mine[:, h * dim : (h + 1) * dim] for h in range(heads)], axis=0)
    count = query.shape[0]

    spread = one_hot(piece, 16 * piece, lambda i: i)
    lane = lax.broadcasted_iota(jnp.int32, (piece, 16 * piece), 1)
    sub = lax.broadcasted_iota(jnp.int32, (piece, 16 * piece), 0)
    spread = jnp.where(lane % piece == sub, 1.0, 0.0).astype(BF)
    tiled = jnp.dot(flat[:, nq:], spread, preferred_element_type=F32)
    lane = lax.broadcasted_iota(jnp.int32, (128, 16 * piece), 1)
    sub = lax.broadcasted_iota(jnp.int32, (128, 16 * piece), 0)
    tiled = jnp.where(lane // piece == sub >> 3, tiled, 0.0).astype(BF)
    sub = lax.broadcasted_iota(jnp.int32, (8, 128), 0)
    lane = lax.broadcasted_iota(jnp.int32, (8, 128), 1)
    gather = jnp.where((lane & 7) == sub * 4 + row, 1.0, 0.0).astype(BF)
    fresh = jnp.dot(gather, tiled, preferred_element_type=F32)

    scores = (
        lax.dot_general(query, keys[0], (((1,), (1,)), ((), ())), preferred_element_type=F32)
        * factor
    )
    position = lax.broadcasted_iota(jnp.int32, (count, length), 1)
    scores = jnp.where(position < lens[row], scores, -1e30)
    query_f = query.astype(F32)
    new_0 = jnp.sum(query_f * fresh[0:1, :dim], axis=-1, keepdims=True) * factor
    new_1 = jnp.sum(query_f * fresh[1:2, :dim], axis=-1, keepdims=True) * factor
    step = lax.broadcasted_iota(jnp.int32, (count, 1), 0) & 1
    new_1 = jnp.where(step == 1, new_1, -1e30)
    top = jnp.maximum(jnp.max(scores, axis=-1, keepdims=True), jnp.maximum(new_0, new_1))
    exp_c = jnp.exp(scores - top)
    exp_0 = jnp.exp(new_0 - top)
    exp_1 = jnp.exp(new_1 - top)
    scale = 1.0 / (jnp.sum(exp_c, axis=-1, keepdims=True) + exp_0 + exp_1)
    weight = (exp_c * scale).astype(BF)
    mixed = jnp.dot(weight, values[0], preferred_element_type=F32)
    mixed = mixed + (exp_0 * scale).astype(BF).astype(F32) * fresh[0:1, dim:]
    mixed = mixed + (exp_1 * scale).astype(BF).astype(F32) * fresh[1:2, dim:]
    mixed = mixed.astype(BF)
    mixed = jnp.concatenate([mixed[h * 32 : (h + 1) * 32] for h in range(heads)], axis=1)
    sub = lax.broadcasted_iota(jnp.int32, (128, 32), 0)
    lane = lax.broadcasted_iota(jnp.int32, (128, 32), 1)
    back = jnp.where(sub == (lane >> 1) * 8 + (lane & 1) * 4 + row, 1.0, 0.0).astype(BF)
    placed = jnp.dot(back, mixed, preferred_element_type=F32)

    @pl.when(row == 0)
    def _():
        acc[...] = placed

    @pl.when(row > 0)
    def _():
        acc[...] += placed

    @pl.when(row == pl.num_programs(0) - 1)
    def _():
        out[...] = acc[...].reshape(16, 8, nq).astype(BF)


def attend(lens, x, keys, values, nq):
    rows, length, dim = keys.shape
    cache = pl.BlockSpec((1, length, dim), lambda r, p: (r, 0, 0))
    return kernel_call(
        attend_body,
        (rows,),
        [whole(x.shape), cache, cache],
        whole((16, 8, nq)),
        jax.ShapeDtypeStruct((16, 8, nq), BF),
        [pltpu.VMEM((128, nq), F32)],
        4 * rows * 96 * length * dim,
        2 * keys.size * 2,
        "attend",
    )(lens, x, keys, values)


def output_body(place, *refs):
    mixed, w_out = refs[:8], refs[8]
    outs, left = refs[9:13], refs[13]
    x, y, z, c = place[0], place[1], place[2], place[3]
    order = one_hot(
        128, 128, lambda o: (o & 64) + ((o >> 2) & 7) * 8 + ((o >> 5) & 1) * 4 + (o & 3)
    )
    for k in range(8):
        bz = (z + k % 4) & 3
        bc = c if k < 4 else 1 - c
        value = mixed[k][...].astype(F32).reshape(128, mixed[k].shape[-1]).astype(BF)
        moved = jnp.dot(order, value, preferred_element_type=F32).astype(BF)
        left[bz * 4 + bc * 2] = moved[:64]
        left[bz * 4 + bc * 2 + 1] = moved[64:]
    mine = jnp.where(c == 0, y, x)
    chunk = w_out.shape[1] // 3
    for d in (2, 1, 3, 0):
        group = (mine + d) & 3
        parts = [left[jnp.where(c == 0, group * 4 + i, i * 4 + group)] for i in range(4)]
        lhs = jnp.concatenate(parts, axis=0)
        for j in range(3):
            cols = pl.ds(j * chunk, chunk)
            outs[d][:, cols] = jnp.dot(
                lhs, w_out[:, cols], preferred_element_type=F32
            ).astype(BF)


def output_partials(place, mixed, w_out):
    depth, width = w_out.shape
    return kernel_call(
        output_body,
        (1,),
        [whole(mixed[0].shape)] * 8 + [whole(w_out.shape)],
        [whole((256, width))] * 4,
        [jax.ShapeDtypeStruct((256, width), BF)] * 4,
        [pltpu.VMEM((16, 64, depth), BF)],
        2 * 1024 * depth * width,
        1024 * depth * 2 + depth * width * 2 + 1024 * width * 2,
        "output_partials",
    )(place, *mixed, w_out)


def group_sum_body(place, a0, a1, a2, a3, own, s1, s2, s3):
    value = a0[...].astype(F32) + a1[...].astype(F32) + a2[...].astype(F32) + a3[...].astype(F32)
    step = pl.program_id(0)

    @pl.when(step == 0)
    def _():
        own[...] = value

    for d, ref in ((1, s1), (2, s2), (3, s3)):

        @pl.when(step == d)
        def _(ref=ref):
            ref[...] = value.astype(BF)


def group_sum(place, parts):
    width = parts[0].shape[-1]
    block = pl.BlockSpec((64, width), lambda d, p: ((jnp.where(p[3] == 0, p[0], p[1]) + d) & 3, 0))
    return kernel_call(
        group_sum_body,
        (4,),
        [block] * 4,
        [whole((64, width))] * 4,
        [jax.ShapeDtypeStruct((64, width), F32)] + [jax.ShapeDtypeStruct((64, width), BF)] * 3,
        [],
        1024 * width,
        1024 * width * 2,
        "group_sum",
    )(place, *parts)


def last_sum_body(place, own, r1, r2, r3, out):
    total = own[...] + r1[...].astype(F32) + r2[...].astype(F32) + r3[...].astype(F32)
    out[...] = total.reshape(out.shape).astype(BF)


def last_sum(place, own, got):
    rows, width = own.shape
    return kernel_call(
        last_sum_body,
        (1,),
        [whole((rows, width))] * 4,
        whole((2, rows // 2, width)),
        jax.ShapeDtypeStruct((2, rows // 2, width), BF),
        [],
        rows * width * 4,
        rows * width * 12,
        "last_sum",
    )(place, own, *got)


def row_statistics(tok, x, y, width_all):
    value = tok.astype(F32)
    count = tok.shape[1]
    mean = jnp.mean(value, axis=-1)
    centred = value - mean[:, None]
    held = jnp.stack([mean, jnp.sum(centred * centred, axis=-1)])
    for place in (
        other_core,
        lambda z, c, y, x: (z ^ 1, c, y, x),
        lambda z, c, y, x: (z ^ 2, c, y, x),
    ):
        other = send(held, place)
        delta = other[0] - held[0]
        held = jnp.stack(
            [(held[0] + other[0]) * 0.5, held[1] + other[1] + delta * delta * (count * 0.5)]
        )
        count = count * 2
    held = jnp.stack([held[0], lax.rsqrt(held[1] / width_all + 1e-05)])[None]
    for bit, place in (
        (x & 1, lambda z, c, y, x: (z, c, y, x ^ 1)),
        (x >> 1, lambda z, c, y, x: (z, c, y, x ^ 2)),
        (y & 1, lambda z, c, y, x: (z, c, y ^ 1, x)),
        (y >> 1, lambda z, c, y, x: (z, c, y ^ 2, x)),
    ):
        other = send(held, place)
        held = jnp.where(
            bit == 1, jnp.concatenate([other, held]), jnp.concatenate([held, other])
        )
    return jnp.swapaxes(held, 1, 2)


def per_device(tokens, norm_gain, w_query, w_kv, w_out, cache_keys, cache_values, lengths):
    gx, gy = lax.axis_index("gx"), lax.axis_index("gy")
    z, c, y, x = gx // 2, gx % 2, gy // 4, gy % 4
    width = tokens.shape[2]
    nq = w_query.shape[1]
    piece = w_kv.shape[1] // 16
    place = jnp.stack([x, y, z, c, c]).astype(jnp.int32)
    place_far = jnp.stack([x, y, z, c, 1 - c]).astype(jnp.int32)

    tok = tokens.reshape(64, width)
    got = [send(tok, first_axis(-1)), send(tok, first_axis(2)), send(tok, first_axis(1))]
    group = jnp.concatenate([tok] + got, axis=0)
    plus = send(group, second_axis(-1))
    minus = send(group, second_axis(1))
    half_a = send(minus[:128], second_axis(1))
    half_b = send(plus[128:], second_axis(-1))
    pieces = (group, plus, minus, half_a, half_b)
    stat = row_statistics(tok, x, y, width * 8)

    gain = norm_gain[None]
    wkv = lax.dynamic_slice_in_dim(w_kv, gy * piece, piece, 1)
    far = project(place_far, pieces, stat, gain, w_query, wkv)
    far_got = send(far, other_core)
    near = project(place, pieces, stat, gain, w_query, wkv)
    own, s1, s2, s3 = pair_sum(place, near, far_got)
    r = [send(s1, z_axis(1)), send(s2, z_axis(2)), send(s3, z_axis(-1))]
    query = finish_query(place, own, r)
    query = lax.all_to_all(query, "gy", 0, 0)
    mixed = attend(lengths, query, cache_keys, cache_values, nq)
    mixed = lax.all_to_all(mixed, "gy", 0, 0)
    same = [mixed, send(mixed, z_axis(-1)), send(mixed, z_axis(2)), send(mixed, z_axis(1))]
    cross = [send(m, other_core) for m in same]
    parts = output_partials(place, same + cross, w_out)
    got = [send(parts[1], second_axis(1)), send(parts[2], second_axis(2)), send(parts[3], second_axis(-1))]
    own, s1, s2, s3 = group_sum(place, [parts[0]] + got)
    got = [send(s1, first_axis(1)), send(s2, first_axis(2)), send(s3, first_axis(-1))]
    return last_sum(place, own, got)


def solution(mesh):
    in_specs = (
        P(None, "gy", "gx"),
        P("gx"),
        P("gx", "gy"),
        P("gx", None),
        P("gy", "gx"),
        P(("gx", "gy"), None, None),
        P(("gx", "gy"), None, None),
        P(("gx", "gy")),
    )
    out_specs = P(None, "gy", "gx")
    return jax.shard_map(
        per_device, mesh=mesh, in_specs=in_specs, out_specs=out_specs, check_vma=False
    )
```

time: 674 us -> 205 us (0.30); the launches traced: 661 us -> 203 us
  waiting for transfers between devices: 244 us -> 72.7 us
  other arithmetic: 153 us -> 6.86 us
  local copies, waits for them, and re-layouts: 121 us -> 21.6 us
  blocking collectives: 79.9 us -> 23.6 us
  matrix products: 41.3 us -> 0 us
  Pallas kernels: 0 us -> 38.2 us
  starting transfers between devices: 7.51 us -> 40.4 us
  between operations: 13.9 us -> 0.18 us
    reduce_scatter x6 -> x0, waiting for transfers between devices: 153 us -> none  [the longest x2 72.4 us: per_device(): lax.psum_scatter(partial_out.astype(jnp.bfloat16), 'gy', scatter_dimensio...]
    unnamed x4 -> x0, other arithmetic: 142 us -> none
    all_gather x2 -> x0, waiting for transfers between devices: 85.5 us -> none  [per_device(): gathered = lax.all_gather(normed, 'gy', axis=1, tiled=True)]
    ppermute x0 -> x31, waiting for transfers between devices: none -> 72.7 us  [send(): return lax.ppermute(value, ('gx', 'gy'), flat_perm(place))]
    dot_general x13 -> x0, matrix products: 41.3 us -> none  [the longest x2 11.8 us: per_device(): jnp.einsum('sbd,dc->sbc', gathered, w_query, preferred_element_type=jnp.f...]
    ppermute x0 -> x31, starting transfers between devices: none -> 40.4 us  [send(): return lax.ppermute(value, ('gx', 'gy'), flat_perm(place))]
    all_to_all x12 -> x0, local copies, waits for them, and re-layouts: 40.4 us -> none  [the longest x6 30 us: per_device(): lax.all_to_all(finish_mixed, 'gy', split_axis=2, concat_axis=1, tiled=True)]
    unnamed x23 -> x22, local copies, waits for them, and re-layouts: 46.7 us -> 6.68 us
  transfers between devices with their start and end apart: 9 -> 31, of which waited for: 7 -> 17; matrix products, arithmetic and copies ran while one was open for 46% -> 8% of each run, Pallas kernels for 0% -> 4%
where the time goes in v1:
time: 205 us; the launch traced here: 203 us
  waiting for transfers between devices  72.7 us (35%)
  starting transfers between devices  40.4 us (20%)
  Pallas kernels  38.2 us (19%)
  blocking collectives  23.6 us (12%)
  local copies, waits for them, and re-layouts  21.6 us (11%)
  other arithmetic  6.86 us (3%)
    ppermute x31, waiting for transfers between devices, send(): return lax.ppermute(value, ('gx', 'gy'), flat_perm(place))  72.7 us
    ppermute x31, starting transfers between devices, send(): return lax.ppermute(value, ('gx', 'gy'), flat_perm(place))  40.4 us
    pallas_call x2, Pallas kernels, project(): kernel_call(project_body, (1,), [any_spec] * 5 + [whole(stat.shape), whol...  17.6 us
    all_to_all x1, blocking collectives, per_device(): query = lax.all_to_all(query, 'gy', 0, 0)  12.3 us
    all_to_all x1, blocking collectives, per_device(): mixed = lax.all_to_all(mixed, 'gy', 0, 0)  11.3 us
    pallas_call x1, Pallas kernels, attend(): kernel_call(attend_body, (rows,), [whole(x.shape), cache, cache], whole((...  8 us
    pallas_call x1, Pallas kernels, output_partials(): kernel_call(output_body, (1,), [whole(mixed[0].shape)] * 8 + [whole(w_out...  7.72 us
    unnamed x22, local copies, waits for them, and re-layouts  6.68 us
  transfers between devices with their start and end apart: 31, of which 17 were waited for; matrix products, arithmetic and copies ran while one was open for 8% of the time, Pallas kernels for 4%

profile of v1, /device:TPU:24, one launch (start us, length us, event | category | flops | bytes accessed | tf_op | source)
XLA Modules:
  0.0 203.5 jit_solution(10393715580414187777)
XLA Ops:
  0.0 1.5 collective-permute-start.2
  1.5 2.7 %collective-permute-start.1 = (bf16[64,2304]{1,0:T(8,128)(2,1)}, bf16[64,2304]{1,0:T(8,128)(2,1)S(1)}, u32[]{:S(2)}, u32[]{:S(2)}) collective-permute-start(bf16[64,2304]{1,0:T(8,128)(2,1)} %bitcast.11), channel_id=1, source_target_pairs={{0,2},{1,3},{2,0},{3,1},{4,6},{5,7},{6,4},{7,5},{8,10},{9,11},{10,... | collective-permute-start | bytes 884744 | tf_op jit(solution)/shard_map/ppermute | solution.py:25
  4.2 1.4 collective-permute-start
  5.7 1.1 convert_reduce_fusion
  6.9 1.2 fusion.1
  8.3 4.0 %collective-permute-done.1 = bf16[64,2304]{1,0:T(8,128)(2,1)S(1)} collective-permute-done((bf16[64,2304]{1,0:T(8,128)(2,1)}, bf16[64,2304]{1,0:T(8,128)(2,1)S(1)}, u32[]{:S(2)}, u32[]{:S(2)}) %collective-permute-start.1) | collective-permute-done | bytes 294944 | tf_op jit(solution)/shard_map/ppermute | solution.py:25
  12.3 0.7 copy-done.10
  13.0 1.3 pad_maximum_fusion.own
  14.6 1.8 collective-permute-start.3
  16.5 2.0 collective-permute-start.8
  18.4 1.7 collective-permute-done.8
  20.1 4.0 %collective-permute-start.9 = (f32[2,64]{1,0:T(2,128)S(1)}, f32[2,64]{1,0:T(2,128)S(1)}, u32[]{:S(2)}, u32[]{:S(2)}) collective-permute-start(f32[2,64]{1,0:T(2,128)S(1)} %pad_maximum_fusion.5), channel_id=1, source_target_pairs={{0,64},{1,65},{2,66},{3,67},{4,68},{5,69},{6,70},{7,71},{8,72},{9,... | collective-permute-start | bytes 1544 | tf_op jit(solution)/shard_map/ppermute | solution.py:25
  24.1 1.5 collective-permute-done.9
  25.6 1.4 collective-permute-start.10
  27.0 2.3 %collective-permute-done.10 = f32[1,2,64]{2,1,0:T(2,128)S(1)} collective-permute-done((f32[1,2,64]{2,1,0:T(2,128)S(1)}, f32[1,2,64]{2,1,0:T(2,128)S(1)}, u32[]{:S(2)}, u32[]{:S(2)}) %collective-permute-start.10) | collective-permute-done | bytes 544 | tf_op jit(solution)/shard_map/ppermute | solution.py:25
  29.3 2.3 %collective-permute-start.11 = (f32[2,2,64]{2,1,0:T(2,128)S(1)}, f32[2,2,64]{2,1,0:T(2,128)S(1)}, u32[]{:S(2)}, u32[]{:S(2)}) collective-permute-start(f32[2,2,64]{2,1,0:T(2,128)S(1)} %maximum_select_fusion.2), channel_id=1, source_target_pairs={{0,2},{1,3},{2,0},{3,1},{4,6},{5,7},{6,4},{7,5},{8,10},{9,11},{10,... | collective-permute-start | bytes 3080 | tf_op jit(solution)/shard_map/ppermute | solution.py:25
  31.6 2.8 %collective-permute-done.11 = f32[2,2,64]{2,1,0:T(2,128)S(1)} collective-permute-done((f32[2,2,64]{2,1,0:T(2,128)S(1)}, f32[2,2,64]{2,1,0:T(2,128)S(1)}, u32[]{:S(2)}, u32[]{:S(2)}) %collective-permute-start.11) | collective-permute-done | bytes 1056 | tf_op jit(solution)/shard_map/ppermute | solution.py:25
  34.4 0.8 collective-permute-start.12
  35.2 2.9 %collective-permute-done.12 = f32[4,2,64]{2,0,1:T(4,128)S(1)} collective-permute-done((f32[4,2,64]{2,0,1:T(4,128)S(1)}, f32[4,2,64]{2,0,1:T(4,128)S(1)}, u32[]{:S(2)}, u32[]{:S(2)}) %collective-permute-start.12) | collective-permute-done | bytes 2080 | tf_op jit(solution)/shard_map/ppermute | solution.py:25
  38.7 1.2 collective-permute-start.13
  39.9 1.9 slice.35
  41.9 2.2 %collective-permute-start.5 = (bf16[128,2304]{1,0:T(8,128)(2,1)}, bf16[128,2304]{1,0:T(8,128)(2,1)}, u32[]{:S(2)}, u32[]{:S(2)}) collective-permute-start(bf16[128,2304]{1,0:T(8,128)(2,1)} %slice.35), channel_id=1, source_target_pairs={{0,4},{1,5},{2,6},{3,7},{4,8},{5,9},{6,10},{7,11},{8,12},{9,13},{1... | collective-permute-start | bytes 1769480 | tf_op jit(solution)/shard_map/ppermute | solution.py:25
  44.0 2.0 slice.36
  46.0 1.1 constant_dynamic-slice_fusion.wkv
  47.9 1.4 pad_maximum_fusion.2
  49.3 1.8 copy.17
  51.0 1.8 copy.16
  52.8 1.2 select_bitcast_fusion.stat
  54.0 3.5 %collective-permute-done.6.half_b = bf16[128,2304]{1,0:T(8,128)(2,1)} collective-permute-done((bf16[128,2304]{1,0:T(8,128)(2,1)}, bf16[128,2304]{1,0:T(8,128)(2,1)}, u32[]{:S(2)}, u32[]{:S(2)}) %collective-permute-start.6) | collective-permute-done | bytes 589856 | tf_op jit(solution)/shard_map/ppermute | solution.py:25
  57.4 8.7 %project.3 = f32[4,128,800]{2,1,0:T(8,128)} custom-call(s32[5]{0:T(128)S(1)} %stack.59.place, bf16[256,2304]{1,0:T(8,128)(2,1)S(1)} %pad_maximum_fusion.own, bf16[256,2304]{1,0:T(8,128)(2,1)} %collective-permute-done.3.plus, bf16[256,2304]{1,0:T(8,128)(2,1)} %collective-permute-done.4.minus, bf16[128,2304]{1,0:T(8,128)(2,1)} %collective-permute-done.5.half_a, ...), custom_call_target="tpu_custom_call" | custom-call | flops 1887436800 | bytes 7684096 | tf_op jit(solution)/shard_map/project/pallas_call | solution.py:113
  66.1 0.8 copy-done.5
  67.0 2.7 %copy.18 = f32[4,128,800]{1,2,0:T(8,128)} copy(f32[4,128,800]{2,1,0:T(8,128)} %project.3) | data formatting | bytes 3276800 | tf_op jit(solution)/shard_map/project/pallas_call | solution.py:113
  69.7 1.1 copy-done.4
  70.8 1.0 copy-done.6
  71.9 8.9 %project.2.keep = f32[4,128,800]{2,1,0:T(8,128)} custom-call(s32[5]{0:T(128)S(1)} %stack.52.place, bf16[256,2304]{1,0:T(8,128)(2,1)S(1)} %pad_maximum_fusion.own, bf16[256,2304]{1,0:T(8,128)(2,1)} %collective-permute-done.3.plus, bf16[256,2304]{1,0:T(8,128)(2,1)} %collective-permute-done.4.minus, bf16[128,2304]{1,0:T(8,128)(2,1)} %collective-permute-done.5.half_a, ...), custom_call_target="tpu_custom_call" | custom-call | flops 1887436800 | bytes 7684096 | tf_op jit(solution)/shard_map/project/pallas_call | solution.py:113
  80.8 2.7 %copy.19.got = f32[4,128,800]{2,1,0:T(8,128)} copy(f32[4,128,800]{1,2,0:T(8,128)} %collective-permute-done.14) | data formatting | bytes 3276800 | tf_op jit(solution)/shard_map/ppermute | solution.py:25
  83.5 1.5 copy-done.1
  85.0 1.5 copy-done.2
  86.5 0.9 pair_sum.1
  87.5 1.6 collective-permute-start.15
  89.1 3.6 %collective-permute-start.16 = (bf16[128,800]{1,0:T(8,128)(2,1)S(1)}, bf16[128,800]{1,0:T(8,128)(2,1)S(1)}, u32[]{:S(2)}, u32[]{:S(2)}) collective-permute-start(bf16[128,800]{1,0:T(8,128)(2,1)S(1)} %get-tuple-element.19), channel_id=1, source_target_pairs={{0,64},{1,65},{2,66},{3,67},{4,68},{5,69},{6,70},{7,71},{8,72},{9,... | collective-permute-start | bytes 614408 | tf_op jit(solution)/shard_map/ppermute | solution.py:25
  92.7 1.0 collective-permute-start.17
  93.7 3.9 %collective-permute-done.15.r1 = bf16[128,800]{1,0:T(8,128)(2,1)S(1)} collective-permute-done((bf16[128,800]{1,0:T(8,128)(2,1)S(1)}, bf16[128,800]{1,0:T(8,128)(2,1)S(1)}, u32[]{:S(2)}, u32[]{:S(2)}) %collective-permute-start.15) | collective-permute-done | bytes 204832 | tf_op jit(solution)/shard_map/ppermute | solution.py:25
  97.6 6.1 %collective-permute-done.16.r2 = bf16[128,800]{1,0:T(8,128)(2,1)S(1)} collective-permute-done((bf16[128,800]{1,0:T(8,128)(2,1)S(1)}, bf16[128,800]{1,0:T(8,128)(2,1)S(1)}, u32[]{:S(2)}, u32[]{:S(2)}) %collective-permute-start.16) | collective-permute-done | bytes 204832 | tf_op jit(solution)/shard_map/ppermute | solution.py:25
  103.6 0.8 finish_query.1
  104.5 12.3 %all_to_all.10.x = bf16[16,8,800]{2,1,0:T(8,128)(2,1)S(1)} all-to-all(bf16[16,8,800]{2,1,0:T(8,128)(2,1)S(1)} %finish_query.1), channel_id=1, replica_groups=mesh['gx'=8,'gy'=16] {'gy'}, dimensions={0} | all-to-all | bytes 409600 | tf_op jit(solution)/shard_map/all_to_all | solution.py:419
  116.8 8.0 %attend.1 = bf16[16,8,768]{2,1,0:T(8,128)(2,1)S(1)} custom-call(s32[4]{0:T(128)S(1)} %copy-done.8, bf16[16,8,800]{2,1,0:T(8,128)(2,1)S(1)} %all_to_all.10.x, bf16[4,2048,256]{2,1,0:T(8,128)(2,1)S(1)} %copy-done.7, bf16[4,2048,256]{2,1,0:T(8,128)(2,1)} %values.1), custom_call_target="tpu_custom_call" | custom-call | flops 805306368 | bytes 8388608 | tf_op jit(solution)/shard_map/attend/pallas_call | solution.py:255
  124.8 11.3 %all_to_all.11.refs_0_ = bf16[16,8,768]{2,1,0:T(8,128)(2,1)S(1)} all-to-all(bf16[16,8,768]{2,1,0:T(8,128)(2,1)S(1)} %attend.1), channel_id=1, replica_groups=mesh['gx'=8,'gy'=16] {'gy'}, dimensions={0} | all-to-all | bytes 393216 | tf_op jit(solution)/shard_map/all_to_all | solution.py:421
  136.1 1.2 collective-permute-start.20
  137.3 2.4 %collective-permute-start.19 = (bf16[16,8,768]{2,1,0:T(8,128)(2,1)S(1)}, bf16[16,8,768]{2,1,0:T(8,128)(2,1)S(1)}, u32[]{:S(2)}, u32[]{:S(2)}) collective-permute-start(bf16[16,8,768]{2,1,0:T(8,128)(2,1)S(1)} %all_to_all.11.refs_0_), channel_id=1, source_target_pairs={{0,64},{1,65},{2,66},{3,67},{4,68},{5,69},{6,70},{7,71},{8,72},{9,... | collective-permute-start | bytes 589832 | tf_op jit(solution)/shard_map/ppermute | solution.py:25
  139.7 1.2 collective-permute-start.18
  141.0 3.1 %collective-permute-done.20.refs_3_ = bf16[16,8,768]{2,1,0:T(8,128)(2,1)S(1)} collective-permute-done((bf16[16,8,768]{2,1,0:T(8,128)(2,1)S(1)}, bf16[16,8,768]{2,1,0:T(8,128)(2,1)S(1)}, u32[]{:S(2)}, u32[]{:S(2)}) %collective-permute-start.20) | collective-permute-done | bytes 196640 | tf_op jit(solution)/shard_map/ppermute | solution.py:25
  144.1 2.1 %collective-permute-done.19.refs_2_ = bf16[16,8,768]{2,1,0:T(8,128)(2,1)S(1)} collective-permute-done((bf16[16,8,768]{2,1,0:T(8,128)(2,1)S(1)}, bf16[16,8,768]{2,1,0:T(8,128)(2,1)S(1)}, u32[]{:S(2)}, u32[]{:S(2)}) %collective-permute-start.19) | collective-permute-done | bytes 196640 | tf_op jit(solution)/shard_map/ppermute | solution.py:25
  146.7 0.9 collective-permute-done.23.refs_6_
  147.9 7.7 %output_partials.1 = (bf16[256,2304]{1,0:T(8,128)(2,1)S(1)}, bf16[256,2304]{1,0:T(8,128)(2,1)S(1)}, bf16[256,2304]{1,0:T(8,128)(2,1)S(1)}, bf16[256,2304]{1,0:T(8,128)(2,1)}) custom-call(s32[5]{0:T(128)S(1)} %stack.52.place, bf16[16,8,768]{2,1,0:T(8,128)(2,1)S(1)} %all_to_all.11.refs_0_, bf16[16,8,768]{2,1,0:T(8,128)(2,1)S(1)} %collective-permute-done.18.refs_1_, ...), custom_call_target="tpu_custom_call" | custom-call | flops 3623878656 | bytes 9830400 | tf_op jit(solution)/shard_map/output_partials/pallas_call | solution.py:297
  155.6 2.4 %collective-permute-start.25 = (bf16[256,2304]{1,0:T(8,128)(2,1)S(1)}, bf16[256,2304]{1,0:T(8,128)(2,1)S(1)}, u32[]{:S(2)}, u32[]{:S(2)}) collective-permute-start(bf16[256,2304]{1,0:T(8,128)(2,1)S(1)} %get-tuple-element.22), channel_id=1, source_target_pairs={{0,4},{1,5},{2,6},{3,7},{4,8},{5,9},{6,10},{7,11},{8,12},{9,13},{1... | collective-permute-start | bytes 3538952 | tf_op jit(solution)/shard_map/ppermute | solution.py:25
  158.9 25.5 %collective-permute-done.25.a1 = bf16[256,2304]{1,0:T(8,128)(2,1)S(1)} collective-permute-done((bf16[256,2304]{1,0:T(8,128)(2,1)S(1)}, bf16[256,2304]{1,0:T(8,128)(2,1)S(1)}, u32[]{:S(2)}, u32[]{:S(2)}) %collective-permute-start.25) | collective-permute-done | bytes 1179680 | tf_op jit(solution)/shard_map/ppermute | solution.py:25
  184.4 3.9 %collective-permute-done.27.a3 = bf16[256,2304]{1,0:T(8,128)(2,1)S(1)} collective-permute-done((bf16[256,2304]{1,0:T(8,128)(2,1)}, bf16[256,2304]{1,0:T(8,128)(2,1)S(1)}, u32[]{:S(2)}, u32[]{:S(2)}) %collective-permute-start.27) | collective-permute-done | bytes 1179680 | tf_op jit(solution)/shard_map/ppermute | solution.py:25
  188.3 1.7 group_sum.1
  190.8 1.7 collective-permute-start.29
  192.4 1.4 collective-permute-start.30
  193.8 7.4 %collective-permute-done.28.r1 = bf16[64,2304]{1,0:T(8,128)(2,1)S(1)} collective-permute-done((bf16[64,2304]{1,0:T(8,128)(2,1)S(1)}, bf16[64,2304]{1,0:T(8,128)(2,1)S(1)}, u32[]{:S(2)}, u32[]{:S(2)}) %collective-permute-start.28) | collective-permute-done | bytes 294944 | tf_op jit(solution)/shard_map/ppermute | solution.py:25
  201.2 0.9 collective-permute-done.30.r3
  202.1 1.4 last_sum.1
  (60 shorter events, 4.6 us)
Async XLA Ops:
  0.0 46.0 %copy-start = (bf16[2304,512]{1,0:T(8,128)(2,1)S(1)}, bf16[2304,512]{1,0:T(8,128)(2,1)}, u32[]{:S(2)}) copy-start(bf16[2304,512]{1,0:T(8,128)(2,1)} %param.11) | copy-start | bytes 7077892
  0.0 8.2 %collective-permute-start.2 = (bf16[64,2304]{1,0:T(8,128)(2,1)}, bf16[64,2304]{1,0:T(8,128)(2,1)S(1)}, u32[]{:S(2)}, u32[]{:S(2)}) collective-permute-start(bf16[64,2304]{1,0:T(8,128)(2,1)} %bitcast.10), channel_id=1, source_target_pairs={{0,1},{1,2},{2,3},{3,0},{4,5},{5,6},{6,7},{7,4},{8,9},{9,10},{10,1... | collective-permute-start | bytes 884744 | tf_op jit(solution)/shard_map/ppermute | solution.py:25
  1.5 10.8 %collective-permute-start.1 = (bf16[64,2304]{1,0:T(8,128)(2,1)}, bf16[64,2304]{1,0:T(8,128)(2,1)S(1)}, u32[]{:S(2)}, u32[]{:S(2)}) collective-permute-start(bf16[64,2304]{1,0:T(8,128)(2,1)} %bitcast.11), channel_id=1, source_target_pairs={{0,2},{1,3},{2,0},{3,1},{4,6},{5,7},{6,4},{7,5},{8,10},{9,11},{10,... | collective-permute-start | bytes 884744 | tf_op jit(solution)/shard_map/ppermute | solution.py:25
  4.2 8.8 %collective-permute-start = (bf16[64,2304]{1,0:T(8,128)(2,1)}, bf16[64,2304]{1,0:T(8,128)(2,1)}, u32[]{:S(2)}, u32[]{:S(2)}) collective-permute-start(bf16[64,2304]{1,0:T(8,128)(2,1)} %bitcast.12), channel_id=1, source_target_pairs={{0,3},{1,0},{2,1},{3,2},{4,7},{5,4},{6,5},{7,6},{8,11},{9,8},{10,9... | collective-permute-start | bytes 884744 | tf_op jit(solution)/shard_map/ppermute | solution.py:25
  8.2 8.3 %collective-permute-start.7 = (f32[2,64]{1,0:T(2,128)S(1)}, f32[2,64]{1,0:T(2,128)S(1)}, u32[]{:S(2)}, u32[]{:S(2)}) collective-permute-start(f32[2,64]{1,0:T(2,128)S(1)} %pad_maximum_fusion.3), channel_id=1, source_target_pairs={{0,16},{1,17},{2,18},{3,19},{4,20},{5,21},{6,22},{7,23},{8,24},{9,... | collective-permute-start | bytes 1544 | tf_op jit(solution)/shard_map/ppermute | solution.py:25
  8.3 4.0 %copy-start.9 = (bf16[64,2304]{1,0:T(8,128)(2,1)}, bf16[64,2304]{1,0:T(8,128)(2,1)S(1)}, u32[]{:S(2)}) copy-start(bf16[64,2304]{1,0:T(8,128)(2,1)S(1)} %collective-permute-done.2) | copy-start | bytes 884740
  12.3 0.7 copy-start.10
  14.3 25.6 %collective-permute-start.4 = (bf16[256,2304]{1,0:T(8,128)(2,1)S(1)}, bf16[256,2304]{1,0:T(8,128)(2,1)}, u32[]{:S(2)}, u32[]{:S(2)}) collective-permute-start(bf16[256,2304]{1,0:T(8,128)(2,1)S(1)} %pad_maximum_fusion.own), channel_id=1, source_target_pairs={{0,4},{1,5},{2,6},{3,7},{4,8},{5,9},{6,10},{7,11},{8,12},{9,13},{1... | collective-permute-start | bytes 3538952 | tf_op jit(solution)/shard_map/ppermute | solution.py:25
  14.6 29.4 %collective-permute-start.3 = (bf16[256,2304]{1,0:T(8,128)(2,1)S(1)}, bf16[256,2304]{1,0:T(8,128)(2,1)}, u32[]{:S(2)}, u32[]{:S(2)}) collective-permute-start(bf16[256,2304]{1,0:T(8,128)(2,1)S(1)} %pad_maximum_fusion.own), channel_id=1, source_target_pairs={{0,12},{1,13},{2,14},{3,15},{4,0},{5,1},{6,2},{7,3},{8,4},{9,5},{1... | collective-permute-start | bytes 3538952 | tf_op jit(solution)/shard_map/ppermute | solution.py:25
  16.5 3.6 %collective-permute-start.8 = (f32[2,64]{1,0:T(2,128)S(1)}, f32[2,64]{1,0:T(2,128)S(1)}, u32[]{:S(2)}, u32[]{:S(2)}) collective-permute-start(f32[2,64]{1,0:T(2,128)S(1)} %pad_maximum_fusion.4), channel_id=1, source_target_pairs={{0,32},{1,33},{2,34},{3,35},{4,36},{5,37},{6,38},{7,39},{8,40},{9,... | collective-permute-start | bytes 1544 | tf_op jit(solution)/shard_map/ppermute | solution.py:25
  20.1 5.5 %collective-permute-start.9 = (f32[2,64]{1,0:T(2,128)S(1)}, f32[2,64]{1,0:T(2,128)S(1)}, u32[]{:S(2)}, u32[]{:S(2)}) collective-permute-start(f32[2,64]{1,0:T(2,128)S(1)} %pad_maximum_fusion.5), channel_id=1, source_target_pairs={{0,64},{1,65},{2,66},{3,67},{4,68},{5,69},{6,70},{7,71},{8,72},{9,... | collective-permute-start | bytes 1544 | tf_op jit(solution)/shard_map/ppermute | solution.py:25
  25.6 3.6 %collective-permute-start.10 = (f32[1,2,64]{2,1,0:T(2,128)S(1)}, f32[1,2,64]{2,1,0:T(2,128)S(1)}, u32[]{:S(2)}, u32[]{:S(2)}) collective-permute-start(f32[1,2,64]{2,1,0:T(2,128)S(1)} %maximum_bitcast_fusion), channel_id=1, source_target_pairs={{0,1},{1,0},{2,3},{3,2},{4,5},{5,4},{6,7},{7,6},{8,9},{9,8},{10,11... | collective-permute-start | bytes 1544 | tf_op jit(solution)/shard_map/ppermute | solution.py:25
  29.3 5.1 %collective-permute-start.11 = (f32[2,2,64]{2,1,0:T(2,128)S(1)}, f32[2,2,64]{2,1,0:T(2,128)S(1)}, u32[]{:S(2)}, u32[]{:S(2)}) collective-permute-start(f32[2,2,64]{2,1,0:T(2,128)S(1)} %maximum_select_fusion.2), channel_id=1, source_target_pairs={{0,2},{1,3},{2,0},{3,1},{4,6},{5,7},{6,4},{7,5},{8,10},{9,11},{10,... | collective-permute-start | bytes 3080 | tf_op jit(solution)/shard_map/ppermute | solution.py:25
  34.4 3.7 %collective-permute-start.12 = (f32[4,2,64]{2,0,1:T(4,128)S(1)}, f32[4,2,64]{2,0,1:T(4,128)S(1)}, u32[]{:S(2)}, u32[]{:S(2)}) collective-permute-start(f32[4,2,64]{2,0,1:T(4,128)S(1)} %maximum_select_fusion.1), channel_id=1, source_target_pairs={{0,4},{1,5},{2,6},{3,7},{4,0},{5,1},{6,2},{7,3},{8,12},{9,13},{10,... | collective-permute-start | bytes 6152 | tf_op jit(solution)/shard_map/ppermute | solution.py:25
  38.7 9.2 %collective-permute-start.13 = (f32[8,2,64]{2,0,1:T(8,128)}, f32[8,2,64]{2,0,1:T(8,128)}, u32[]{:S(2)}, u32[]{:S(2)}) collective-permute-start(f32[8,2,64]{2,0,1:T(8,128)} %maximum_select_fusion), channel_id=1, source_target_pairs={{0,8},{1,9},{2,10},{3,11},{4,12},{5,13},{6,14},{7,15},{8,0},{9,1},... | collective-permute-start | bytes 12296 | tf_op jit(solution)/shard_map/ppermute | solution.py:25
  41.9 12.1 %collective-permute-start.5 = (bf16[128,2304]{1,0:T(8,128)(2,1)}, bf16[128,2304]{1,0:T(8,128)(2,1)}, u32[]{:S(2)}, u32[]{:S(2)}) collective-permute-start(bf16[128,2304]{1,0:T(8,128)(2,1)} %slice.35), channel_id=1, source_target_pairs={{0,4},{1,5},{2,6},{3,7},{4,8},{5,9},{6,10},{7,11},{8,12},{9,13},{1... | collective-permute-start | bytes 1769480 | tf_op jit(solution)/shard_map/ppermute | solution.py:25
  46.0 11.4 %collective-permute-start.6 = (bf16[128,2304]{1,0:T(8,128)(2,1)}, bf16[128,2304]{1,0:T(8,128)(2,1)}, u32[]{:S(2)}, u32[]{:S(2)}) collective-permute-start(bf16[128,2304]{1,0:T(8,128)(2,1)} %slice.36), channel_id=1, source_target_pairs={{0,12},{1,13},{2,14},{3,15},{4,0},{5,1},{6,2},{7,3},{8,4},{9,5},{1... | collective-permute-start | bytes 1769480 | tf_op jit(solution)/shard_map/ppermute | solution.py:25
  52.8 4.6 %copy-start.3 = (bf16[2304,32]{1,0:T(8,128)(2,1)S(1)}, bf16[2304,32]{1,0:T(8,128)(2,1)}, u32[]{:S(2)}) copy-start(bf16[2304,32]{1,0:T(8,128)(2,1)} %constant_dynamic-slice_fusion.wkv) | copy-start | bytes 442372
  66.1 0.8 copy-start.5
  69.7 11.2 %collective-permute-start.14 = (f32[4,128,800]{1,2,0:T(8,128)}, f32[4,128,800]{1,2,0:T(8,128)}, u32[]{:S(2)}, u32[]{:S(2)}) collective-permute-start(f32[4,128,800]{1,2,0:T(8,128)} %copy.18), channel_id=1, source_target_pairs={{0,16},{1,17},{2,18},{3,19},{4,20},{5,21},{6,22},{7,23},{8,24},{9,... | collective-permute-start | bytes 4915208 | tf_op jit(solution)/shard_map/ppermute | solution.py:25
  69.7 1.1 copy-start.4
  70.8 1.0 copy-start.6
  83.5 1.5 copy-start.1
  85.0 1.5 copy-start.2
  86.5 30.3 %copy-start.7 = (bf16[4,2048,256]{2,1,0:T(8,128)(2,1)S(1)}, bf16[4,2048,256]{2,1,0:T(8,128)(2,1)}, u32[]{:S(2)}) copy-start(bf16[4,2048,256]{2,1,0:T(8,128)(2,1)} %keys.1) | copy-start | bytes 12582916
  87.5 29.3 %copy-start.8 = (s32[4]{0:T(128)S(1)}, s32[4]{0:T(128)}, u32[]{:S(2)}) copy-start(s32[4]{0:T(128)} %lens.1) | copy-start | bytes 52
  87.5 10.1 %collective-permute-start.15 = (bf16[128,800]{1,0:T(8,128)(2,1)S(1)}, bf16[128,800]{1,0:T(8,128)(2,1)S(1)}, u32[]{:S(2)}, u32[]{:S(2)}) collective-permute-start(bf16[128,800]{1,0:T(8,128)(2,1)S(1)} %get-tuple-element.18), channel_id=1, source_target_pairs={{0,32},{1,33},{2,34},{3,35},{4,36},{5,37},{6,38},{7,39},{8,40},{9,... | collective-permute-start | bytes 614408 | tf_op jit(solution)/shard_map/ppermute | solution.py:25
  89.1 14.5 %collective-permute-start.16 = (bf16[128,800]{1,0:T(8,128)(2,1)S(1)}, bf16[128,800]{1,0:T(8,128)(2,1)S(1)}, u32[]{:S(2)}, u32[]{:S(2)}) collective-permute-start(bf16[128,800]{1,0:T(8,128)(2,1)S(1)} %get-tuple-element.19), channel_id=1, source_target_pairs={{0,64},{1,65},{2,66},{3,67},{4,68},{5,69},{6,70},{7,71},{8,72},{9,... | collective-permute-start | bytes 614408 | tf_op jit(solution)/shard_map/ppermute | solution.py:25
  92.7 11.0 %collective-permute-start.17 = (bf16[128,800]{1,0:T(8,128)(2,1)S(1)}, bf16[128,800]{1,0:T(8,128)(2,1)S(1)}, u32[]{:S(2)}, u32[]{:S(2)}) collective-permute-start(bf16[128,800]{1,0:T(8,128)(2,1)S(1)} %get-tuple-element.20), channel_id=1, source_target_pairs={{0,96},{1,97},{2,98},{3,99},{4,100},{5,101},{6,102},{7,103},{8,104... | collective-permute-start | bytes 614408 | tf_op jit(solution)/shard_map/ppermute | solution.py:25
  136.1 8.0 %collective-permute-start.20 = (bf16[16,8,768]{2,1,0:T(8,128)(2,1)S(1)}, bf16[16,8,768]{2,1,0:T(8,128)(2,1)S(1)}, u32[]{:S(2)}, u32[]{:S(2)}) collective-permute-start(bf16[16,8,768]{2,1,0:T(8,128)(2,1)S(1)} %all_to_all.11.refs_0_), channel_id=1, source_target_pairs={{0,32},{1,33},{2,34},{3,35},{4,36},{5,37},{6,38},{7,39},{8,40},{9,... | collective-permute-start | bytes 589832 | tf_op jit(solution)/shard_map/ppermute | solution.py:25
  137.3 8.8 %collective-permute-start.19 = (bf16[16,8,768]{2,1,0:T(8,128)(2,1)S(1)}, bf16[16,8,768]{2,1,0:T(8,128)(2,1)S(1)}, u32[]{:S(2)}, u32[]{:S(2)}) collective-permute-start(bf16[16,8,768]{2,1,0:T(8,128)(2,1)S(1)} %all_to_all.11.refs_0_), channel_id=1, source_target_pairs={{0,64},{1,65},{2,66},{3,67},{4,68},{5,69},{6,70},{7,71},{8,72},{9,... | collective-permute-start | bytes 589832 | tf_op jit(solution)/shard_map/ppermute | solution.py:25
  139.7 6.4 %collective-permute-start.18 = (bf16[16,8,768]{2,1,0:T(8,128)(2,1)S(1)}, bf16[16,8,768]{2,1,0:T(8,128)(2,1)S(1)}, u32[]{:S(2)}, u32[]{:S(2)}) collective-permute-start(bf16[16,8,768]{2,1,0:T(8,128)(2,1)S(1)} %all_to_all.11.refs_0_), channel_id=1, source_target_pairs={{0,96},{1,97},{2,98},{3,99},{4,100},{5,101},{6,102},{7,103},{8,104... | collective-permute-start | bytes 589832 | tf_op jit(solution)/shard_map/ppermute | solution.py:25
  141.0 5.7 %collective-permute-start.21 = (bf16[16,8,768]{2,1,0:T(8,128)(2,1)S(1)}, bf16[16,8,768]{2,1,0:T(8,128)(2,1)S(1)}, u32[]{:S(2)}, u32[]{:S(2)}) collective-permute-start(bf16[16,8,768]{2,1,0:T(8,128)(2,1)S(1)} %all_to_all.11.refs_0_), channel_id=1, source_target_pairs={{0,16},{1,17},{2,18},{3,19},{4,20},{5,21},{6,22},{7,23},{8,24},{9,... | collective-permute-start | bytes 589832 | tf_op jit(solution)/shard_map/ppermute | solution.py:25
  144.1 2.6 %collective-permute-start.24 = (bf16[16,8,768]{2,1,0:T(8,128)(2,1)S(1)}, bf16[16,8,768]{2,1,0:T(8,128)(2,1)S(1)}, u32[]{:S(2)}, u32[]{:S(2)}) collective-permute-start(bf16[16,8,768]{2,1,0:T(8,128)(2,1)S(1)} %collective-permute-done.20.refs_3_), channel_id=1, source_target_pairs={{0,16},{1,17},{2,18},{3,19},{4,20},{5,21},{6,22},{7,23},{8,24},{9,... | collective-permute-start | bytes 589832 | tf_op jit(solution)/shard_map/ppermute | solution.py:25
  146.2 1.4 collective-permute-start.23
  146.2 1.7 collective-permute-start.22
  155.6 28.8 %collective-permute-start.25 = (bf16[256,2304]{1,0:T(8,128)(2,1)S(1)}, bf16[256,2304]{1,0:T(8,128)(2,1)S(1)}, u32[]{:S(2)}, u32[]{:S(2)}) collective-permute-start(bf16[256,2304]{1,0:T(8,128)(2,1)S(1)} %get-tuple-element.22), channel_id=1, source_target_pairs={{0,4},{1,5},{2,6},{3,7},{4,8},{5,9},{6,10},{7,11},{8,12},{9,13},{1... | collective-permute-start | bytes 3538952 | tf_op jit(solution)/shard_map/ppermute | solution.py:25
  158.0 26.4 %collective-permute-start.26 = (bf16[256,2304]{1,0:T(8,128)(2,1)S(1)}, bf16[256,2304]{1,0:T(8,128)(2,1)S(1)}, u32[]{:S(2)}, u32[]{:S(2)}) collective-permute-start(bf16[256,2304]{1,0:T(8,128)(2,1)S(1)} %get-tuple-element.23), channel_id=1, source_target_pairs={{0,8},{1,9},{2,10},{3,11},{4,12},{5,13},{6,14},{7,15},{8,0},{9,1},... | collective-permute-start | bytes 3538952 | tf_op jit(solution)/shard_map/ppermute | solution.py:25
  158.3 30.0 %collective-permute-start.27 = (bf16[256,2304]{1,0:T(8,128)(2,1)}, bf16[256,2304]{1,0:T(8,128)(2,1)S(1)}, u32[]{:S(2)}, u32[]{:S(2)}) collective-permute-start(bf16[256,2304]{1,0:T(8,128)(2,1)} %get-tuple-element.24), channel_id=1, source_target_pairs={{0,12},{1,13},{2,14},{3,15},{4,0},{5,1},{6,2},{7,3},{8,4},{9,5},{1... | collective-permute-start | bytes 3538952 | tf_op jit(solution)/shard_map/ppermute | solution.py:25
  190.0 11.2 %collective-permute-start.28 = (bf16[64,2304]{1,0:T(8,128)(2,1)S(1)}, bf16[64,2304]{1,0:T(8,128)(2,1)S(1)}, u32[]{:S(2)}, u32[]{:S(2)}) collective-permute-start(bf16[64,2304]{1,0:T(8,128)(2,1)S(1)} %get-tuple-element.26), channel_id=1, source_target_pairs={{0,1},{1,2},{2,3},{3,0},{4,5},{5,6},{6,7},{7,4},{8,9},{9,10},{10,1... | collective-permute-start | bytes 884744 | tf_op jit(solution)/shard_map/ppermute | solution.py:25
  190.8 10.5 %collective-permute-start.29 = (bf16[64,2304]{1,0:T(8,128)(2,1)S(1)}, bf16[64,2304]{1,0:T(8,128)(2,1)S(1)}, u32[]{:S(2)}, u32[]{:S(2)}) collective-permute-start(bf16[64,2304]{1,0:T(8,128)(2,1)S(1)} %get-tuple-element.27), channel_id=1, source_target_pairs={{0,2},{1,3},{2,0},{3,1},{4,6},{5,7},{6,4},{7,5},{8,10},{9,11},{10,... | collective-permute-start | bytes 884744 | tf_op jit(solution)/shard_map/ppermute | solution.py:25
  192.4 9.7 %collective-permute-start.30 = (bf16[64,2304]{1,0:T(8,128)(2,1)S(1)}, bf16[64,2304]{1,0:T(8,128)(2,1)S(1)}, u32[]{:S(2)}, u32[]{:S(2)}) collective-permute-start(bf16[64,2304]{1,0:T(8,128)(2,1)S(1)} %get-tuple-element.28), channel_id=1, source_target_pairs={{0,3},{1,0},{2,1},{3,2},{4,7},{5,4},{6,5},{7,6},{8,11},{9,8},{10,9... | collective-permute-start | bytes 884744 | tf_op jit(solution)/shard_map/ppermute | solution.py:25

commit v2 on v0

v2 whole, which is shorter than its diff:
```python
import functools

import jax
import jax.numpy as jnp
from jax import lax
from jax.experimental import pallas as pl
from jax.experimental.pallas import tpu as pltpu
from jax.sharding import PartitionSpec as P

HEADS = 48
BF = jnp.bfloat16
F32 = jnp.float32
VMEM_LIMIT = 20 * 1024 * 1024
ATTEND_VMEM = 57 * 1024 * 1024
PARTIAL_SCALE = 32.0


def flat_perm(place):
    pairs = []
    for gx in range(8):
        for gy in range(16):
            z, c, y, x = gx // 2, gx % 2, gy // 4, gy % 4
            z2, c2, y2, x2 = place(z, c, y, x)
            pairs.append((gx * 16 + gy, ((z2 % 4) * 2 + c2) * 16 + (y2 % 4) * 4 + x2 % 4))
    return pairs


def send(value, place):
    return lax.ppermute(value, ("gx", "gy"), flat_perm(place))


def first_axis(d):
    return lambda z, c, y, x: (z, c, y, x + d) if c == 0 else (z, c, y + d, x)


def second_axis(d):
    return lambda z, c, y, x: (z, c, y + d, x) if c == 0 else (z, c, y, x + d)


def z_axis(d):
    return lambda z, c, y, x: (z + d, c, y, x)


def other_core(z, c, y, x):
    return (z, 1 - c, y, x)


def whole(shape):
    return pl.BlockSpec(shape, lambda *_: (0,) * len(shape))


IN_VMEM = pl.BlockSpec(memory_space=pltpu.VMEM)
IN_SMEM = pl.BlockSpec(memory_space=pltpu.SMEM)
IN_HBM = pl.BlockSpec(memory_space=pltpu.HBM)


def kernel_call(body, grid, in_specs, out_specs, out_shape, scratch, flops, nbytes, name):
    return pl.pallas_call(
        body,
        grid_spec=pltpu.PrefetchScalarGridSpec(
            num_scalar_prefetch=1,
            grid=grid,
            in_specs=in_specs,
            out_specs=out_specs,
            scratch_shapes=scratch,
        ),
        out_shape=out_shape,
        compiler_params=pltpu.CompilerParams(vmem_limit_bytes=VMEM_LIMIT),
        cost_estimate=pl.CostEstimate(flops=flops, bytes_accessed=nbytes, transcendentals=0),
        name=name,
    )


def one_step(body, in_specs, out_shape, scratch, flops, nbytes, name):
    many = isinstance(out_shape, list)
    return pl.pallas_call(
        body,
        in_specs=in_specs,
        out_specs=[IN_VMEM] * len(out_shape) if many else IN_VMEM,
        out_shape=out_shape,
        scratch_shapes=scratch,
        compiler_params=pltpu.CompilerParams(vmem_limit_bytes=VMEM_LIMIT),
        cost_estimate=pl.CostEstimate(flops=flops, bytes_accessed=nbytes, transcendentals=0),
        name=name,
    )


def one_hot(rows, cols, source):
    row = lax.broadcasted_iota(jnp.int32, (rows, cols), 0)
    col = lax.broadcasted_iota(jnp.int32, (rows, cols), 1)
    return jnp.where(col == source(row), 1.0, 0.0).astype(BF)


def one_hot_rows(rows, cols):
    row = lax.broadcasted_iota(jnp.int32, (rows, cols), 0)
    col = lax.broadcasted_iota(jnp.int32, (rows, cols), 1)
    return jnp.where(col % rows == row, 1.0, 0.0).astype(BF)


def row_statistics_body(tok, out):
    value = tok[...].astype(F32)
    rows = value.shape[0]
    mean = jnp.mean(value, axis=-1, keepdims=True)
    centred = value - mean
    squares = jnp.sum(centred * centred, axis=-1, keepdims=True)
    lane = lax.broadcasted_iota(jnp.int32, (rows, 128), 1)
    cols = jnp.where(lane == 0, mean, jnp.where(lane == 1, squares, 0.0))
    cols = jnp.concatenate([cols, jnp.zeros((128 - rows, 128), F32)], axis=0)
    out[0] = jnp.transpose(cols)[:8]


def row_statistics(tok):
    return one_step(
        row_statistics_body,
        [IN_VMEM],
        jax.ShapeDtypeStruct((1, 8, 128), F32),
        [],
        6 * tok.size,
        tok.size * 2,
        "row_statistics",
    )(tok)


def combine(tiles, count, width_all):
    def body(*refs):
        held = [ref[...] for ref in refs[:-1]]
        mean = sum(h[:, 0:1] for h in held) * (1.0 / len(held))
        squares = sum(h[:, 1:2] for h in held)
        spread = sum((h[:, 0:1] - mean) * (h[:, 0:1] - mean) for h in held)
        squares = squares + spread * float(count)
        if width_all:
            squares = lax.rsqrt(squares * (1.0 / width_all) + 1e-05)
        refs[-1][:, 0:1] = mean
        refs[-1][:, 1:2] = squares

    shape = tiles[0].shape
    return one_step(
        body,
        [IN_VMEM] * len(tiles),
        jax.ShapeDtypeStruct(shape, F32),
        [],
        1024 * 10,
        tiles[0].size * 4 * (len(tiles) + 1),
        "combine",
    )(*tiles)


def normalise_body(tok, tile, gain, out):
    cols = jnp.transpose(jnp.concatenate([tile[0], jnp.zeros((120, 128), F32)], axis=0))
    value = tok[...].astype(F32)
    out[...] = ((value - cols[:64, 0:1]) * cols[:64, 1:2] * gain[...]).astype(BF)


def normalise(tok, tile, gain):
    return one_step(
        normalise_body,
        [IN_VMEM] * 3,
        jax.ShapeDtypeStruct(tok.shape, BF),
        [],
        tok.size * 6,
        tok.size * 4,
        "normalise",
    )(tok, tile, gain)


def project_body(places, place, *refs):
    count = len(places)
    halves = refs[: 2 * count]
    wq, wkv = refs[2 * count : 2 * count + 2]
    far, near, rows, sums, sems_in, sems_out = refs[-6:]
    x, y, c = place[0], place[1], place[3]
    nq = wq.shape[1]
    loads = [
        pltpu.make_async_copy(
            ref, rows.at[k // 2, pl.ds((k % 2) * 128, 128)], sems_in.at[k // 2, k % 2]
        )
        for k, ref in enumerate(halves)
    ]
    for copy in loads:
        copy.start()
    for i, d1 in enumerate(places):
        loads[2 * i].wait()
        loads[2 * i + 1].wait()
        sums[i, :, :nq] = jnp.dot(rows[i], wq[...], preferred_element_type=F32)
        sums[i, :, nq:] = jnp.dot(rows[i], wkv[...], preferred_element_type=F32)
        for d2 in range(4):
            bx = (x + jnp.where(c == 0, d2, d1)) & 3
            by = (y + jnp.where(c == 0, d1, d2)) & 3
            slot = by * 2 + (bx & 1)
            source = sums.at[i, pl.ds(d2 * 64, 64)]

            @pl.when((bx >> 1) == c)
            def _(source=source, slot=slot, sem=sems_out.at[i, d2]):
                pltpu.make_async_copy(source, near.at[slot], sem).start()

            @pl.when((bx >> 1) != c)
            def _(source=source, slot=slot, sem=sems_out.at[i, d2]):
                pltpu.make_async_copy(source, far.at[slot], sem).start()

    for i in range(count):
        for d2 in range(4):
            source = sums.at[i, pl.ds(d2 * 64, 64)]
            pltpu.make_async_copy(source, near.at[0], sems_out.at[i, d2]).wait()


def project(places, place, halves, wq, wkv, held):
    width, nq = wq.shape
    n = nq + wkv.shape[1]
    count = len(places)
    rows = 256 * count
    return pl.pallas_call(
        functools.partial(project_body, places),
        in_specs=[IN_SMEM] + [IN_HBM] * (2 * count) + [IN_VMEM] * 2 + [IN_HBM] * len(held),
        out_specs=[IN_HBM] * 2,
        out_shape=[jax.ShapeDtypeStruct((8, 64, n), F32)] * 2,
        scratch_shapes=[
            pltpu.VMEM((count, 256, width), BF),
            pltpu.VMEM((count, 256, n), F32),
            pltpu.SemaphoreType.DMA((count, 2)),
            pltpu.SemaphoreType.DMA((count, 4)),
        ],
        input_output_aliases={2 * count + 3 + i: i for i in range(len(held))},
        compiler_params=pltpu.CompilerParams(vmem_limit_bytes=VMEM_LIMIT),
        cost_estimate=pl.CostEstimate(
            flops=2 * rows * width * n,
            bytes_accessed=rows * width * 2 + width * n * 2 + rows * n * 4,
            transcendentals=0,
        ),
        name="project",
    )(place, *halves, wq, wkv, *held)


def reorder_query_body(total, out):
    order = one_hot(
        128, 128, lambda i: (i & 64) + ((i >> 2) & 1) * 32 + ((i >> 3) & 7) * 4 + (i & 3)
    )
    moved = jnp.dot(order, total[...], preferred_element_type=F32)
    out[...] = moved.reshape(16, 8, moved.shape[-1]).astype(BF)


def reorder_query(total):
    n = total.shape[-1]
    return one_step(
        reorder_query_body,
        [IN_VMEM],
        jax.ShapeDtypeStruct((16, 8, n), BF),
        [],
        2 * 128 * 128 * n,
        128 * n * 4,
        "reorder_query",
    )(total)


def attend_body(lens, x, keys_hbm, values_hbm, out, keys, values, sems):
    nq = out.shape[-1]
    rows, length, dim = keys.shape
    copies = []
    for row in range(rows):
        copies.append(pltpu.make_async_copy(keys_hbm.at[row], keys.at[row], sems.at[0, row]))
        copies.append(pltpu.make_async_copy(values_hbm.at[row], values.at[row], sems.at[1, row]))
    for copy in copies:
        copy.start()
    piece = 2 * dim // 16
    factor = dim ** (-0.5)
    heads = nq // dim
    flat = x[...].astype(F32).reshape(128, x.shape[-1]).astype(BF)

    lane = lax.broadcasted_iota(jnp.int32, (128, 16 * piece), 1)
    sub = lax.broadcasted_iota(jnp.int32, (128, 16 * piece), 0)
    spread = jnp.where((lane % piece == sub) & (sub < piece), 1.0, 0.0).astype(BF)
    tiled = jnp.dot(flat[:, nq : nq + 128], spread, preferred_element_type=F32)
    tiled = jnp.where(lane // piece == sub >> 3, tiled, 0.0).astype(BF)
    fresh = jnp.dot(one_hot_rows(8, 128), tiled, preferred_element_type=F32)

    count = heads * 32
    step = lax.broadcasted_iota(jnp.int32, (count, 1), 0) & 1
    position = lax.broadcasted_iota(jnp.int32, (1, length), 1)
    placed = None
    for row in range(rows):
        if row % 2 == 0:
            for copy in copies[2 * row : 2 * row + 4]:
                copy.wait()
        pick = one_hot(32, 128, lambda i: (i >> 1) * 8 + (i & 1) * 4 + row)
        mine = jnp.dot(pick, flat[:, :nq], preferred_element_type=F32).astype(BF)
        query = jnp.concatenate([mine[:, h * dim : (h + 1) * dim] for h in range(heads)], axis=0)
        scores = (
            lax.dot_general(
                query, keys[row], (((1,), (1,)), ((), ())), preferred_element_type=F32
            )
            * factor
        )
        scores = jnp.where(position < lens[row], scores, -1e30)
        query_f = query.astype(F32)
        key_0, key_1 = fresh[row : row + 1, :dim], fresh[rows + row : rows + row + 1, :dim]
        val_0, val_1 = fresh[row : row + 1, dim:], fresh[rows + row : rows + row + 1, dim:]
        new_0 = jnp.sum(query_f * key_0, axis=-1, keepdims=True) * factor
        new_1 = jnp.sum(query_f * key_1, axis=-1, keepdims=True) * factor
        new_1 = jnp.where(step == 1, new_1, -1e30)
        top = jnp.maximum(jnp.max(scores, axis=-1, keepdims=True), jnp.maximum(new_0, new_1))
        exp_c = jnp.exp(scores - top)
        exp_0 = jnp.exp(new_0 - top)
        exp_1 = jnp.exp(new_1 - top)
        scale = 1.0 / (jnp.sum(exp_c, axis=-1, keepdims=True) + exp_0 + exp_1)
        weight = (exp_c * scale).astype(BF)
        mixed = jnp.dot(weight, values[row], preferred_element_type=F32)
        mixed = mixed + (exp_0 * scale).astype(BF).astype(F32) * val_0
        mixed = mixed + (exp_1 * scale).astype(BF).astype(F32) * val_1
        mixed = mixed.astype(BF)
        mixed = jnp.concatenate([mixed[h * 32 : (h + 1) * 32] for h in range(heads)], axis=1)
        sub = lax.broadcasted_iota(jnp.int32, (128, 32), 0)
        lane = lax.broadcasted_iota(jnp.int32, (128, 32), 1)
        back = jnp.where(sub == (lane >> 1) * 8 + (lane & 1) * 4 + row, 1.0, 0.0).astype(BF)
        term = jnp.dot(back, mixed, preferred_element_type=F32)
        placed = term if placed is None else placed + term
    out[...] = placed.reshape(16, 8, nq).astype(BF)


def attend(lens, x, keys, values, nq):
    rows, length, dim = keys.shape
    return pl.pallas_call(
        attend_body,
        in_specs=[IN_SMEM, IN_VMEM, IN_HBM, IN_HBM],
        out_specs=IN_VMEM,
        out_shape=jax.ShapeDtypeStruct((16, 8, nq), BF),
        scratch_shapes=[
            pltpu.VMEM(keys.shape, BF),
            pltpu.VMEM(values.shape, BF),
            pltpu.SemaphoreType.DMA((2, rows)),
        ],
        compiler_params=pltpu.CompilerParams(vmem_limit_bytes=ATTEND_VMEM),
        cost_estimate=pl.CostEstimate(
            flops=4 * rows * 96 * length * dim, bytes_accessed=4 * keys.size, transcendentals=0
        ),
        name="attend",
    )(lens, x, keys, values)


def output_far_body(place, *refs):
    mixed, w_out = refs[:8], refs[8]
    left, half_a, half_b = refs[9:]
    z, c = place[2], place[3]
    order = one_hot(
        128, 128, lambda o: (o & 64) + ((o >> 2) & 7) * 8 + ((o >> 5) & 1) * 4 + (o & 3)
    )
    for k in range(8):
        bz = (z + k % 4) & 3
        bc = c if k < 4 else 1 - c
        value = mixed[k][...].astype(F32).reshape(128, mixed[k].shape[-1]).astype(BF)
        moved = jnp.dot(order, value, preferred_element_type=F32).astype(BF)
        left[bz * 4 + bc * 2] = moved[:64]
        left[bz * 4 + bc * 2 + 1] = moved[64:]
    partial_rows(place, 2, left, w_out, (half_a, half_b))


def partial_rows(place, d, left, w_out, outs):
    x, y, c = place[0], place[1], place[3]
    group = (jnp.where(c == 0, y, x) + d) & 3
    parts = [left[jnp.where(c == 0, group * 4 + i, i * 4 + group)] for i in range(4)]
    rows = jnp.concatenate(parts, axis=0)
    chunk = w_out.shape[1] // 3
    for j in range(3):
        cols = pl.ds(j * chunk, chunk)
        value = jnp.dot(rows, w_out[:, cols], preferred_element_type=F32).astype(BF)
        at = 0
        for out in outs:
            out[:, cols] = value[at : at + out.shape[0]]
            at += out.shape[0]


def output_far(place, mixed, w_out):
    depth, width = w_out.shape
    return one_step(
        output_far_body,
        [IN_SMEM] + [IN_VMEM] * 9,
        [jax.ShapeDtypeStruct((16, 64, depth), BF)] + [jax.ShapeDtypeStruct((128, width), BF)] * 2,
        [],
        2 * 256 * depth * width,
        1024 * depth * 4 + depth * width * 2 + 256 * width * 2,
        "output_far",
    )(place, *mixed, w_out)


def output_near_body(place, left, w_out, plus_a, plus_b, minus_a, minus_b):
    partial_rows(place, 1, left, w_out, (plus_a, plus_b))
    partial_rows(place, 3, left, w_out, (minus_a, minus_b))


def output_near(place, left, w_out):
    depth, width = w_out.shape
    return one_step(
        output_near_body,
        [IN_SMEM] + [IN_VMEM] * 2,
        [jax.ShapeDtypeStruct((128, width), BF)] * 4,
        [],
        4 * 256 * depth * width,
        1024 * depth * 2 + depth * width * 2 + 512 * width * 2,
        "output_near",
    )(place, left, w_out)


def output_own_body(place, left, w_out, out):
    partial_rows(place, 0, left, w_out, (out,))


def output_own(place, left, w_out):
    depth, width = w_out.shape
    return one_step(
        output_own_body,
        [IN_SMEM] + [IN_VMEM] * 2,
        jax.ShapeDtypeStruct((256, width), BF),
        [],
        2 * 256 * depth * width,
        1024 * depth * 2 + depth * width * 2 + 256 * width * 2,
        "output_own",
    )(place, left, w_out)


def pair_add_body(a0, a1, b0, b1, a, b):
    a[...] = (a0[...].astype(F32) + a1[...].astype(F32)).astype(BF)
    b[...] = (b0[...].astype(F32) + b1[...].astype(F32)).astype(BF)


def pair_add(a0, a1, b0, b1):
    return one_step(
        pair_add_body,
        [IN_VMEM] * 4,
        [jax.ShapeDtypeStruct(a0.shape, BF)] * 2,
        [],
        2 * a0.size,
        a0.size * 12,
        "pair_add",
    )(a0, a1, b0, b1)


def group_sum_body(place, a, b0, b1, c0, c1, own, s1, s2, s3):
    step = pl.program_id(0)
    low = ((jnp.where(place[3] == 0, place[0], place[1]) + step) & 3) < 2
    value = a[...].astype(F32)
    value = value + jnp.where(low, b0[...], b1[...]).astype(F32)
    value = value + jnp.where(low, c0[...], c1[...]).astype(F32)

    @pl.when(step == 0)
    def _():
        own[...] = value

    for d, ref in ((1, s1), (2, s2), (3, s3)):

        @pl.when(step == d)
        def _(ref=ref):
            ref[...] = value.astype(BF)


def group_sum(place, own, halves):
    width = own.shape[-1]
    mine = lambda d, p: (jnp.where(p[3] == 0, p[0], p[1]) + d) & 3
    block = pl.BlockSpec((64, width), lambda d, p: (mine(d, p), 0))
    half = pl.BlockSpec((64, width), lambda d, p: (mine(d, p) & 1, 0))
    return kernel_call(
        group_sum_body,
        (4,),
        [block] + [half] * 4,
        [whole((64, width))] * 4,
        [jax.ShapeDtypeStruct((64, width), F32)] + [jax.ShapeDtypeStruct((64, width), BF)] * 3,
        [],
        1024 * width,
        1024 * width * 2,
        "group_sum",
    )(place, own, *halves)


def last_sum_body(place, own, r1, r2, r3, out):
    total = own[...] + r1[...].astype(F32) + r2[...].astype(F32) + r3[...].astype(F32)
    out[...] = total.reshape(out.shape).astype(BF)


def last_sum(place, own, got):
    rows, width = own.shape
    return one_step(
        last_sum_body,
        [IN_SMEM] + [IN_VMEM] * 4,
        jax.ShapeDtypeStruct((2, rows // 2, width), BF),
        [],
        rows * width * 4,
        rows * width * 12,
        "last_sum",
    )(place, own, *got)


def after(value, other):
    return lax.optimization_barrier((value, other))


def gather_and_project(place, tok, gain, wq, wkv, width_all):
    count = tok.shape[1]
    stat = row_statistics(tok)
    stat = combine([stat, send(stat, other_core)], count, 0)
    stat = combine([stat, send(stat, lambda z, c, y, x: (z ^ 1, c, y, x))], count * 2, 0)
    stat = combine(
        [stat, send(stat, lambda z, c, y, x: (z ^ 2, c, y, x))], count * 4, width_all
    )
    tok = normalise(tok, stat, gain)
    b1, b2, b3 = [send(tok, first_axis(d)) for d in (-1, 2, 1)]
    low = jnp.concatenate([tok, b1], axis=0)
    high = jnp.concatenate([b2, b3], axis=0)
    minus_low = send(low, second_axis(1))
    plus_high = send(high, second_axis(-1))
    minus_high = send(high, second_axis(1))
    plus_low = send(low, second_axis(-1))
    held = project((0,), place, (low, high), wq, wkv, ())
    near, minus_low = after(held[1], minus_low)
    near, plus_high = after(near, plus_high)
    twice_low = send(minus_low, second_axis(1))
    twice_high = send(plus_high, second_axis(-1))
    held = (held[0], near)
    halves = (plus_low, plus_high, minus_low, minus_high)
    held = project((1, 3), place, halves, wq, wkv, held)
    return project((2,), place, (twice_low, twice_high), wq, wkv, held)


def per_device(tokens, norm_gain, w_query, w_kv, w_out, cache_keys, cache_values, lengths):
    gx, gy = lax.axis_index("gx"), lax.axis_index("gy")
    z, c, y, x = gx // 2, gx % 2, gy // 4, gy % 4
    width = tokens.shape[2]
    nq = w_query.shape[1]
    piece = w_kv.shape[1] // 16
    place = jnp.stack([x, y, z, c]).astype(jnp.int32)
    gain = norm_gain[None]
    wkv = lax.dynamic_slice_in_dim(w_kv, gy * piece, piece, 1)
    wkv = jnp.pad(wkv, ((0, 0), (0, 128 - piece)))

    far, near = gather_and_project(
        place, tokens.reshape(64, width), gain, w_query, wkv, width * 8
    )
    n = near.shape[-1]
    far_got = send(far, other_core).reshape(4, 128, n)
    near = near.reshape(4, 128, n)

    def chip_sum(d):
        at = (z + d) & 3
        return lax.dynamic_index_in_dim(near, at, 0, False) + lax.dynamic_index_in_dim(
            far_got, at, 0, False
        )

    got = [
        send((chip_sum(d) * PARTIAL_SCALE).astype(jnp.float16), z_axis(d)) for d in (2, 1, 3)
    ]
    query = chip_sum(0)
    for g in got:
        query = query + g.astype(F32) * (1.0 / PARTIAL_SCALE)
    query = reorder_query(query.astype(BF))
    query = lax.all_to_all(query, "gy", 0, 0)
    mixed = attend(lengths, query, cache_keys, cache_values, nq)
    mixed = lax.all_to_all(mixed, "gy", 0, 0)
    same = [mixed, send(mixed, z_axis(-1)), send(mixed, z_axis(2)), send(mixed, z_axis(1))]
    cross = [send(m, other_core) for m in same]

    left, far_a, far_b = output_far(place, same + cross, w_out)
    got_a = send(far_a, second_axis(1))
    got_b = send(far_b, second_axis(-1))
    plus_a, plus_b, minus_a, minus_b = output_near(place, left, w_out)
    from_minus_b = send(plus_b, second_axis(1))
    from_plus_a = send(minus_a, second_axis(-1))
    own = output_own(place, left, w_out)
    plus_a, minus_b = pair_add(plus_a, got_a, minus_b, got_b)
    from_minus_a = send(plus_a, second_axis(1))
    from_plus_b = send(minus_b, second_axis(-1))
    own, s1, s2, s3 = group_sum(
        place, own, [from_minus_a, from_minus_b, from_plus_a, from_plus_b]
    )
    got = [send(s1, first_axis(1)), send(s2, first_axis(2)), send(s3, first_axis(-1))]
    return last_sum(place, own, got)


def solution(mesh):
    in_specs = (
        P(None, "gy", "gx"),
        P("gx"),
        P("gx", "gy"),
        P("gx", None),
        P("gy", "gx"),
        P(("gx", "gy"), None, None),
        P(("gx", "gy"), None, None),
        P(("gx", "gy")),
    )
    out_specs = P(None, "gy", "gx")
    return jax.shard_map(
        per_device, mesh=mesh, in_specs=in_specs, out_specs=out_specs, check_vma=False
    )
```

time: 674 us -> 173 us (0.26); the launches traced: 661 us -> 173 us
  waiting for transfers between devices: 244 us -> 63.9 us
  other arithmetic: 153 us -> 3.45 us
  local copies, waits for them, and re-layouts: 121 us -> 6.42 us
  blocking collectives: 79.9 us -> 25.2 us
  matrix products: 41.3 us -> 0 us
  Pallas kernels: 0 us -> 33.1 us
  starting transfers between devices: 7.51 us -> 40.3 us
  between operations: 13.9 us -> 0.22 us
    reduce_scatter x6 -> x0, waiting for transfers between devices: 153 us -> none  [the longest x2 72.4 us: per_device(): lax.psum_scatter(partial_out.astype(jnp.bfloat16), 'gy', scatter_dimensio...]
    unnamed x4 -> x0, other arithmetic: 142 us -> none
    all_gather x2 -> x0, waiting for transfers between devices: 85.5 us -> none  [per_device(): gathered = lax.all_gather(normed, 'gy', axis=1, tiled=True)]
    ppermute x0 -> x32, waiting for transfers between devices: none -> 63.9 us  [send(): return lax.ppermute(value, ('gx', 'gy'), flat_perm(place))]
    unnamed x23 -> x15, local copies, waits for them, and re-layouts: 46.7 us -> 5.34 us
    dot_general x13 -> x0, matrix products: 41.3 us -> none  [the longest x2 11.8 us: per_device(): jnp.einsum('sbd,dc->sbc', gathered, w_query, preferred_element_type=jnp.f...]
    all_to_all x12 -> x0, local copies, waits for them, and re-layouts: 40.4 us -> none  [the longest x6 30 us: per_device(): lax.all_to_all(finish_mixed, 'gy', split_axis=2, concat_axis=1, tiled=True)]
    ppermute x0 -> x32, starting transfers between devices: none -> 40.3 us  [send(): return lax.ppermute(value, ('gx', 'gy'), flat_perm(place))]
  transfers between devices with their start and end apart: 9 -> 32, of which waited for: 7 -> 23; matrix products, arithmetic and copies ran while one was open for 46% -> 1% of each run, Pallas kernels for 0% -> 9%
where the time goes in v2:
time: 173 us
  waiting for transfers between devices  63.9 us (37%)
  starting transfers between devices  40.3 us (23%)
  Pallas kernels  33.1 us (19%)
  blocking collectives  25.2 us (15%)
  local copies, waits for them, and re-layouts  6.42 us (4%)
  other arithmetic  3.45 us (2%)
    ppermute x32, waiting for transfers between devices, send(): return lax.ppermute(value, ('gx', 'gy'), flat_perm(place))  63.9 us
    ppermute x32, starting transfers between devices, send(): return lax.ppermute(value, ('gx', 'gy'), flat_perm(place))  40.3 us
    pallas_call x3, Pallas kernels, project(): pl.pallas_call(functools.partial(project_body, places), in_specs=[IN_SMEM...  13.9 us
    all_to_all x1, blocking collectives, per_device(): query = lax.all_to_all(query, 'gy', 0, 0)  13.4 us
    all_to_all x1, blocking collectives, per_device(): mixed = lax.all_to_all(mixed, 'gy', 0, 0)  11.8 us
    pallas_call x1, Pallas kernels, attend(): pl.pallas_call(attend_body, in_specs=[IN_SMEM, IN_VMEM, IN_HBM, IN_HBM],...  8.91 us
    unnamed x15, local copies, waits for them, and re-layouts  5.34 us
  transfers between devices with their start and end apart: 32, of which 23 were waited for; matrix products, arithmetic and copies ran while one was open for 1% of the time, Pallas kernels for 9%

profile of v2, /device:TPU:24, one launch (start us, length us, event | category | flops | bytes accessed | tf_op | source)
XLA Modules:
  0.0 172.6 jit_solution(6098505419273794488)
XLA Ops:
  0.0 1.1 copy-done.5
  1.1 0.3 row_statistics.1.refs_0_
  1.4 1.2 collective-permute-done.refs_1_
  2.6 1.9 %collective-permute-start.1 = (f32[1,8,128]{2,1,0:T(8,128)S(1)}, f32[1,8,128]{2,1,0:T(8,128)S(1)}, u32[]{:S(2)}, u32[]{:S(2)}) collective-permute-start(f32[1,8,128]{2,1,0:T(8,128)S(1)} %combine.3.refs_0_), channel_id=1, source_target_pairs={{0,32},{1,33},{2,34},{3,35},{4,36},{5,37},{6,38},{7,39},{8,40},{9,... | collective-permute-start | bytes 12296 | tf_op jit(solution)/shard_map/ppermute | solution.py:29
  4.5 1.7 collective-permute-done.1.refs_1_
  6.2 3.9 %collective-permute-start.2 = (f32[1,8,128]{2,1,0:T(8,128)S(1)}, f32[1,8,128]{2,1,0:T(8,128)S(1)}, u32[]{:S(2)}, u32[]{:S(2)}) collective-permute-start(f32[1,8,128]{2,1,0:T(8,128)S(1)} %combine.4.refs_0_), channel_id=1, source_target_pairs={{0,64},{1,65},{2,66},{3,67},{4,68},{5,69},{6,70},{7,71},{8,72},{9,... | collective-permute-start | bytes 12296 | tf_op jit(solution)/shard_map/ppermute | solution.py:29
  10.1 0.7 broadcast_in_dim.3.gain
  10.8 0.9 collective-permute-done.2.refs_1_
  11.7 1.0 copy-done.6
  12.9 2.8 %collective-permute-start.3 = (bf16[64,2304]{1,0:T(8,128)(2,1)S(1)}, bf16[64,2304]{1,0:T(8,128)(2,1)S(1)}, u32[]{:S(2)}, u32[]{:S(2)}) collective-permute-start(bf16[64,2304]{1,0:T(8,128)(2,1)S(1)} %normalise.1), channel_id=1, source_target_pairs={{0,3},{1,0},{2,1},{3,2},{4,7},{5,4},{6,5},{7,6},{8,11},{9,8},{10,9... | collective-permute-start | bytes 884744 | tf_op jit(solution)/shard_map/ppermute | solution.py:29
  15.7 0.8 collective-permute-start.4
  16.5 0.9 collective-permute-start.5
  17.4 5.7 %collective-permute-done.3 = bf16[64,2304]{1,0:T(8,128)(2,1)S(1)} collective-permute-done((bf16[64,2304]{1,0:T(8,128)(2,1)S(1)}, bf16[64,2304]{1,0:T(8,128)(2,1)S(1)}, u32[]{:S(2)}, u32[]{:S(2)}) %collective-permute-start.3) | collective-permute-done | bytes 294944 | tf_op jit(solution)/shard_map/ppermute | solution.py:29
  23.5 0.6 collective-permute-done.4
  24.1 4.8 %collective-permute-done.5 = bf16[64,2304]{1,0:T(8,128)(2,1)S(1)} collective-permute-done((bf16[64,2304]{1,0:T(8,128)(2,1)S(1)}, bf16[64,2304]{1,0:T(8,128)(2,1)S(1)}, u32[]{:S(2)}, u32[]{:S(2)}) %collective-permute-start.5) | collective-permute-done | bytes 294944 | tf_op jit(solution)/shard_map/ppermute | solution.py:29
  28.9 2.2 %collective-permute-start.8 = (bf16[128,2304]{1,0:T(8,128)(2,1)S(1)}, bf16[128,2304]{1,0:T(8,128)(2,1)}, u32[]{:S(2)}, u32[]{:S(2)}) collective-permute-start(bf16[128,2304]{1,0:T(8,128)(2,1)S(1)} %constant_dynamic-update-slice_fusion.refs_1_), channel_id=1, source_target_pairs={{0,12},{1,13},{2,14},{3,15},{4,0},{5,1},{6,2},{7,3},{8,4},{9,5},{1... | collective-permute-start | bytes 1769480 | tf_op jit(solution)/shard_map/ppermute | solution.py:29
  31.5 1.1 collective-permute-start.11
  32.6 1.0 collective-permute-start.10
  33.7 2.0 %copy-done.1 = bf16[2304,768]{1,0:T(8,128)(2,1)S(1)} copy-done((bf16[2304,768]{1,0:T(8,128)(2,1)S(1)}, bf16[2304,768]{1,0:T(8,128)(2,1)}, u32[]{:S(2)}) %copy-start.1) | copy-done | bytes 3538968
  35.7 3.6 %project.3 = (f32[8,64,896]{2,1,0:T(8,128)}, f32[8,64,896]{2,1,0:T(8,128)S(1)}) custom-call(s32[4]{0:T(128)S(1)} %pad_add_fusion.place, bf16[128,2304]{1,0:T(8,128)(2,1)S(1)} %pad_maximum_fusion.refs_0_, bf16[128,2304]{1,0:T(8,128)(2,1)S(1)} %constant_dynamic-update-slice_fusion.refs_1_, bf16[2304,768]{1,0:T(8,128)(2,1)S(1)} %copy-done.1, ...), custom_call_target="tpu_custom_call" | custom-call | flops 1056964608 | bytes 6225920 | tf_op jit(solution)/shard_map/project/pallas_call | solution.py:211
  39.3 0.9 collective-permute-done.8.refs_1_
  40.2 1.0 collective-permute-start.9
  41.1 2.3 %collective-permute-start.7 = (bf16[128,2304]{1,0:T(8,128)(2,1)}, bf16[128,2304]{1,0:T(8,128)(2,1)S(1)}, u32[]{:S(2)}, u32[]{:S(2)}) collective-permute-start(bf16[128,2304]{1,0:T(8,128)(2,1)} %collective-permute-done.6.refs_2_), channel_id=1, source_target_pairs={{0,4},{1,5},{2,6},{3,7},{4,8},{5,9},{6,10},{7,11},{8,12},{9,13},{1... | collective-permute-start | bytes 1769480 | tf_op jit(solution)/shard_map/ppermute | solution.py:29
  43.4 3.0 %collective-permute-done.10.refs_0_ = bf16[128,2304]{1,0:T(8,128)(2,1)S(1)} collective-permute-done((bf16[128,2304]{1,0:T(8,128)(2,1)S(1)}, bf16[128,2304]{1,0:T(8,128)(2,1)S(1)}, u32[]{:S(2)}, u32[]{:S(2)}) %collective-permute-start.10) | collective-permute-done | bytes 589856 | tf_op jit(solution)/shard_map/ppermute | solution.py:29
  46.4 6.6 %project.4 = (f32[8,64,896]{2,1,0:T(8,128)}, f32[8,64,896]{2,1,0:T(8,128)S(1)}) custom-call(s32[4]{0:T(128)S(1)} %pad_add_fusion.place, bf16[128,2304]{1,0:T(8,128)(2,1)S(1)} %collective-permute-done.10.refs_0_, bf16[128,2304]{1,0:T(8,128)(2,1)} %collective-permute-done.8.refs_1_, ...), custom_call_target="tpu_custom_call", output_to_operand_aliasing={{0}: (7, {}), {1}: (8, {})} | custom-call | flops 2113929216 | bytes 8323072 | tf_op jit(solution)/shard_map/project/pallas_call | solution.py:211
  53.1 3.6 %project.5 = (f32[8,64,896]{2,1,0:T(8,128)}, f32[8,64,896]{2,1,0:T(8,128)S(1)}) custom-call(s32[4]{0:T(128)S(1)} %pad_add_fusion.place, bf16[128,2304]{1,0:T(8,128)(2,1)S(1)} %collective-permute-done.7.refs_0_, bf16[128,2304]{1,0:T(8,128)(2,1)S(1)} %collective-permute-done.9.refs_1_, ...), custom_call_target="tpu_custom_call", output_to_operand_aliasing={{0}: (5, {}), {1}: (6, {})} | custom-call | flops 1056964608 | bytes 6225920 | tf_op jit(solution)/shard_map/project/pallas_call | solution.py:211
  56.7 1.2 copy-done.3
  57.9 4.1 %collective-permute-done.12 = f32[8,64,896]{2,1,0:T(8,128)} collective-permute-done((f32[8,64,896]{2,1,0:T(8,128)}, f32[8,64,896]{2,1,0:T(8,128)}, u32[]{:S(2)}, u32[]{:S(2)}) %collective-permute-start.12) | collective-permute-done | bytes 1835040 | tf_op jit(solution)/shard_map/ppermute | solution.py:29
  62.1 1.9 %fusion.3 = (f16[128,896]{1,0:T(8,128)(2,1)S(1)}, f16[128,896]{1,0:T(8,128)(2,1)S(1)}, f16[128,896]{1,0:T(8,128)(2,1)S(1)}) fusion(f32[4,128,896]{2,1,0:T(8,128)} %bitcast.6, s32[]{:T(128)S(6)} %select_n.44, f32[4,128,896]{2,1,0:T(8,128)} %bitcast.21, s32[]{:T(128)S(6)} %select_n.46, s32[]{:T(128)S(6)} %select_n.45), kind=kLoop, calls=%fused_computation.8 | loop fusion | flops 1032192 | bytes 3440652 | tf_op jit(solution)/shard_map/convert_element_type | solution.py:545
  63.9 3.9 %collective-permute-start.13 = (f16[128,896]{1,0:T(8,128)(2,1)S(1)}, f16[128,896]{1,0:T(8,128)(2,1)S(1)}, u32[]{:S(2)}, u32[]{:S(2)}) collective-permute-start(f16[128,896]{1,0:T(8,128)(2,1)S(1)} %get-tuple-element.51), channel_id=1, source_target_pairs={{0,64},{1,65},{2,66},{3,67},{4,68},{5,69},{6,70},{7,71},{8,72},{9,... | collective-permute-start | bytes 688136 | tf_op jit(solution)/shard_map/ppermute | solution.py:29
  67.8 1.0 collective-permute-start.14
  68.8 2.2 %collective-permute-start.15 = (f16[128,896]{1,0:T(8,128)(2,1)S(1)}, f16[128,896]{1,0:T(8,128)(2,1)}, u32[]{:S(2)}, u32[]{:S(2)}) collective-permute-start(f16[128,896]{1,0:T(8,128)(2,1)S(1)} %get-tuple-element.52), channel_id=1, source_target_pairs={{0,96},{1,97},{2,98},{3,99},{4,100},{5,101},{6,102},{7,103},{8,104... | collective-permute-start | bytes 688136 | tf_op jit(solution)/shard_map/ppermute | solution.py:29
  71.1 3.2 %collective-permute-done.13 = f16[128,896]{1,0:T(8,128)(2,1)S(1)} collective-permute-done((f16[128,896]{1,0:T(8,128)(2,1)S(1)}, f16[128,896]{1,0:T(8,128)(2,1)S(1)}, u32[]{:S(2)}, u32[]{:S(2)}) %collective-permute-start.13) | collective-permute-done | bytes 229408 | tf_op jit(solution)/shard_map/ppermute | solution.py:29
  74.2 4.4 %collective-permute-done.14 = f16[128,896]{1,0:T(8,128)(2,1)S(1)} collective-permute-done((f16[128,896]{1,0:T(8,128)(2,1)S(1)}, f16[128,896]{1,0:T(8,128)(2,1)S(1)}, u32[]{:S(2)}, u32[]{:S(2)}) %collective-permute-start.14) | collective-permute-done | bytes 229408 | tf_op jit(solution)/shard_map/ppermute | solution.py:29
  78.6 0.9 collective-permute-done.15
  79.5 1.5 fusion.2.total
  81.2 13.4 %all_to_all.10.x = bf16[16,8,896]{2,1,0:T(8,128)(2,1)} all-to-all(bf16[16,8,896]{2,1,0:T(8,128)(2,1)S(1)} %reorder_query.1), channel_id=1, replica_groups=mesh['gx'=8,'gy'=16] {'gy'}, dimensions={0} | all-to-all | bytes 458752 | tf_op jit(solution)/shard_map/all_to_all | solution.py:551
  94.7 8.9 %attend.1 = bf16[16,8,768]{2,1,0:T(8,128)(2,1)} custom-call(s32[4]{0:T(128)} %lens.1, bf16[16,8,896]{2,1,0:T(8,128)(2,1)} %all_to_all.10.x, bf16[4,2048,256]{2,1,0:T(8,128)(2,1)} %keys_hbm.1, bf16[4,2048,256]{2,1,0:T(8,128)(2,1)} %values_hbm.1), custom_call_target="tpu_custom_call" | custom-call | flops 805306368 | bytes 8388608 | tf_op jit(solution)/shard_map/attend/pallas_call | solution.py:320
  103.6 11.8 %all_to_all.11.refs_0_ = bf16[16,8,768]{2,1,0:T(8,128)(2,1)S(1)} all-to-all(bf16[16,8,768]{2,1,0:T(8,128)(2,1)} %attend.1), channel_id=1, replica_groups=mesh['gx'=8,'gy'=16] {'gy'}, dimensions={0} | all-to-all | bytes 393216 | tf_op jit(solution)/shard_map/all_to_all | solution.py:553
  115.4 2.6 %collective-permute-start.16 = (bf16[16,8,768]{2,1,0:T(8,128)(2,1)S(1)}, bf16[16,8,768]{2,1,0:T(8,128)(2,1)S(1)}, u32[]{:S(2)}, u32[]{:S(2)}) collective-permute-start(bf16[16,8,768]{2,1,0:T(8,128)(2,1)S(1)} %all_to_all.11.refs_0_), channel_id=1, source_target_pairs={{0,96},{1,97},{2,98},{3,99},{4,100},{5,101},{6,102},{7,103},{8,104... | collective-permute-start | bytes 589832 | tf_op jit(solution)/shard_map/ppermute | solution.py:29
  118.0 0.4 collective-permute-start.17
  118.4 0.5 collective-permute-start.18
  118.9 5.5 %collective-permute-done.16.refs_1_ = bf16[16,8,768]{2,1,0:T(8,128)(2,1)S(1)} collective-permute-done((bf16[16,8,768]{2,1,0:T(8,128)(2,1)S(1)}, bf16[16,8,768]{2,1,0:T(8,128)(2,1)S(1)}, u32[]{:S(2)}, u32[]{:S(2)}) %collective-permute-start.16) | collective-permute-done | bytes 196640 | tf_op jit(solution)/shard_map/ppermute | solution.py:29
  124.4 1.7 %collective-permute-done.17.refs_2_ = bf16[16,8,768]{2,1,0:T(8,128)(2,1)S(1)} collective-permute-done((bf16[16,8,768]{2,1,0:T(8,128)(2,1)S(1)}, bf16[16,8,768]{2,1,0:T(8,128)(2,1)S(1)}, u32[]{:S(2)}, u32[]{:S(2)}) %collective-permute-start.17) | collective-permute-done | bytes 196640 | tf_op jit(solution)/shard_map/ppermute | solution.py:29
  126.1 1.7 collective-permute-done.18.refs_3_
  127.8 1.4 collective-permute-done.22.refs_7_
  129.2 2.2 %output_far.1 = (bf16[16,64,768]{2,1,0:T(8,128)(2,1)S(1)}, bf16[128,2304]{1,0:T(8,128)(2,1)S(1)}, bf16[128,2304]{1,0:T(8,128)(2,1)S(1)}) custom-call(s32[4]{0:T(128)S(1)} %pad_add_fusion.place, bf16[16,8,768]{2,1,0:T(8,128)(2,1)S(1)} %all_to_all.11.refs_0_, bf16[16,8,768]{2,1,0:T(8,128)(2,1)S(1)} %collective-permute-done.16.refs_1_, ...), custom_call_target="tpu_custom_call" | custom-call | flops 905969664 | bytes 7864320 | tf_op jit(solution)/shard_map/output_far/pallas_call | solution.py:372
  131.4 2.5 %collective-permute-start.23 = (bf16[128,2304]{1,0:T(8,128)(2,1)S(1)}, bf16[128,2304]{1,0:T(8,128)(2,1)S(1)}, u32[]{:S(2)}, u32[]{:S(2)}) collective-permute-start(bf16[128,2304]{1,0:T(8,128)(2,1)S(1)} %get-tuple-element.40), channel_id=1, source_target_pairs={{0,4},{1,5},{2,6},{3,7},{4,8},{5,9},{6,10},{7,11},{8,12},{9,13},{1... | collective-permute-start | bytes 1769480 | tf_op jit(solution)/shard_map/ppermute | solution.py:29
  133.9 2.5 %output_near.1 = (bf16[128,2304]{1,0:T(8,128)(2,1)S(1)}, bf16[128,2304]{1,0:T(8,128)(2,1)S(1)}, bf16[128,2304]{1,0:T(8,128)(2,1)S(1)}, bf16[128,2304]{1,0:T(8,128)(2,1)S(1)}) custom-call(s32[4]{0:T(128)S(1)} %pad_add_fusion.place, bf16[16,64,768]{2,1,0:T(8,128)(2,1)S(1)} %get-tuple-element.38.left, bf16[768,2304]{1,0:T(8,128)(2,1)S(1)} %copy-done.4), custom_call_target="tpu_custom_call" | custom-call | flops 1811939328 | bytes 7471104 | tf_op jit(solution)/shard_map/output_near/pallas_call | solution.py:390
  136.5 3.3 %collective-permute-start.26 = (bf16[128,2304]{1,0:T(8,128)(2,1)S(1)}, bf16[128,2304]{1,0:T(8,128)(2,1)S(1)}, u32[]{:S(2)}, u32[]{:S(2)}) collective-permute-start(bf16[128,2304]{1,0:T(8,128)(2,1)S(1)} %get-tuple-element.44), channel_id=1, source_target_pairs={{0,4},{1,5},{2,6},{3,7},{4,8},{5,9},{6,10},{7,11},{8,12},{9,13},{1... | collective-permute-start | bytes 1769480 | tf_op jit(solution)/shard_map/ppermute | solution.py:29
  139.8 1.6 collective-permute-done.23.a1
  141.4 3.6 %collective-permute-done.24.b1 = bf16[128,2304]{1,0:T(8,128)(2,1)S(1)} collective-permute-done((bf16[128,2304]{1,0:T(8,128)(2,1)S(1)}, bf16[128,2304]{1,0:T(8,128)(2,1)S(1)}, u32[]{:S(2)}, u32[]{:S(2)}) %collective-permute-start.24) | collective-permute-done | bytes 589856 | tf_op jit(solution)/shard_map/ppermute | solution.py:29
  145.4 2.0 %collective-permute-start.28 = (bf16[128,2304]{1,0:T(8,128)(2,1)S(1)}, bf16[128,2304]{1,0:T(8,128)(2,1)S(1)}, u32[]{:S(2)}, u32[]{:S(2)}) collective-permute-start(bf16[128,2304]{1,0:T(8,128)(2,1)S(1)} %get-tuple-element.46), channel_id=1, source_target_pairs={{0,12},{1,13},{2,14},{3,15},{4,0},{5,1},{6,2},{7,3},{8,4},{9,5},{1... | collective-permute-start | bytes 1769480 | tf_op jit(solution)/shard_map/ppermute | solution.py:29
  147.4 1.6 output_own.1.a
  149.0 2.3 %collective-permute-done.27.c0 = bf16[128,2304]{1,0:T(8,128)(2,1)S(1)} collective-permute-done((bf16[128,2304]{1,0:T(8,128)(2,1)S(1)}, bf16[128,2304]{1,0:T(8,128)(2,1)S(1)}, u32[]{:S(2)}, u32[]{:S(2)}) %collective-permute-start.27) | collective-permute-done | bytes 589856 | tf_op jit(solution)/shard_map/ppermute | solution.py:29
  151.3 3.9 %collective-permute-done.25.b0 = bf16[128,2304]{1,0:T(8,128)(2,1)S(1)} collective-permute-done((bf16[128,2304]{1,0:T(8,128)(2,1)S(1)}, bf16[128,2304]{1,0:T(8,128)(2,1)S(1)}, u32[]{:S(2)}, u32[]{:S(2)}) %collective-permute-start.25) | collective-permute-done | bytes 589856 | tf_op jit(solution)/shard_map/ppermute | solution.py:29
  155.2 2.4 %collective-permute-done.28.c1 = bf16[128,2304]{1,0:T(8,128)(2,1)S(1)} collective-permute-done((bf16[128,2304]{1,0:T(8,128)(2,1)S(1)}, bf16[128,2304]{1,0:T(8,128)(2,1)S(1)}, u32[]{:S(2)}, u32[]{:S(2)}) %collective-permute-start.28) | collective-permute-done | bytes 589856 | tf_op jit(solution)/shard_map/ppermute | solution.py:29
  157.7 1.5 group_sum.1
  159.2 0.6 collective-permute-start.29
  159.8 1.6 collective-permute-start.30
  161.5 1.4 collective-permute-start.31
  162.8 7.5 %collective-permute-done.29.r1 = bf16[64,2304]{1,0:T(8,128)(2,1)S(1)} collective-permute-done((bf16[64,2304]{1,0:T(8,128)(2,1)S(1)}, bf16[64,2304]{1,0:T(8,128)(2,1)S(1)}, u32[]{:S(2)}, u32[]{:S(2)}) %collective-permute-start.29) | collective-permute-done | bytes 294944 | tf_op jit(solution)/shard_map/ppermute | solution.py:29
  170.3 0.9 collective-permute-done.31.r3
  171.2 1.4 last_sum.1
  (41 shorter events, 1.7 us)
Async XLA Ops:
  0.0 31.1 %copy-start = (bf16[2304,512]{1,0:T(8,128)(2,1)S(1)}, bf16[2304,512]{1,0:T(8,128)(2,1)}, u32[]{:S(2)}) copy-start(bf16[2304,512]{1,0:T(8,128)(2,1)} %param.11) | copy-start | bytes 7077892
  0.0 1.1 copy-start.5
  1.4 1.2 collective-permute-start
  2.6 3.6 %collective-permute-start.1 = (f32[1,8,128]{2,1,0:T(8,128)S(1)}, f32[1,8,128]{2,1,0:T(8,128)S(1)}, u32[]{:S(2)}, u32[]{:S(2)}) collective-permute-start(f32[1,8,128]{2,1,0:T(8,128)S(1)} %combine.3.refs_0_), channel_id=1, source_target_pairs={{0,32},{1,33},{2,34},{3,35},{4,36},{5,37},{6,38},{7,39},{8,40},{9,... | collective-permute-start | bytes 12296 | tf_op jit(solution)/shard_map/ppermute | solution.py:29
  6.2 5.5 %collective-permute-start.2 = (f32[1,8,128]{2,1,0:T(8,128)S(1)}, f32[1,8,128]{2,1,0:T(8,128)S(1)}, u32[]{:S(2)}, u32[]{:S(2)}) collective-permute-start(f32[1,8,128]{2,1,0:T(8,128)S(1)} %combine.4.refs_0_), channel_id=1, source_target_pairs={{0,64},{1,65},{2,66},{3,67},{4,68},{5,69},{6,70},{7,71},{8,72},{9,... | collective-permute-start | bytes 12296 | tf_op jit(solution)/shard_map/ppermute | solution.py:29
  11.7 1.0 copy-start.6
  12.9 10.3 %collective-permute-start.3 = (bf16[64,2304]{1,0:T(8,128)(2,1)S(1)}, bf16[64,2304]{1,0:T(8,128)(2,1)S(1)}, u32[]{:S(2)}, u32[]{:S(2)}) collective-permute-start(bf16[64,2304]{1,0:T(8,128)(2,1)S(1)} %normalise.1), channel_id=1, source_target_pairs={{0,3},{1,0},{2,1},{3,2},{4,7},{5,4},{6,5},{7,6},{8,11},{9,8},{10,9... | collective-permute-start | bytes 884744 | tf_op jit(solution)/shard_map/ppermute | solution.py:29
  15.7 8.3 %collective-permute-start.4 = (bf16[64,2304]{1,0:T(8,128)(2,1)S(1)}, bf16[64,2304]{1,0:T(8,128)(2,1)S(1)}, u32[]{:S(2)}, u32[]{:S(2)}) collective-permute-start(bf16[64,2304]{1,0:T(8,128)(2,1)S(1)} %normalise.1), channel_id=1, source_target_pairs={{0,2},{1,3},{2,0},{3,1},{4,6},{5,7},{6,4},{7,5},{8,10},{9,11},{10,... | collective-permute-start | bytes 884744 | tf_op jit(solution)/shard_map/ppermute | solution.py:29
  16.5 12.4 %collective-permute-start.5 = (bf16[64,2304]{1,0:T(8,128)(2,1)S(1)}, bf16[64,2304]{1,0:T(8,128)(2,1)S(1)}, u32[]{:S(2)}, u32[]{:S(2)}) collective-permute-start(bf16[64,2304]{1,0:T(8,128)(2,1)S(1)} %normalise.1), channel_id=1, source_target_pairs={{0,1},{1,2},{2,3},{3,0},{4,5},{5,6},{6,7},{7,4},{8,9},{9,10},{10,1... | collective-permute-start | bytes 884744 | tf_op jit(solution)/shard_map/ppermute | solution.py:29
  23.2 16.1 %collective-permute-start.6 = (bf16[128,2304]{1,0:T(8,128)(2,1)S(1)}, bf16[128,2304]{1,0:T(8,128)(2,1)}, u32[]{:S(2)}, u32[]{:S(2)}) collective-permute-start(bf16[128,2304]{1,0:T(8,128)(2,1)S(1)} %pad_maximum_fusion.refs_0_), channel_id=1, source_target_pairs={{0,4},{1,5},{2,6},{3,7},{4,8},{5,9},{6,10},{7,11},{8,12},{9,13},{1... | collective-permute-start | bytes 1769480 | tf_op jit(solution)/shard_map/ppermute | solution.py:29
  28.9 11.3 %collective-permute-start.8 = (bf16[128,2304]{1,0:T(8,128)(2,1)S(1)}, bf16[128,2304]{1,0:T(8,128)(2,1)}, u32[]{:S(2)}, u32[]{:S(2)}) collective-permute-start(bf16[128,2304]{1,0:T(8,128)(2,1)S(1)} %constant_dynamic-update-slice_fusion.refs_1_), channel_id=1, source_target_pairs={{0,12},{1,13},{2,14},{3,15},{4,0},{5,1},{6,2},{7,3},{8,4},{9,5},{1... | collective-permute-start | bytes 1769480 | tf_op jit(solution)/shard_map/ppermute | solution.py:29
  31.5 11.9 %collective-permute-start.11 = (bf16[128,2304]{1,0:T(8,128)(2,1)S(1)}, bf16[128,2304]{1,0:T(8,128)(2,1)S(1)}, u32[]{:S(2)}, u32[]{:S(2)}) collective-permute-start(bf16[128,2304]{1,0:T(8,128)(2,1)S(1)} %constant_dynamic-update-slice_fusion.refs_1_), channel_id=1, source_target_pairs={{0,4},{1,5},{2,6},{3,7},{4,8},{5,9},{6,10},{7,11},{8,12},{9,13},{1... | collective-permute-start | bytes 1769480 | tf_op jit(solution)/shard_map/ppermute | solution.py:29
  32.6 13.8 %collective-permute-start.10 = (bf16[128,2304]{1,0:T(8,128)(2,1)S(1)}, bf16[128,2304]{1,0:T(8,128)(2,1)S(1)}, u32[]{:S(2)}, u32[]{:S(2)}) collective-permute-start(bf16[128,2304]{1,0:T(8,128)(2,1)S(1)} %pad_maximum_fusion.refs_0_), channel_id=1, source_target_pairs={{0,12},{1,13},{2,14},{3,15},{4,0},{5,1},{6,2},{7,3},{8,4},{9,5},{1... | collective-permute-start | bytes 1769480 | tf_op jit(solution)/shard_map/ppermute | solution.py:29
  33.7 2.0 %copy-start.1 = (bf16[2304,768]{1,0:T(8,128)(2,1)S(1)}, bf16[2304,768]{1,0:T(8,128)(2,1)}, u32[]{:S(2)}) copy-start(bf16[2304,768]{1,0:T(8,128)(2,1)} %refs_2_.3) | copy-start | bytes 10616836
  35.7 10.7 %copy-start.2 = (bf16[2304,768]{1,0:T(8,128)(2,1)S(1)}, bf16[2304,768]{1,0:T(8,128)(2,1)}, u32[]{:S(2)}) copy-start(bf16[2304,768]{1,0:T(8,128)(2,1)} %refs_2_.3) | copy-start | bytes 10616836
  40.2 12.9 %collective-permute-start.9 = (bf16[128,2304]{1,0:T(8,128)(2,1)}, bf16[128,2304]{1,0:T(8,128)(2,1)S(1)}, u32[]{:S(2)}, u32[]{:S(2)}) collective-permute-start(bf16[128,2304]{1,0:T(8,128)(2,1)} %collective-permute-done.8.refs_1_), channel_id=1, source_target_pairs={{0,12},{1,13},{2,14},{3,15},{4,0},{5,1},{6,2},{7,3},{8,4},{9,5},{1... | collective-permute-start | bytes 1769480 | tf_op jit(solution)/shard_map/ppermute | solution.py:29
  41.1 11.9 %collective-permute-start.7 = (bf16[128,2304]{1,0:T(8,128)(2,1)}, bf16[128,2304]{1,0:T(8,128)(2,1)S(1)}, u32[]{:S(2)}, u32[]{:S(2)}) collective-permute-start(bf16[128,2304]{1,0:T(8,128)(2,1)} %collective-permute-done.6.refs_2_), channel_id=1, source_target_pairs={{0,4},{1,5},{2,6},{3,7},{4,8},{5,9},{6,10},{7,11},{8,12},{9,13},{1... | collective-permute-start | bytes 1769480 | tf_op jit(solution)/shard_map/ppermute | solution.py:29
  56.7 1.2 copy-start.3
  57.9 4.1 %collective-permute-start.12 = (f32[8,64,896]{2,1,0:T(8,128)}, f32[8,64,896]{2,1,0:T(8,128)}, u32[]{:S(2)}, u32[]{:S(2)}) collective-permute-start(f32[8,64,896]{2,1,0:T(8,128)} %get-tuple-element.37), channel_id=1, source_target_pairs={{0,16},{1,17},{2,18},{3,19},{4,20},{5,21},{6,22},{7,23},{8,24},{9,... | collective-permute-start | bytes 5505032 | tf_op jit(solution)/shard_map/ppermute | solution.py:29
  63.9 10.3 %collective-permute-start.13 = (f16[128,896]{1,0:T(8,128)(2,1)S(1)}, f16[128,896]{1,0:T(8,128)(2,1)S(1)}, u32[]{:S(2)}, u32[]{:S(2)}) collective-permute-start(f16[128,896]{1,0:T(8,128)(2,1)S(1)} %get-tuple-element.51), channel_id=1, source_target_pairs={{0,64},{1,65},{2,66},{3,67},{4,68},{5,69},{6,70},{7,71},{8,72},{9,... | collective-permute-start | bytes 688136 | tf_op jit(solution)/shard_map/ppermute | solution.py:29
  67.8 10.8 %collective-permute-start.14 = (f16[128,896]{1,0:T(8,128)(2,1)S(1)}, f16[128,896]{1,0:T(8,128)(2,1)S(1)}, u32[]{:S(2)}, u32[]{:S(2)}) collective-permute-start(f16[128,896]{1,0:T(8,128)(2,1)S(1)} %get-tuple-element.53), channel_id=1, source_target_pairs={{0,32},{1,33},{2,34},{3,35},{4,36},{5,37},{6,38},{7,39},{8,40},{9,... | collective-permute-start | bytes 688136 | tf_op jit(solution)/shard_map/ppermute | solution.py:29
  68.8 10.7 %collective-permute-start.15 = (f16[128,896]{1,0:T(8,128)(2,1)S(1)}, f16[128,896]{1,0:T(8,128)(2,1)}, u32[]{:S(2)}, u32[]{:S(2)}) collective-permute-start(f16[128,896]{1,0:T(8,128)(2,1)S(1)} %get-tuple-element.52), channel_id=1, source_target_pairs={{0,96},{1,97},{2,98},{3,99},{4,100},{5,101},{6,102},{7,103},{8,104... | collective-permute-start | bytes 688136 | tf_op jit(solution)/shard_map/ppermute | solution.py:29
  94.7 34.6 %copy-start.4 = (bf16[768,2304]{1,0:T(8,128)(2,1)S(1)}, bf16[768,2304]{1,0:T(8,128)(2,1)}, u32[]{:S(2)}) copy-start(bf16[768,2304]{1,0:T(8,128)(2,1)} %w_out.3) | copy-start | bytes 10616836
  115.4 9.0 %collective-permute-start.16 = (bf16[16,8,768]{2,1,0:T(8,128)(2,1)S(1)}, bf16[16,8,768]{2,1,0:T(8,128)(2,1)S(1)}, u32[]{:S(2)}, u32[]{:S(2)}) collective-permute-start(bf16[16,8,768]{2,1,0:T(8,128)(2,1)S(1)} %all_to_all.11.refs_0_), channel_id=1, source_target_pairs={{0,96},{1,97},{2,98},{3,99},{4,100},{5,101},{6,102},{7,103},{8,104... | collective-permute-start | bytes 589832 | tf_op jit(solution)/shard_map/ppermute | solution.py:29
  118.0 8.1 %collective-permute-start.17 = (bf16[16,8,768]{2,1,0:T(8,128)(2,1)S(1)}, bf16[16,8,768]{2,1,0:T(8,128)(2,1)S(1)}, u32[]{:S(2)}, u32[]{:S(2)}) collective-permute-start(bf16[16,8,768]{2,1,0:T(8,128)(2,1)S(1)} %all_to_all.11.refs_0_), channel_id=1, source_target_pairs={{0,64},{1,65},{2,66},{3,67},{4,68},{5,69},{6,70},{7,71},{8,72},{9,... | collective-permute-start | bytes 589832 | tf_op jit(solution)/shard_map/ppermute | solution.py:29
  118.4 9.4 %collective-permute-start.18 = (bf16[16,8,768]{2,1,0:T(8,128)(2,1)S(1)}, bf16[16,8,768]{2,1,0:T(8,128)(2,1)S(1)}, u32[]{:S(2)}, u32[]{:S(2)}) collective-permute-start(bf16[16,8,768]{2,1,0:T(8,128)(2,1)S(1)} %all_to_all.11.refs_0_), channel_id=1, source_target_pairs={{0,32},{1,33},{2,34},{3,35},{4,36},{5,37},{6,38},{7,39},{8,40},{9,... | collective-permute-start | bytes 589832 | tf_op jit(solution)/shard_map/ppermute | solution.py:29
  118.9 8.9 %collective-permute-start.19 = (bf16[16,8,768]{2,1,0:T(8,128)(2,1)S(1)}, bf16[16,8,768]{2,1,0:T(8,128)(2,1)S(1)}, u32[]{:S(2)}, u32[]{:S(2)}) collective-permute-start(bf16[16,8,768]{2,1,0:T(8,128)(2,1)S(1)} %all_to_all.11.refs_0_), channel_id=1, source_target_pairs={{0,16},{1,17},{2,18},{3,19},{4,20},{5,21},{6,22},{7,23},{8,24},{9,... | collective-permute-start | bytes 589832 | tf_op jit(solution)/shard_map/ppermute | solution.py:29
  124.4 3.4 %collective-permute-start.20 = (bf16[16,8,768]{2,1,0:T(8,128)(2,1)S(1)}, bf16[16,8,768]{2,1,0:T(8,128)(2,1)S(1)}, u32[]{:S(2)}, u32[]{:S(2)}) collective-permute-start(bf16[16,8,768]{2,1,0:T(8,128)(2,1)S(1)} %collective-permute-done.16.refs_1_), channel_id=1, source_target_pairs={{0,16},{1,17},{2,18},{3,19},{4,20},{5,21},{6,22},{7,23},{8,24},{9,... | collective-permute-start | bytes 589832 | tf_op jit(solution)/shard_map/ppermute | solution.py:29
  126.1 1.7 collective-permute-start.21
  127.8 1.4 collective-permute-start.22
  131.4 10.0 %collective-permute-start.23 = (bf16[128,2304]{1,0:T(8,128)(2,1)S(1)}, bf16[128,2304]{1,0:T(8,128)(2,1)S(1)}, u32[]{:S(2)}, u32[]{:S(2)}) collective-permute-start(bf16[128,2304]{1,0:T(8,128)(2,1)S(1)} %get-tuple-element.40), channel_id=1, source_target_pairs={{0,4},{1,5},{2,6},{3,7},{4,8},{5,9},{6,10},{7,11},{8,12},{9,13},{1... | collective-permute-start | bytes 1769480 | tf_op jit(solution)/shard_map/ppermute | solution.py:29
  133.9 11.1 %collective-permute-start.24 = (bf16[128,2304]{1,0:T(8,128)(2,1)S(1)}, bf16[128,2304]{1,0:T(8,128)(2,1)S(1)}, u32[]{:S(2)}, u32[]{:S(2)}) collective-permute-start(bf16[128,2304]{1,0:T(8,128)(2,1)S(1)} %get-tuple-element.42), channel_id=1, source_target_pairs={{0,12},{1,13},{2,14},{3,15},{4,0},{5,1},{6,2},{7,3},{8,4},{9,5},{1... | collective-permute-start | bytes 1769480 | tf_op jit(solution)/shard_map/ppermute | solution.py:29
  136.5 12.6 %collective-permute-start.26 = (bf16[128,2304]{1,0:T(8,128)(2,1)S(1)}, bf16[128,2304]{1,0:T(8,128)(2,1)S(1)}, u32[]{:S(2)}, u32[]{:S(2)}) collective-permute-start(bf16[128,2304]{1,0:T(8,128)(2,1)S(1)} %get-tuple-element.44), channel_id=1, source_target_pairs={{0,4},{1,5},{2,6},{3,7},{4,8},{5,9},{6,10},{7,11},{8,12},{9,13},{1... | collective-permute-start | bytes 1769480 | tf_op jit(solution)/shard_map/ppermute | solution.py:29
  139.8 11.6 %collective-permute-start.27 = (bf16[128,2304]{1,0:T(8,128)(2,1)S(1)}, bf16[128,2304]{1,0:T(8,128)(2,1)S(1)}, u32[]{:S(2)}, u32[]{:S(2)}) collective-permute-start(bf16[128,2304]{1,0:T(8,128)(2,1)S(1)} %get-tuple-element.45), channel_id=1, source_target_pairs={{0,12},{1,13},{2,14},{3,15},{4,0},{5,1},{6,2},{7,3},{8,4},{9,5},{1... | collective-permute-start | bytes 1769480 | tf_op jit(solution)/shard_map/ppermute | solution.py:29
  145.3 10.0 %collective-permute-start.25 = (bf16[128,2304]{1,0:T(8,128)(2,1)S(1)}, bf16[128,2304]{1,0:T(8,128)(2,1)S(1)}, u32[]{:S(2)}, u32[]{:S(2)}) collective-permute-start(bf16[128,2304]{1,0:T(8,128)(2,1)S(1)} %get-tuple-element.43), channel_id=1, source_target_pairs={{0,4},{1,5},{2,6},{3,7},{4,8},{5,9},{6,10},{7,11},{8,12},{9,13},{1... | collective-permute-start | bytes 1769480 | tf_op jit(solution)/shard_map/ppermute | solution.py:29
  145.4 12.3 %collective-permute-start.28 = (bf16[128,2304]{1,0:T(8,128)(2,1)S(1)}, bf16[128,2304]{1,0:T(8,128)(2,1)S(1)}, u32[]{:S(2)}, u32[]{:S(2)}) collective-permute-start(bf16[128,2304]{1,0:T(8,128)(2,1)S(1)} %get-tuple-element.46), channel_id=1, source_target_pairs={{0,12},{1,13},{2,14},{3,15},{4,0},{5,1},{6,2},{7,3},{8,4},{9,5},{1... | collective-permute-start | bytes 1769480 | tf_op jit(solution)/shard_map/ppermute | solution.py:29
  159.2 11.2 %collective-permute-start.29 = (bf16[64,2304]{1,0:T(8,128)(2,1)S(1)}, bf16[64,2304]{1,0:T(8,128)(2,1)S(1)}, u32[]{:S(2)}, u32[]{:S(2)}) collective-permute-start(bf16[64,2304]{1,0:T(8,128)(2,1)S(1)} %get-tuple-element.48), channel_id=1, source_target_pairs={{0,1},{1,2},{2,3},{3,0},{4,5},{5,6},{6,7},{7,4},{8,9},{9,10},{10,1... | collective-permute-start | bytes 884744 | tf_op jit(solution)/shard_map/ppermute | solution.py:29
  159.8 10.5 %collective-permute-start.30 = (bf16[64,2304]{1,0:T(8,128)(2,1)S(1)}, bf16[64,2304]{1,0:T(8,128)(2,1)S(1)}, u32[]{:S(2)}, u32[]{:S(2)}) collective-permute-start(bf16[64,2304]{1,0:T(8,128)(2,1)S(1)} %get-tuple-element.49), channel_id=1, source_target_pairs={{0,2},{1,3},{2,0},{3,1},{4,6},{5,7},{6,4},{7,5},{8,10},{9,11},{10,... | collective-permute-start | bytes 884744 | tf_op jit(solution)/shard_map/ppermute | solution.py:29
  161.5 9.8 %collective-permute-start.31 = (bf16[64,2304]{1,0:T(8,128)(2,1)S(1)}, bf16[64,2304]{1,0:T(8,128)(2,1)S(1)}, u32[]{:S(2)}, u32[]{:S(2)}) collective-permute-start(bf16[64,2304]{1,0:T(8,128)(2,1)S(1)} %get-tuple-element.50), channel_id=1, source_target_pairs={{0,3},{1,0},{2,1},{3,2},{4,7},{5,4},{6,5},{7,6},{8,11},{9,8},{10,9... | collective-permute-start | bytes 884744 | tf_op jit(solution)/shard_map/ppermute | solution.py:29

commit v3 on v2

--- a/solution.py
+++ b/solution.py
@@ -43,6 +43,11 @@
 
 def other_core(z, c, y, x):
     return (z, 1 - c, y, x)
+
+
+def exchange(value):
+    groups = [[(2 * z + c) * 16 + g for z in range(4) for g in range(16)] for c in range(2)]
+    return lax.all_to_all(value, ("gx", "gy"), 0, 0, axis_index_groups=groups)
 
 
 def whole(shape):
@@ -148,7 +153,9 @@
 def normalise_body(tok, tile, gain, out):
     cols = jnp.transpose(jnp.concatenate([tile[0], jnp.zeros((120, 128), F32)], axis=0))
     value = tok[...].astype(F32)
-    out[...] = ((value - cols[:64, 0:1]) * cols[:64, 1:2] * gain[...]).astype(BF)
+    value = ((value - cols[:64, 0:1]) * cols[:64, 1:2] * gain[...]).astype(BF)
+    order = one_hot(64, 64, lambda o: ((o >> 2) & 1) * 32 + (o >> 3) * 4 + (o & 3))
+    out[...] = jnp.dot(order, value, preferred_element_type=F32).astype(BF)
 
 
 def normalise(tok, tile, gain):
@@ -230,27 +237,6 @@
     )(place, *halves, wq, wkv, *held)
 
 
-def reorder_query_body(total, out):
-    order = one_hot(
-        128, 128, lambda i: (i & 64) + ((i >> 2) & 1) * 32 + ((i >> 3) & 7) * 4 + (i & 3)
-    )
-    moved = jnp.dot(order, total[...], preferred_element_type=F32)
-    out[...] = moved.reshape(16, 8, moved.shape[-1]).astype(BF)
-
-
-def reorder_query(total):
-    n = total.shape[-1]
-    return one_step(
-        reorder_query_body,
-        [IN_VMEM],
-        jax.ShapeDtypeStruct((16, 8, n), BF),
-        [],
-        2 * 128 * 128 * n,
-        128 * n * 4,
-        "reorder_query",
-    )(total)
-
-
 def attend_body(lens, x, keys_hbm, values_hbm, out, keys, values, sems):
     nq = out.shape[-1]
     rows, length, dim = keys.shape
@@ -277,9 +263,8 @@
     position = lax.broadcasted_iota(jnp.int32, (1, length), 1)
     placed = None
     for row in range(rows):
-        if row % 2 == 0:
-            for copy in copies[2 * row : 2 * row + 4]:
-                copy.wait()
+        for copy in copies[2 * row : 2 * row + 2]:
+            copy.wait()
         pick = one_hot(32, 128, lambda i: (i >> 1) * 8 + (i & 1) * 4 + row)
         mine = jnp.dot(pick, flat[:, :nq], preferred_element_type=F32).astype(BF)
         query = jnp.concatenate([mine[:, h * dim : (h + 1) * dim] for h in range(heads)], axis=0)
@@ -312,7 +297,9 @@
         back = jnp.where(sub == (lane >> 1) * 8 + (lane & 1) * 4 + row, 1.0, 0.0).astype(BF)
         term = jnp.dot(back, mixed, preferred_element_type=F32)
         placed = term if placed is None else placed + term
-    out[...] = placed.reshape(16, 8, nq).astype(BF)
+    placed = placed.reshape(16, 8, nq).astype(BF)
+    for copy in range(4):
+        out[copy] = placed
 
 
 def attend(lens, x, keys, values, nq):
@@ -321,7 +308,7 @@
         attend_body,
         in_specs=[IN_SMEM, IN_VMEM, IN_HBM, IN_HBM],
         out_specs=IN_VMEM,
-        out_shape=jax.ShapeDtypeStruct((16, 8, nq), BF),
+        out_shape=jax.ShapeDtypeStruct((4, 16, 8, nq), BF),
         scratch_shapes=[
             pltpu.VMEM(keys.shape, BF),
             pltpu.VMEM(values.shape, BF),
@@ -335,20 +322,14 @@
     )(lens, x, keys, values)
 
 
-def output_far_body(place, *refs):
-    mixed, w_out = refs[:8], refs[8]
-    left, half_a, half_b = refs[9:]
-    z, c = place[2], place[3]
-    order = one_hot(
-        128, 128, lambda o: (o & 64) + ((o >> 2) & 7) * 8 + ((o >> 5) & 1) * 4 + (o & 3)
-    )
-    for k in range(8):
-        bz = (z + k % 4) & 3
-        bc = c if k < 4 else 1 - c
-        value = mixed[k][...].astype(F32).reshape(128, mixed[k].shape[-1]).astype(BF)
-        moved = jnp.dot(order, value, preferred_element_type=F32).astype(BF)
-        left[bz * 4 + bc * 2] = moved[:64]
-        left[bz * 4 + bc * 2 + 1] = moved[64:]
+def output_far_body(place, same, cross, w_out, left, half_a, half_b):
+    c = place[3]
+    depth = left.shape[-1]
+    for mixed, bc in ((same, c), (cross, 1 - c)):
+        for bz in range(4):
+            for half in range(2):
+                value = mixed[bz, half * 8 : half * 8 + 8].astype(F32)
+                left[bz * 4 + bc * 2 + half] = value.reshape(64, depth).astype(BF)
     partial_rows(place, 2, left, w_out, (half_a, half_b))
 
 
@@ -367,17 +348,17 @@
             at += out.shape[0]
 
 
-def output_far(place, mixed, w_out):
+def output_far(place, same, cross, w_out):
     depth, width = w_out.shape
     return one_step(
         output_far_body,
-        [IN_SMEM] + [IN_VMEM] * 9,
+        [IN_SMEM] + [IN_VMEM] * 3,
         [jax.ShapeDtypeStruct((16, 64, depth), BF)] + [jax.ShapeDtypeStruct((128, width), BF)] * 2,
         [],
         2 * 256 * depth * width,
         1024 * depth * 4 + depth * width * 2 + 256 * width * 2,
         "output_far",
-    )(place, *mixed, w_out)
+    )(place, same, cross, w_out)
 
 
 def output_near_body(place, left, w_out, plus_a, plus_b, minus_a, minus_b):
@@ -470,6 +451,8 @@
 
 def last_sum_body(place, own, r1, r2, r3, out):
     total = own[...] + r1[...].astype(F32) + r2[...].astype(F32) + r3[...].astype(F32)
+    order = one_hot(64, 64, lambda o: ((o >> 2) & 7) * 8 + (o >> 5) * 4 + (o & 3))
+    total = jnp.dot(order, total.astype(BF), preferred_element_type=F32)
     out[...] = total.reshape(out.shape).astype(BF)
 
 
@@ -502,6 +485,7 @@
     b1, b2, b3 = [send(tok, first_axis(d)) for d in (-1, 2, 1)]
     low = jnp.concatenate([tok, b1], axis=0)
     high = jnp.concatenate([b2, b3], axis=0)
+    low, high = after(low, high)
     minus_low = send(low, second_axis(1))
     plus_high = send(high, second_axis(-1))
     minus_high = send(high, second_axis(1))
@@ -532,29 +516,15 @@
         place, tokens.reshape(64, width), gain, w_query, wkv, width * 8
     )
     n = near.shape[-1]
-    far_got = send(far, other_core).reshape(4, 128, n)
-    near = near.reshape(4, 128, n)
-
-    def chip_sum(d):
-        at = (z + d) & 3
-        return lax.dynamic_index_in_dim(near, at, 0, False) + lax.dynamic_index_in_dim(
-            far_got, at, 0, False
-        )
-
-    got = [
-        send((chip_sum(d) * PARTIAL_SCALE).astype(jnp.float16), z_axis(d)) for d in (2, 1, 3)
-    ]
-    query = chip_sum(0)
-    for g in got:
-        query = query + g.astype(F32) * (1.0 / PARTIAL_SCALE)
-    query = reorder_query(query.astype(BF))
-    query = lax.all_to_all(query, "gy", 0, 0)
-    mixed = attend(lengths, query, cache_keys, cache_values, nq)
-    mixed = lax.all_to_all(mixed, "gy", 0, 0)
-    same = [mixed, send(mixed, z_axis(-1)), send(mixed, z_axis(2)), send(mixed, z_axis(1))]
-    cross = [send(m, other_core) for m in same]
-
-    left, far_a, far_b = output_far(place, same + cross, w_out)
+
+    partial = (near + send(far, other_core)) * PARTIAL_SCALE
+    partial = exchange(partial.astype(jnp.float16).reshape(64, 8, n))
+    query = jnp.sum(partial.astype(F32).reshape(4, 16, 8, n), axis=0) * (1.0 / PARTIAL_SCALE)
+    mixed = attend(lengths, query.astype(BF), cache_keys, cache_values, nq)
+    mixed = exchange(mixed.reshape(64, 8, nq)).reshape(4, 16, 8, nq)
+    cross = send(mixed, other_core)
+
+    left, far_a, far_b = output_far(place, mixed, cross, w_out)
     got_a = send(far_a, second_axis(1))
     got_b = send(far_b, second_axis(-1))
     plus_a, plus_b, minus_a, minus_b = output_near(place, left, w_out)

time: 173 us -> 160 us (0.925)
  waiting for transfers between devices: 63.9 us -> 44.3 us
  blocking collectives: 25.2 us -> 43.6 us
  starting transfers between devices: 40.3 us -> 31.9 us
  other arithmetic: 3.45 us -> 1.3 us
    ppermute x32 -> x23, waiting for transfers between devices: 63.9 us -> 44.3 us  [send(): return lax.ppermute(value, ('gx', 'gy'), flat_perm(place))]
    all_to_all x2, blocking collectives: 25.2 us -> 43.6 us  [exchange(): return lax.all_to_all(value, ('gx', 'gy'), 0, 0, axis_index_groups=groups)]
    ppermute x32 -> x23, starting transfers between devices: 40.3 us -> 31.9 us  [send(): return lax.ppermute(value, ('gx', 'gy'), flat_perm(place))]
    convert_element_type x2, other arithmetic: 3.34 us -> 1.03 us  [the longest x1 0.72 us: per_device(): mixed = attend(lengths, query.astype(BF), cache_keys, cache_values, nq)]
    unnamed x15 -> x12, local copies, waits for them, and re-layouts: 5.34 us -> 4.08 us
  transfers between devices with their start and end apart: 32 -> 23, of which waited for: 23 -> 15; matrix products, arithmetic and copies ran while one was open for 1% -> 1% of each run, Pallas kernels for 9% -> 9%
where the time goes in v3:
time: 160 us; the launch traced here: 159 us
  waiting for transfers between devices  44.3 us (28%)
  blocking collectives  43.6 us (27%)
  Pallas kernels  32.8 us (20%)
  starting transfers between devices  31.9 us (20%)
  local copies, waits for them, and re-layouts  5.14 us (3%)
    ppermute x23, waiting for transfers between devices, send(): return lax.ppermute(value, ('gx', 'gy'), flat_perm(place))  44.3 us
    all_to_all x2, blocking collectives, exchange(): return lax.all_to_all(value, ('gx', 'gy'), 0, 0, axis_index_groups=groups)  43.6 us
    ppermute x23, starting transfers between devices, send(): return lax.ppermute(value, ('gx', 'gy'), flat_perm(place))  31.9 us
    pallas_call x3, Pallas kernels, project(): pl.pallas_call(functools.partial(project_body, places), in_specs=[IN_SMEM...  14 us
    pallas_call x1, Pallas kernels, attend(): pl.pallas_call(attend_body, in_specs=[IN_SMEM, IN_VMEM, IN_HBM, IN_HBM],...  8.87 us
    unnamed x12, local copies, waits for them, and re-layouts  4.08 us
  transfers between devices with their start and end apart: 23, of which 15 were waited for; matrix products, arithmetic and copies ran while one was open for 1% of the time, Pallas kernels for 9%

profile of v3, /device:TPU:24, one launch (start us, length us, event | category | flops | bytes accessed | tf_op | source)
XLA Modules:
  0.0 159.2 jit_solution(1918635247901309580)
XLA Ops:
  0.0 1.1 copy-done.4
  1.1 0.3 row_statistics.1.refs_0_
  1.4 0.0 collective-permute-start
  1.4 1.2 collective-permute-done.refs_1_
  2.6 1.9 %collective-permute-start.1 = (f32[1,8,128]{2,1,0:T(8,128)S(1)}, f32[1,8,128]{2,1,0:T(8,128)S(1)}, u32[]{:S(2)}, u32[]{:S(2)}) collective-permute-start(f32[1,8,128]{2,1,0:T(8,128)S(1)} %combine.3.refs_0_), channel_id=1, source_target_pairs={{0,32},{1,33},{2,34},{3,35},{4,36},{5,37},{6,38},{7,39},{8,40},{9,... | collective-permute-start | bytes 12296 | tf_op jit(solution)/shard_map/ppermute | solution.py:29
  4.5 1.7 %collective-permute-done.1.refs_1_ = f32[1,8,128]{2,1,0:T(8,128)S(1)} collective-permute-done((f32[1,8,128]{2,1,0:T(8,128)S(1)}, f32[1,8,128]{2,1,0:T(8,128)S(1)}, u32[]{:S(2)}, u32[]{:S(2)}) %collective-permute-start.1) | collective-permute-done | bytes 4128 | tf_op jit(solution)/shard_map/ppermute | solution.py:29
  6.2 3.9 %collective-permute-start.2 = (f32[1,8,128]{2,1,0:T(8,128)S(1)}, f32[1,8,128]{2,1,0:T(8,128)S(1)}, u32[]{:S(2)}, u32[]{:S(2)}) collective-permute-start(f32[1,8,128]{2,1,0:T(8,128)S(1)} %combine.4.refs_0_), channel_id=1, source_target_pairs={{0,64},{1,65},{2,66},{3,67},{4,68},{5,69},{6,70},{7,71},{8,72},{9,... | collective-permute-start | bytes 12296 | tf_op jit(solution)/shard_map/ppermute | solution.py:29
  10.1 0.7 broadcast_in_dim.3.gain
  10.8 0.9 collective-permute-done.2.refs_1_
  11.7 1.0 copy-done.5
  12.7 0.4 normalise.1
  13.1 2.8 %collective-permute-start.3 = (bf16[64,2304]{1,0:T(8,128)(2,1)S(1)}, bf16[64,2304]{1,0:T(8,128)(2,1)S(1)}, u32[]{:S(2)}, u32[]{:S(2)}) collective-permute-start(bf16[64,2304]{1,0:T(8,128)(2,1)S(1)} %normalise.1), channel_id=1, source_target_pairs={{0,3},{1,0},{2,1},{3,2},{4,7},{5,4},{6,5},{7,6},{8,11},{9,8},{10,9... | collective-permute-start | bytes 884744 | tf_op jit(solution)/shard_map/ppermute | solution.py:29
  15.9 0.0 collective-permute-start.5
  15.9 2.3 %collective-permute-start.4 = (bf16[64,2304]{1,0:T(8,128)(2,1)S(1)}, bf16[64,2304]{1,0:T(8,128)(2,1)S(1)}, u32[]{:S(2)}, u32[]{:S(2)}) collective-permute-start(bf16[64,2304]{1,0:T(8,128)(2,1)S(1)} %normalise.1), channel_id=1, source_target_pairs={{0,2},{1,3},{2,0},{3,1},{4,6},{5,7},{6,4},{7,5},{8,10},{9,11},{10,... | collective-permute-start | bytes 884744 | tf_op jit(solution)/shard_map/ppermute | solution.py:29
  18.2 2.0 %collective-permute-done.3 = bf16[64,2304]{1,0:T(8,128)(2,1)S(1)} collective-permute-done((bf16[64,2304]{1,0:T(8,128)(2,1)S(1)}, bf16[64,2304]{1,0:T(8,128)(2,1)S(1)}, u32[]{:S(2)}, u32[]{:S(2)}) %collective-permute-start.3) | collective-permute-done | bytes 294944 | tf_op jit(solution)/shard_map/ppermute | solution.py:29
  20.2 7.6 %collective-permute-done.5 = bf16[64,2304]{1,0:T(8,128)(2,1)S(1)} collective-permute-done((bf16[64,2304]{1,0:T(8,128)(2,1)S(1)}, bf16[64,2304]{1,0:T(8,128)(2,1)S(1)}, u32[]{:S(2)}, u32[]{:S(2)}) %collective-permute-start.5) | collective-permute-done | bytes 294944 | tf_op jit(solution)/shard_map/ppermute | solution.py:29
  27.8 0.1 collective-permute-start.6
  27.9 2.0 %collective-permute-start.8 = (bf16[128,2304]{1,0:T(8,128)(2,1)S(1)}, bf16[128,2304]{1,0:T(8,128)(2,1)}, u32[]{:S(2)}, u32[]{:S(2)}) collective-permute-start(bf16[128,2304]{1,0:T(8,128)(2,1)S(1)} %pad_maximum_fusion.1.refs_1_), channel_id=1, source_target_pairs={{0,12},{1,13},{2,14},{3,15},{4,0},{5,1},{6,2},{7,3},{8,4},{9,5},{1... | collective-permute-start | bytes 1769480 | tf_op jit(solution)/shard_map/ppermute | solution.py:29
  29.9 0.2 constant_dynamic-slice_fusion
  30.1 0.1 pad.4.refs_3_.refs_5_
  30.3 0.8 collective-permute-start.10
  31.1 2.5 %collective-permute-start.11 = (bf16[128,2304]{1,0:T(8,128)(2,1)S(1)}, bf16[128,2304]{1,0:T(8,128)(2,1)S(1)}, u32[]{:S(2)}, u32[]{:S(2)}) collective-permute-start(bf16[128,2304]{1,0:T(8,128)(2,1)S(1)} %pad_maximum_fusion.1.refs_1_), channel_id=1, source_target_pairs={{0,4},{1,5},{2,6},{3,7},{4,8},{5,9},{6,10},{7,11},{8,12},{9,13},{1... | collective-permute-start | bytes 1769480 | tf_op jit(solution)/shard_map/ppermute | solution.py:29
  33.6 0.1 pad_add_fusion.place
  33.7 2.0 %copy-done.1 = bf16[2304,768]{1,0:T(8,128)(2,1)S(1)} copy-done((bf16[2304,768]{1,0:T(8,128)(2,1)S(1)}, bf16[2304,768]{1,0:T(8,128)(2,1)}, u32[]{:S(2)}) %copy-start.1) | copy-done | bytes 3538968
  35.7 3.5 %project.3 = (f32[8,64,896]{2,1,0:T(8,128)S(1)}, f32[8,64,896]{2,1,0:T(8,128)S(1)}) custom-call(s32[4]{0:T(128)S(1)} %pad_add_fusion.place, bf16[128,2304]{1,0:T(8,128)(2,1)S(1)} %pad_maximum_fusion.refs_0_, bf16[128,2304]{1,0:T(8,128)(2,1)S(1)} %pad_maximum_fusion.1.refs_1_, bf16[2304,768]{1,0:T(8,128)(2,1)S(1)} %copy-done.1, ...), custom_call_target="tpu_custom_call" | custom-call | flops 1056964608 | bytes 6225920 | tf_op jit(solution)/shard_map/project/pallas_call | solution.py:218
  39.1 0.0 collective-permute-done.6.refs_2_
  39.1 0.0 collective-permute-done.8.refs_1_
  39.2 0.7 collective-permute-start.9
  39.9 2.6 %collective-permute-start.7 = (bf16[128,2304]{1,0:T(8,128)(2,1)}, bf16[128,2304]{1,0:T(8,128)(2,1)S(1)}, u32[]{:S(2)}, u32[]{:S(2)}) collective-permute-start(bf16[128,2304]{1,0:T(8,128)(2,1)} %collective-permute-done.6.refs_2_), channel_id=1, source_target_pairs={{0,4},{1,5},{2,6},{3,7},{4,8},{5,9},{6,10},{7,11},{8,12},{9,13},{1... | collective-permute-start | bytes 1769480 | tf_op jit(solution)/shard_map/ppermute | solution.py:29
  42.5 2.9 %collective-permute-done.10.refs_0_ = bf16[128,2304]{1,0:T(8,128)(2,1)S(1)} collective-permute-done((bf16[128,2304]{1,0:T(8,128)(2,1)S(1)}, bf16[128,2304]{1,0:T(8,128)(2,1)S(1)}, u32[]{:S(2)}, u32[]{:S(2)}) %collective-permute-start.10) | collective-permute-done | bytes 589856 | tf_op jit(solution)/shard_map/ppermute | solution.py:29
  45.4 0.0 collective-permute-done.11.refs_3_
  45.4 7.1 %project.4 = (f32[8,64,896]{2,1,0:T(8,128)S(1)}, f32[8,64,896]{2,1,0:T(8,128)S(1)}) custom-call(s32[4]{0:T(128)S(1)} %pad_add_fusion.place, bf16[128,2304]{1,0:T(8,128)(2,1)S(1)} %collective-permute-done.10.refs_0_, bf16[128,2304]{1,0:T(8,128)(2,1)} %collective-permute-done.8.refs_1_, ...), custom_call_target="tpu_custom_call", output_to_operand_aliasing={{0}: (7, {}), {1}: (8, {})} | custom-call | flops 2113929216 | bytes 8323072 | tf_op jit(solution)/shard_map/project/pallas_call | solution.py:218
  52.5 0.0 collective-permute-done.7.refs_0_
  52.5 3.5 %project.5 = (f32[8,64,896]{2,1,0:T(8,128)S(1)}, f32[8,64,896]{2,1,0:T(8,128)S(1)}) custom-call(s32[4]{0:T(128)S(1)} %pad_add_fusion.place, bf16[128,2304]{1,0:T(8,128)(2,1)S(1)} %collective-permute-done.7.refs_0_, bf16[128,2304]{1,0:T(8,128)(2,1)S(1)} %collective-permute-done.9.refs_1_, ...), custom_call_target="tpu_custom_call", output_to_operand_aliasing={{0}: (5, {}), {1}: (6, {})} | custom-call | flops 1056964608 | bytes 6225920 | tf_op jit(solution)/shard_map/project/pallas_call | solution.py:218
  56.0 0.1 collective-permute-start.12
  56.1 3.8 %collective-permute-done.12 = f32[8,64,896]{2,1,0:T(8,128)S(1)} collective-permute-done((f32[8,64,896]{2,1,0:T(8,128)S(1)}, f32[8,64,896]{2,1,0:T(8,128)S(1)}, u32[]{:S(2)}, u32[]{:S(2)}) %collective-permute-start.12) | collective-permute-done | bytes 1835040 | tf_op jit(solution)/shard_map/ppermute | solution.py:29
  59.8 0.3 multiply_convert_fusion
  60.2 23.6 %all_to_all.10 = f16[64,8,896]{2,1,0:T(8,128)(2,1)S(1)} all-to-all(f16[64,8,896]{2,1,0:T(8,128)(2,1)S(1)} %bitcast.15), channel_id=1, replica_groups={{0,1,2,3,4,5,6,7,8,9,10,11,12,13,14,15,32,33,34,35,36,37,38,39,40,41,42..., dimensions={0} | all-to-all | bytes 1835008 | tf_op jit(solution)/shard_map/all_to_all | solution.py:50
  83.8 0.1 convert_reduce_fusion
  83.9 0.7 multiply_convert_fusion.1.x
  84.6 8.9 %attend.1 = bf16[4,16,8,768]{3,2,1,0:T(8,128)(2,1)} custom-call(s32[4]{0:T(128)} %lens.1, bf16[16,8,896]{2,1,0:T(8,128)(2,1)} %multiply_convert_fusion.1.x, bf16[4,2048,256]{2,1,0:T(8,128)(2,1)} %keys_hbm.1, bf16[4,2048,256]{2,1,0:T(8,128)(2,1)} %values_hbm.1), custom_call_target="tpu_custom_call" | custom-call | flops 805306368 | bytes 8388608 | tf_op jit(solution)/shard_map/attend/pallas_call | solution.py:307
  93.5 20.0 %all_to_all.11 = bf16[64,8,768]{2,1,0:T(8,128)(2,1)S(1)} all-to-all(bf16[64,8,768]{2,1,0:T(8,128)(2,1)} %bitcast.16), channel_id=1, replica_groups={{0,1,2,3,4,5,6,7,8,9,10,11,12,13,14,15,32,33,34,35,36,37,38,39,40,41,42..., dimensions={0} | all-to-all | bytes 1572864 | tf_op jit(solution)/shard_map/all_to_all | solution.py:50
  113.5 0.0 collective-permute-start.13
  113.5 2.3 %collective-permute-done.13.cross = bf16[4,16,8,768]{3,2,1,0:T(8,128)(2,1)S(1)} collective-permute-done((bf16[4,16,8,768]{3,2,1,0:T(8,128)(2,1)S(1)}, bf16[4,16,8,768]{3,2,1,0:T(8,128)(2,1)S(1)}, u32[]{:S(2)}, u32[]{:S(2)}) %collective-permute-start.13) | collective-permute-done | bytes 786464 | tf_op jit(solution)/shard_map/ppermute | solution.py:29
  115.8 1.7 %output_far.1 = (bf16[16,64,768]{2,1,0:T(8,128)(2,1)S(1)}, bf16[128,2304]{1,0:T(8,128)(2,1)S(1)}, bf16[128,2304]{1,0:T(8,128)(2,1)S(1)}) custom-call(s32[4]{0:T(128)S(1)} %pad_add_fusion.place, bf16[4,16,8,768]{3,2,1,0:T(8,128)(2,1)S(1)} %bitcast.11, bf16[4,16,8,768]{3,2,1,0:T(8,128)(2,1)S(1)} %collective-permute-done.13.cross, bf16[768,2304]{1,0:T(8,128)(2,1)S(1)} %copy-done.3), custom_call_target="tpu_custom_call" | custom-call | flops 905969664 | bytes 7864320 | tf_op jit(solution)/shard_map/output_far/pallas_call | solution.py:353
  117.5 2.9 %collective-permute-start.14 = (bf16[128,2304]{1,0:T(8,128)(2,1)S(1)}, bf16[128,2304]{1,0:T(8,128)(2,1)S(1)}, u32[]{:S(2)}, u32[]{:S(2)}) collective-permute-start(bf16[128,2304]{1,0:T(8,128)(2,1)S(1)} %get-tuple-element.44), channel_id=1, source_target_pairs={{0,4},{1,5},{2,6},{3,7},{4,8},{5,9},{6,10},{7,11},{8,12},{9,13},{1... | collective-permute-start | bytes 1769480 | tf_op jit(solution)/shard_map/ppermute | solution.py:29
  120.4 2.6 %output_near.1 = (bf16[128,2304]{1,0:T(8,128)(2,1)S(1)}, bf16[128,2304]{1,0:T(8,128)(2,1)S(1)}, bf16[128,2304]{1,0:T(8,128)(2,1)S(1)}, bf16[128,2304]{1,0:T(8,128)(2,1)S(1)}) custom-call(s32[4]{0:T(128)S(1)} %pad_add_fusion.place, bf16[16,64,768]{2,1,0:T(8,128)(2,1)S(1)} %get-tuple-element.42.left, bf16[768,2304]{1,0:T(8,128)(2,1)S(1)} %copy-done.3), custom_call_target="tpu_custom_call" | custom-call | flops 1811939328 | bytes 7471104 | tf_op jit(solution)/shard_map/output_near/pallas_call | solution.py:371
  122.9 3.3 %collective-permute-start.17 = (bf16[128,2304]{1,0:T(8,128)(2,1)S(1)}, bf16[128,2304]{1,0:T(8,128)(2,1)S(1)}, u32[]{:S(2)}, u32[]{:S(2)}) collective-permute-start(bf16[128,2304]{1,0:T(8,128)(2,1)S(1)} %get-tuple-element.48), channel_id=1, source_target_pairs={{0,4},{1,5},{2,6},{3,7},{4,8},{5,9},{6,10},{7,11},{8,12},{9,13},{1... | collective-permute-start | bytes 1769480 | tf_op jit(solution)/shard_map/ppermute | solution.py:29
  126.2 1.5 collective-permute-done.14.a1
  127.8 3.7 %collective-permute-done.15.b1 = bf16[128,2304]{1,0:T(8,128)(2,1)S(1)} collective-permute-done((bf16[128,2304]{1,0:T(8,128)(2,1)S(1)}, bf16[128,2304]{1,0:T(8,128)(2,1)S(1)}, u32[]{:S(2)}, u32[]{:S(2)}) %collective-permute-start.15) | collective-permute-done | bytes 589856 | tf_op jit(solution)/shard_map/ppermute | solution.py:29
  131.5 0.3 pair_add.1
  131.7 0.1 collective-permute-start.16
  131.8 2.0 %collective-permute-start.19 = (bf16[128,2304]{1,0:T(8,128)(2,1)S(1)}, bf16[128,2304]{1,0:T(8,128)(2,1)S(1)}, u32[]{:S(2)}, u32[]{:S(2)}) collective-permute-start(bf16[128,2304]{1,0:T(8,128)(2,1)S(1)} %get-tuple-element.50), channel_id=1, source_target_pairs={{0,12},{1,13},{2,14},{3,15},{4,0},{5,1},{6,2},{7,3},{8,4},{9,5},{1... | collective-permute-start | bytes 1769480 | tf_op jit(solution)/shard_map/ppermute | solution.py:29
  133.8 1.6 %output_own.1.a = bf16[256,2304]{1,0:T(8,128)(2,1)S(1)} custom-call(s32[4]{0:T(128)S(1)} %pad_add_fusion.place, bf16[16,64,768]{2,1,0:T(8,128)(2,1)S(1)} %get-tuple-element.42.left, bf16[768,2304]{1,0:T(8,128)(2,1)S(1)} %copy-done.3), custom_call_target="tpu_custom_call" | custom-call | flops 905969664 | bytes 6291456 | tf_op jit(solution)/shard_map/output_own/pallas_call | solution.py:388
  135.5 2.3 %collective-permute-done.18.c0 = bf16[128,2304]{1,0:T(8,128)(2,1)S(1)} collective-permute-done((bf16[128,2304]{1,0:T(8,128)(2,1)S(1)}, bf16[128,2304]{1,0:T(8,128)(2,1)S(1)}, u32[]{:S(2)}, u32[]{:S(2)}) %collective-permute-start.18) | collective-permute-done | bytes 589856 | tf_op jit(solution)/shard_map/ppermute | solution.py:29
  137.8 3.9 %collective-permute-done.16.b0 = bf16[128,2304]{1,0:T(8,128)(2,1)S(1)} collective-permute-done((bf16[128,2304]{1,0:T(8,128)(2,1)S(1)}, bf16[128,2304]{1,0:T(8,128)(2,1)S(1)}, u32[]{:S(2)}, u32[]{:S(2)}) %collective-permute-start.16) | collective-permute-done | bytes 589856 | tf_op jit(solution)/shard_map/ppermute | solution.py:29
  141.7 2.4 %collective-permute-done.19.c1 = bf16[128,2304]{1,0:T(8,128)(2,1)S(1)} collective-permute-done((bf16[128,2304]{1,0:T(8,128)(2,1)S(1)}, bf16[128,2304]{1,0:T(8,128)(2,1)S(1)}, u32[]{:S(2)}, u32[]{:S(2)}) %collective-permute-start.19) | collective-permute-done | bytes 589856 | tf_op jit(solution)/shard_map/ppermute | solution.py:29
  144.1 1.5 group_sum.1
  145.6 0.6 collective-permute-start.20
  146.3 1.8 %collective-permute-start.21 = (bf16[64,2304]{1,0:T(8,128)(2,1)S(1)}, bf16[64,2304]{1,0:T(8,128)(2,1)S(1)}, u32[]{:S(2)}, u32[]{:S(2)}) collective-permute-start(bf16[64,2304]{1,0:T(8,128)(2,1)S(1)} %get-tuple-element.53), channel_id=1, source_target_pairs={{0,2},{1,3},{2,0},{3,1},{4,6},{5,7},{6,4},{7,5},{8,10},{9,11},{10,... | collective-permute-start | bytes 884744 | tf_op jit(solution)/shard_map/ppermute | solution.py:29
  148.0 1.5 collective-permute-start.22
  149.5 7.2 %collective-permute-done.20.r1 = bf16[64,2304]{1,0:T(8,128)(2,1)S(1)} collective-permute-done((bf16[64,2304]{1,0:T(8,128)(2,1)S(1)}, bf16[64,2304]{1,0:T(8,128)(2,1)S(1)}, u32[]{:S(2)}, u32[]{:S(2)}) %collective-permute-start.20) | collective-permute-done | bytes 294944 | tf_op jit(solution)/shard_map/ppermute | solution.py:29
  156.8 0.9 collective-permute-done.22.r3
  157.7 1.6 last_sum.1
  (20 shorter events, 0.1 us)
Async XLA Ops:
  0.0 29.9 %copy-start = (bf16[2304,512]{1,0:T(8,128)(2,1)S(1)}, bf16[2304,512]{1,0:T(8,128)(2,1)}, u32[]{:S(2)}) copy-start(bf16[2304,512]{1,0:T(8,128)(2,1)} %param.11) | copy-start | bytes 7077892
  0.0 1.1 copy-start.4
  1.4 1.2 collective-permute-start
  2.6 3.6 %collective-permute-start.1 = (f32[1,8,128]{2,1,0:T(8,128)S(1)}, f32[1,8,128]{2,1,0:T(8,128)S(1)}, u32[]{:S(2)}, u32[]{:S(2)}) collective-permute-start(f32[1,8,128]{2,1,0:T(8,128)S(1)} %combine.3.refs_0_), channel_id=1, source_target_pairs={{0,32},{1,33},{2,34},{3,35},{4,36},{5,37},{6,38},{7,39},{8,40},{9,... | collective-permute-start | bytes 12296 | tf_op jit(solution)/shard_map/ppermute | solution.py:29
  6.2 5.5 %collective-permute-start.2 = (f32[1,8,128]{2,1,0:T(8,128)S(1)}, f32[1,8,128]{2,1,0:T(8,128)S(1)}, u32[]{:S(2)}, u32[]{:S(2)}) collective-permute-start(f32[1,8,128]{2,1,0:T(8,128)S(1)} %combine.4.refs_0_), channel_id=1, source_target_pairs={{0,64},{1,65},{2,66},{3,67},{4,68},{5,69},{6,70},{7,71},{8,72},{9,... | collective-permute-start | bytes 12296 | tf_op jit(solution)/shard_map/ppermute | solution.py:29
  11.7 1.0 copy-start.5
  13.1 7.1 %collective-permute-start.3 = (bf16[64,2304]{1,0:T(8,128)(2,1)S(1)}, bf16[64,2304]{1,0:T(8,128)(2,1)S(1)}, u32[]{:S(2)}, u32[]{:S(2)}) collective-permute-start(bf16[64,2304]{1,0:T(8,128)(2,1)S(1)} %normalise.1), channel_id=1, source_target_pairs={{0,3},{1,0},{2,1},{3,2},{4,7},{5,4},{6,5},{7,6},{8,11},{9,8},{10,9... | collective-permute-start | bytes 884744 | tf_op jit(solution)/shard_map/ppermute | solution.py:29
  15.9 11.9 %collective-permute-start.5 = (bf16[64,2304]{1,0:T(8,128)(2,1)S(1)}, bf16[64,2304]{1,0:T(8,128)(2,1)S(1)}, u32[]{:S(2)}, u32[]{:S(2)}) collective-permute-start(bf16[64,2304]{1,0:T(8,128)(2,1)S(1)} %normalise.1), channel_id=1, source_target_pairs={{0,1},{1,2},{2,3},{3,0},{4,5},{5,6},{6,7},{7,4},{8,9},{9,10},{10,1... | collective-permute-start | bytes 884744 | tf_op jit(solution)/shard_map/ppermute | solution.py:29
  15.9 11.9 %collective-permute-start.4 = (bf16[64,2304]{1,0:T(8,128)(2,1)S(1)}, bf16[64,2304]{1,0:T(8,128)(2,1)S(1)}, u32[]{:S(2)}, u32[]{:S(2)}) collective-permute-start(bf16[64,2304]{1,0:T(8,128)(2,1)S(1)} %normalise.1), channel_id=1, source_target_pairs={{0,2},{1,3},{2,0},{3,1},{4,6},{5,7},{6,4},{7,5},{8,10},{9,11},{10,... | collective-permute-start | bytes 884744 | tf_op jit(solution)/shard_map/ppermute | solution.py:29
  27.8 11.3 %collective-permute-start.6 = (bf16[128,2304]{1,0:T(8,128)(2,1)S(1)}, bf16[128,2304]{1,0:T(8,128)(2,1)}, u32[]{:S(2)}, u32[]{:S(2)}) collective-permute-start(bf16[128,2304]{1,0:T(8,128)(2,1)S(1)} %pad_maximum_fusion.refs_0_), channel_id=1, source_target_pairs={{0,4},{1,5},{2,6},{3,7},{4,8},{5,9},{6,10},{7,11},{8,12},{9,13},{1... | collective-permute-start | bytes 1769480 | tf_op jit(solution)/shard_map/ppermute | solution.py:29
  27.9 11.3 %collective-permute-start.8 = (bf16[128,2304]{1,0:T(8,128)(2,1)S(1)}, bf16[128,2304]{1,0:T(8,128)(2,1)}, u32[]{:S(2)}, u32[]{:S(2)}) collective-permute-start(bf16[128,2304]{1,0:T(8,128)(2,1)S(1)} %pad_maximum_fusion.1.refs_1_), channel_id=1, source_target_pairs={{0,12},{1,13},{2,14},{3,15},{4,0},{5,1},{6,2},{7,3},{8,4},{9,5},{1... | collective-permute-start | bytes 1769480 | tf_op jit(solution)/shard_map/ppermute | solution.py:29
  30.3 15.1 %collective-permute-start.10 = (bf16[128,2304]{1,0:T(8,128)(2,1)S(1)}, bf16[128,2304]{1,0:T(8,128)(2,1)S(1)}, u32[]{:S(2)}, u32[]{:S(2)}) collective-permute-start(bf16[128,2304]{1,0:T(8,128)(2,1)S(1)} %pad_maximum_fusion.refs_0_), channel_id=1, source_target_pairs={{0,12},{1,13},{2,14},{3,15},{4,0},{5,1},{6,2},{7,3},{8,4},{9,5},{1... | collective-permute-start | bytes 1769480 | tf_op jit(solution)/shard_map/ppermute | solution.py:29
  31.1 14.3 %collective-permute-start.11 = (bf16[128,2304]{1,0:T(8,128)(2,1)S(1)}, bf16[128,2304]{1,0:T(8,128)(2,1)S(1)}, u32[]{:S(2)}, u32[]{:S(2)}) collective-permute-start(bf16[128,2304]{1,0:T(8,128)(2,1)S(1)} %pad_maximum_fusion.1.refs_1_), channel_id=1, source_target_pairs={{0,4},{1,5},{2,6},{3,7},{4,8},{5,9},{6,10},{7,11},{8,12},{9,13},{1... | collective-permute-start | bytes 1769480 | tf_op jit(solution)/shard_map/ppermute | solution.py:29
  33.7 2.0 %copy-start.1 = (bf16[2304,768]{1,0:T(8,128)(2,1)S(1)}, bf16[2304,768]{1,0:T(8,128)(2,1)}, u32[]{:S(2)}) copy-start(bf16[2304,768]{1,0:T(8,128)(2,1)} %refs_2_.3) | copy-start | bytes 10616836
  35.7 9.7 %copy-start.2 = (bf16[2304,768]{1,0:T(8,128)(2,1)S(1)}, bf16[2304,768]{1,0:T(8,128)(2,1)}, u32[]{:S(2)}) copy-start(bf16[2304,768]{1,0:T(8,128)(2,1)} %refs_2_.3) | copy-start | bytes 10616836
  39.2 13.3 %collective-permute-start.9 = (bf16[128,2304]{1,0:T(8,128)(2,1)}, bf16[128,2304]{1,0:T(8,128)(2,1)S(1)}, u32[]{:S(2)}, u32[]{:S(2)}) collective-permute-start(bf16[128,2304]{1,0:T(8,128)(2,1)} %collective-permute-done.8.refs_1_), channel_id=1, source_target_pairs={{0,12},{1,13},{2,14},{3,15},{4,0},{5,1},{6,2},{7,3},{8,4},{9,5},{1... | collective-permute-start | bytes 1769480 | tf_op jit(solution)/shard_map/ppermute | solution.py:29
  39.9 12.6 %collective-permute-start.7 = (bf16[128,2304]{1,0:T(8,128)(2,1)}, bf16[128,2304]{1,0:T(8,128)(2,1)S(1)}, u32[]{:S(2)}, u32[]{:S(2)}) collective-permute-start(bf16[128,2304]{1,0:T(8,128)(2,1)} %collective-permute-done.6.refs_2_), channel_id=1, source_target_pairs={{0,4},{1,5},{2,6},{3,7},{4,8},{5,9},{6,10},{7,11},{8,12},{9,13},{1... | collective-permute-start | bytes 1769480 | tf_op jit(solution)/shard_map/ppermute | solution.py:29
  56.0 3.9 %collective-permute-start.12 = (f32[8,64,896]{2,1,0:T(8,128)S(1)}, f32[8,64,896]{2,1,0:T(8,128)S(1)}, u32[]{:S(2)}, u32[]{:S(2)}) collective-permute-start(f32[8,64,896]{2,1,0:T(8,128)S(1)} %get-tuple-element.41), channel_id=1, source_target_pairs={{0,16},{1,17},{2,18},{3,19},{4,20},{5,21},{6,22},{7,23},{8,24},{9,... | collective-permute-start | bytes 5505032 | tf_op jit(solution)/shard_map/ppermute | solution.py:29
  84.6 31.2 %copy-start.3 = (bf16[768,2304]{1,0:T(8,128)(2,1)S(1)}, bf16[768,2304]{1,0:T(8,128)(2,1)}, u32[]{:S(2)}) copy-start(bf16[768,2304]{1,0:T(8,128)(2,1)} %w_out.5) | copy-start | bytes 10616836
  113.5 2.3 %collective-permute-start.13 = (bf16[4,16,8,768]{3,2,1,0:T(8,128)(2,1)S(1)}, bf16[4,16,8,768]{3,2,1,0:T(8,128)(2,1)S(1)}, u32[]{:S(2)}, u32[]{:S(2)}) collective-permute-start(bf16[4,16,8,768]{3,2,1,0:T(8,128)(2,1)S(1)} %bitcast.10), channel_id=1, source_target_pairs={{0,16},{1,17},{2,18},{3,19},{4,20},{5,21},{6,22},{7,23},{8,24},{9,... | collective-permute-start | bytes 2359304 | tf_op jit(solution)/shard_map/ppermute | solution.py:29
  117.5 10.3 %collective-permute-start.14 = (bf16[128,2304]{1,0:T(8,128)(2,1)S(1)}, bf16[128,2304]{1,0:T(8,128)(2,1)S(1)}, u32[]{:S(2)}, u32[]{:S(2)}) collective-permute-start(bf16[128,2304]{1,0:T(8,128)(2,1)S(1)} %get-tuple-element.44), channel_id=1, source_target_pairs={{0,4},{1,5},{2,6},{3,7},{4,8},{5,9},{6,10},{7,11},{8,12},{9,13},{1... | collective-permute-start | bytes 1769480 | tf_op jit(solution)/shard_map/ppermute | solution.py:29
  120.4 11.1 %collective-permute-start.15 = (bf16[128,2304]{1,0:T(8,128)(2,1)S(1)}, bf16[128,2304]{1,0:T(8,128)(2,1)S(1)}, u32[]{:S(2)}, u32[]{:S(2)}) collective-permute-start(bf16[128,2304]{1,0:T(8,128)(2,1)S(1)} %get-tuple-element.46), channel_id=1, source_target_pairs={{0,12},{1,13},{2,14},{3,15},{4,0},{5,1},{6,2},{7,3},{8,4},{9,5},{1... | collective-permute-start | bytes 1769480 | tf_op jit(solution)/shard_map/ppermute | solution.py:29
  122.9 12.5 %collective-permute-start.17 = (bf16[128,2304]{1,0:T(8,128)(2,1)S(1)}, bf16[128,2304]{1,0:T(8,128)(2,1)S(1)}, u32[]{:S(2)}, u32[]{:S(2)}) collective-permute-start(bf16[128,2304]{1,0:T(8,128)(2,1)S(1)} %get-tuple-element.48), channel_id=1, source_target_pairs={{0,4},{1,5},{2,6},{3,7},{4,8},{5,9},{6,10},{7,11},{8,12},{9,13},{1... | collective-permute-start | bytes 1769480 | tf_op jit(solution)/shard_map/ppermute | solution.py:29
  126.2 11.5 %collective-permute-start.18 = (bf16[128,2304]{1,0:T(8,128)(2,1)S(1)}, bf16[128,2304]{1,0:T(8,128)(2,1)S(1)}, u32[]{:S(2)}, u32[]{:S(2)}) collective-permute-start(bf16[128,2304]{1,0:T(8,128)(2,1)S(1)} %get-tuple-element.49), channel_id=1, source_target_pairs={{0,12},{1,13},{2,14},{3,15},{4,0},{5,1},{6,2},{7,3},{8,4},{9,5},{1... | collective-permute-start | bytes 1769480 | tf_op jit(solution)/shard_map/ppermute | solution.py:29
  131.7 10.0 %collective-permute-start.16 = (bf16[128,2304]{1,0:T(8,128)(2,1)S(1)}, bf16[128,2304]{1,0:T(8,128)(2,1)S(1)}, u32[]{:S(2)}, u32[]{:S(2)}) collective-permute-start(bf16[128,2304]{1,0:T(8,128)(2,1)S(1)} %get-tuple-element.47), channel_id=1, source_target_pairs={{0,4},{1,5},{2,6},{3,7},{4,8},{5,9},{6,10},{7,11},{8,12},{9,13},{1... | collective-permute-start | bytes 1769480 | tf_op jit(solution)/shard_map/ppermute | solution.py:29
  131.8 12.3 %collective-permute-start.19 = (bf16[128,2304]{1,0:T(8,128)(2,1)S(1)}, bf16[128,2304]{1,0:T(8,128)(2,1)S(1)}, u32[]{:S(2)}, u32[]{:S(2)}) collective-permute-start(bf16[128,2304]{1,0:T(8,128)(2,1)S(1)} %get-tuple-element.50), channel_id=1, source_target_pairs={{0,12},{1,13},{2,14},{3,15},{4,0},{5,1},{6,2},{7,3},{8,4},{9,5},{1... | collective-permute-start | bytes 1769480 | tf_op jit(solution)/shard_map/ppermute | solution.py:29
  145.6 11.2 %collective-permute-start.20 = (bf16[64,2304]{1,0:T(8,128)(2,1)S(1)}, bf16[64,2304]{1,0:T(8,128)(2,1)S(1)}, u32[]{:S(2)}, u32[]{:S(2)}) collective-permute-start(bf16[64,2304]{1,0:T(8,128)(2,1)S(1)} %get-tuple-element.52), channel_id=1, source_target_pairs={{0,1},{1,2},{2,3},{3,0},{4,5},{5,6},{6,7},{7,4},{8,9},{9,10},{10,1... | collective-permute-start | bytes 884744 | tf_op jit(solution)/shard_map/ppermute | solution.py:29
  146.3 10.5 %collective-permute-start.21 = (bf16[64,2304]{1,0:T(8,128)(2,1)S(1)}, bf16[64,2304]{1,0:T(8,128)(2,1)S(1)}, u32[]{:S(2)}, u32[]{:S(2)}) collective-permute-start(bf16[64,2304]{1,0:T(8,128)(2,1)S(1)} %get-tuple-element.53), channel_id=1, source_target_pairs={{0,2},{1,3},{2,0},{3,1},{4,6},{5,7},{6,4},{7,5},{8,10},{9,11},{10,... | collective-permute-start | bytes 884744 | tf_op jit(solution)/shard_map/ppermute | solution.py:29
  148.0 9.6 %collective-permute-start.22 = (bf16[64,2304]{1,0:T(8,128)(2,1)S(1)}, bf16[64,2304]{1,0:T(8,128)(2,1)S(1)}, u32[]{:S(2)}, u32[]{:S(2)}) collective-permute-start(bf16[64,2304]{1,0:T(8,128)(2,1)S(1)} %get-tuple-element.54), channel_id=1, source_target_pairs={{0,3},{1,0},{2,1},{3,2},{4,7},{5,4},{6,5},{7,6},{8,11},{9,8},{10,9... | collective-permute-start | bytes 884744 | tf_op jit(solution)/shard_map/ppermute | solution.py:29

commit v4 on v3

--- a/solution.py
+++ b/solution.py
@@ -111,14 +111,16 @@
     lane = lax.broadcasted_iota(jnp.int32, (rows, 128), 1)
     cols = jnp.where(lane == 0, mean, jnp.where(lane == 1, squares, 0.0))
     cols = jnp.concatenate([cols, jnp.zeros((128 - rows, 128), F32)], axis=0)
-    out[0] = jnp.transpose(cols)[:8]
+    tile = jnp.transpose(cols)[:8]
+    for k in range(8):
+        out[k] = tile
 
 
 def row_statistics(tok):
     return one_step(
         row_statistics_body,
         [IN_VMEM],
-        jax.ShapeDtypeStruct((1, 8, 128), F32),
+        jax.ShapeDtypeStruct((8, 8, 128), F32),
         [],
         6 * tok.size,
         tok.size * 2,
@@ -126,39 +128,20 @@
     )(tok)
 
 
-def combine(tiles, count, width_all):
-    def body(*refs):
-        held = [ref[...] for ref in refs[:-1]]
-        mean = sum(h[:, 0:1] for h in held) * (1.0 / len(held))
-        squares = sum(h[:, 1:2] for h in held)
-        spread = sum((h[:, 0:1] - mean) * (h[:, 0:1] - mean) for h in held)
-        squares = squares + spread * float(count)
-        if width_all:
-            squares = lax.rsqrt(squares * (1.0 / width_all) + 1e-05)
-        refs[-1][:, 0:1] = mean
-        refs[-1][:, 1:2] = squares
-
-    shape = tiles[0].shape
-    return one_step(
-        body,
-        [IN_VMEM] * len(tiles),
-        jax.ShapeDtypeStruct(shape, F32),
-        [],
-        1024 * 10,
-        tiles[0].size * 4 * (len(tiles) + 1),
-        "combine",
-    )(*tiles)
-
-
-def normalise_body(tok, tile, gain, out):
-    cols = jnp.transpose(jnp.concatenate([tile[0], jnp.zeros((120, 128), F32)], axis=0))
+def normalise_body(tok, tiles, gain, out):
+    count = tok.shape[1]
+    held = [tiles[k] for k in range(8)]
+    mean = sum(h[0:1] for h in held) * (1.0 / 8)
+    squares = sum(h[1:2] + (h[0:1] - mean) * (h[0:1] - mean) * float(count) for h in held)
+    inverse = lax.rsqrt(squares * (1.0 / (8 * count)) + 1e-05)
+    cols = jnp.transpose(jnp.concatenate([mean, inverse, jnp.zeros((126, 128), F32)], axis=0))
     value = tok[...].astype(F32)
     value = ((value - cols[:64, 0:1]) * cols[:64, 1:2] * gain[...]).astype(BF)
     order = one_hot(64, 64, lambda o: ((o >> 2) & 1) * 32 + (o >> 3) * 4 + (o & 3))
     out[...] = jnp.dot(order, value, preferred_element_type=F32).astype(BF)
 
 
-def normalise(tok, tile, gain):
+def normalise(tok, tiles, gain):
     return one_step(
         normalise_body,
         [IN_VMEM] * 3,
@@ -167,47 +150,32 @@
         tok.size * 6,
         tok.size * 4,
         "normalise",
-    )(tok, tile, gain)
+    )(tok, tiles, gain)
 
 
 def project_body(places, place, *refs):
     count = len(places)
     halves = refs[: 2 * count]
     wq, wkv = refs[2 * count : 2 * count + 2]
-    far, near, rows, sums, sems_in, sems_out = refs[-6:]
+    far, near = refs[-2:]
     x, y, c = place[0], place[1], place[3]
     nq = wq.shape[1]
-    loads = [
-        pltpu.make_async_copy(
-            ref, rows.at[k // 2, pl.ds((k % 2) * 128, 128)], sems_in.at[k // 2, k % 2]
-        )
-        for k, ref in enumerate(halves)
-    ]
-    for copy in loads:
-        copy.start()
-    for i, d1 in enumerate(places):
-        loads[2 * i].wait()
-        loads[2 * i + 1].wait()
-        sums[i, :, :nq] = jnp.dot(rows[i], wq[...], preferred_element_type=F32)
-        sums[i, :, nq:] = jnp.dot(rows[i], wkv[...], preferred_element_type=F32)
-        for d2 in range(4):
+    for k, ref in enumerate(halves):
+        d1 = places[k // 2]
+        q = jnp.dot(ref[...], wq[...], preferred_element_type=F32)
+        kv = jnp.dot(ref[...], wkv[...], preferred_element_type=F32)
+        for i in range(2):
+            d2 = (k % 2) * 2 + i
             bx = (x + jnp.where(c == 0, d2, d1)) & 3
             by = (y + jnp.where(c == 0, d1, d2)) & 3
             slot = by * 2 + (bx & 1)
-            source = sums.at[i, pl.ds(d2 * 64, 64)]
-
-            @pl.when((bx >> 1) == c)
-            def _(source=source, slot=slot, sem=sems_out.at[i, d2]):
-                pltpu.make_async_copy(source, near.at[slot], sem).start()
-
-            @pl.when((bx >> 1) != c)
-            def _(source=source, slot=slot, sem=sems_out.at[i, d2]):
-                pltpu.make_async_copy(source, far.at[slot], sem).start()
-
-    for i in range(count):
-        for d2 in range(4):
-            source = sums.at[i, pl.ds(d2 * 64, 64)]
-            pltpu.make_async_copy(source, near.at[0], sems_out.at[i, d2]).wait()
+            rows = slice(i * 64, i * 64 + 64)
+            for out, mine in ((near, (bx >> 1) == c), (far, (bx >> 1) != c)):
+
+                @pl.when(mine)
+                def _(out=out, slot=slot, rows=rows, q=q, kv=kv):
+                    out[slot, :, :nq] = q[rows]
+                    out[slot, :, nq:] = kv[rows]
 
 
 def project(places, place, halves, wq, wkv, held):
@@ -217,15 +185,9 @@
     rows = 256 * count
     return pl.pallas_call(
         functools.partial(project_body, places),
-        in_specs=[IN_SMEM] + [IN_HBM] * (2 * count) + [IN_VMEM] * 2 + [IN_HBM] * len(held),
-        out_specs=[IN_HBM] * 2,
+        in_specs=[IN_SMEM] + [IN_VMEM] * (2 * count + 2 + len(held)),
+        out_specs=[IN_VMEM] * 2,
         out_shape=[jax.ShapeDtypeStruct((8, 64, n), F32)] * 2,
-        scratch_shapes=[
-            pltpu.VMEM((count, 256, width), BF),
-            pltpu.VMEM((count, 256, n), F32),
-            pltpu.SemaphoreType.DMA((count, 2)),
-            pltpu.SemaphoreType.DMA((count, 4)),
-        ],
         input_output_aliases={2 * count + 3 + i: i for i in range(len(held))},
         compiler_params=pltpu.CompilerParams(vmem_limit_bytes=VMEM_LIMIT),
         cost_estimate=pl.CostEstimate(
@@ -240,12 +202,19 @@
 def attend_body(lens, x, keys_hbm, values_hbm, out, keys, values, sems):
     nq = out.shape[-1]
     rows, length, dim = keys.shape
-    copies = []
+    key_copies = [
+        pltpu.make_async_copy(keys_hbm.at[row], keys.at[row], sems.at[0, row])
+        for row in range(rows)
+    ]
+    value_copies = [
+        pltpu.make_async_copy(values_hbm.at[row], values.at[row], sems.at[1, row])
+        for row in range(rows)
+    ]
+    key_copies[0].start()
     for row in range(rows):
-        copies.append(pltpu.make_async_copy(keys_hbm.at[row], keys.at[row], sems.at[0, row]))
-        copies.append(pltpu.make_async_copy(values_hbm.at[row], values.at[row], sems.at[1, row]))
-    for copy in copies:
-        copy.start()
+        if row + 1 < rows:
+            key_copies[row + 1].start()
+        value_copies[row].start()
     piece = 2 * dim // 16
     factor = dim ** (-0.5)
     heads = nq // dim
@@ -261,10 +230,8 @@
     count = heads * 32
     step = lax.broadcasted_iota(jnp.int32, (count, 1), 0) & 1
     position = lax.broadcasted_iota(jnp.int32, (1, length), 1)
-    placed = None
-    for row in range(rows):
-        for copy in copies[2 * row : 2 * row + 2]:
-            copy.wait()
+
+    def scores_of(row):
         pick = one_hot(32, 128, lambda i: (i >> 1) * 8 + (i & 1) * 4 + row)
         mine = jnp.dot(pick, flat[:, :nq], preferred_element_type=F32).astype(BF)
         query = jnp.concatenate([mine[:, h * dim : (h + 1) * dim] for h in range(heads)], axis=0)
@@ -277,26 +244,40 @@
         scores = jnp.where(position < lens[row], scores, -1e30)
         query_f = query.astype(F32)
         key_0, key_1 = fresh[row : row + 1, :dim], fresh[rows + row : rows + row + 1, :dim]
-        val_0, val_1 = fresh[row : row + 1, dim:], fresh[rows + row : rows + row + 1, dim:]
         new_0 = jnp.sum(query_f * key_0, axis=-1, keepdims=True) * factor
         new_1 = jnp.sum(query_f * key_1, axis=-1, keepdims=True) * factor
-        new_1 = jnp.where(step == 1, new_1, -1e30)
+        return scores, new_0, jnp.where(step == 1, new_1, -1e30)
+
+    def weights_of(scores, new_0, new_1):
         top = jnp.maximum(jnp.max(scores, axis=-1, keepdims=True), jnp.maximum(new_0, new_1))
         exp_c = jnp.exp(scores - top)
         exp_0 = jnp.exp(new_0 - top)
         exp_1 = jnp.exp(new_1 - top)
         scale = 1.0 / (jnp.sum(exp_c, axis=-1, keepdims=True) + exp_0 + exp_1)
-        weight = (exp_c * scale).astype(BF)
+        return (exp_c * scale).astype(BF), (exp_0 * scale).astype(BF), (exp_1 * scale).astype(BF)
+
+    def mix(row, weight, weight_0, weight_1):
+        val_0, val_1 = fresh[row : row + 1, dim:], fresh[rows + row : rows + row + 1, dim:]
         mixed = jnp.dot(weight, values[row], preferred_element_type=F32)
-        mixed = mixed + (exp_0 * scale).astype(BF).astype(F32) * val_0
-        mixed = mixed + (exp_1 * scale).astype(BF).astype(F32) * val_1
+        mixed = mixed + weight_0.astype(F32) * val_0 + weight_1.astype(F32) * val_1
         mixed = mixed.astype(BF)
         mixed = jnp.concatenate([mixed[h * 32 : (h + 1) * 32] for h in range(heads)], axis=1)
         sub = lax.broadcasted_iota(jnp.int32, (128, 32), 0)
         lane = lax.broadcasted_iota(jnp.int32, (128, 32), 1)
         back = jnp.where(sub == (lane >> 1) * 8 + (lane & 1) * 4 + row, 1.0, 0.0).astype(BF)
-        term = jnp.dot(back, mixed, preferred_element_type=F32)
-        placed = term if placed is None else placed + term
+        return jnp.dot(back, mixed, preferred_element_type=F32)
+
+    key_copies[0].wait()
+    ahead = scores_of(0)
+    placed = jnp.zeros((128, nq), F32)
+    for row in range(rows):
+        scores = ahead
+        if row + 1 < rows:
+            key_copies[row + 1].wait()
+        value_copies[row].wait()
+        if row + 1 < rows:
+            ahead = scores_of(row + 1)
+        placed = placed + mix(row, *weights_of(*scores))
     placed = placed.reshape(16, 8, nq).astype(BF)
     for copy in range(4):
         out[copy] = placed
@@ -473,14 +454,8 @@
     return lax.optimization_barrier((value, other))
 
 
-def gather_and_project(place, tok, gain, wq, wkv, width_all):
-    count = tok.shape[1]
-    stat = row_statistics(tok)
-    stat = combine([stat, send(stat, other_core)], count, 0)
-    stat = combine([stat, send(stat, lambda z, c, y, x: (z ^ 1, c, y, x))], count * 2, 0)
-    stat = combine(
-        [stat, send(stat, lambda z, c, y, x: (z ^ 2, c, y, x))], count * 4, width_all
-    )
+def gather_and_project(place, tok, gain, wq, wkv):
+    stat = lax.all_to_all(row_statistics(tok), "gx", 0, 0)
     tok = normalise(tok, stat, gain)
     b1, b2, b3 = [send(tok, first_axis(d)) for d in (-1, 2, 1)]
     low = jnp.concatenate([tok, b1], axis=0)
@@ -513,7 +488,7 @@
     wkv = jnp.pad(wkv, ((0, 0), (0, 128 - piece)))
 
     far, near = gather_and_project(
-        place, tokens.reshape(64, width), gain, w_query, wkv, width * 8
+        place, tokens.reshape(64, width), gain, w_query, wkv
     )
     n = near.shape[-1]
 

time: 160 us -> 155 us (0.969)
  Pallas kernels: 32.8 us -> 27 us
  waiting for transfers between devices: 44.3 us -> 47.7 us
  blocking collectives: 43.6 us -> 41.5 us
    ppermute x23 -> x20, starting transfers between devices: 31.9 us -> 26 us  [send(): return lax.ppermute(value, ('gx', 'gy'), flat_perm(place))]
    all_to_all x0 -> x1, starting transfers between devices: none -> 5.31 us  [gather_and_project(): stat = lax.all_to_all(row_statistics(tok), 'gx', 0, 0)]
    pallas_call x3, Pallas kernels: 14 us -> 8.93 us  [project(): pl.pallas_call(functools.partial(project_body, places), in_specs=[IN_SMEM...]
    all_to_all x0 -> x1, waiting for transfers between devices: none -> 4.73 us  [gather_and_project(): stat = lax.all_to_all(row_statistics(tok), 'gx', 0, 0)]
    all_to_all x2, blocking collectives: 43.6 us -> 41.5 us  [exchange(): return lax.all_to_all(value, ('gx', 'gy'), 0, 0, axis_index_groups=groups)]
    ppermute x23 -> x20, waiting for transfers between devices: 44.3 us -> 43 us  [send(): return lax.ppermute(value, ('gx', 'gy'), flat_perm(place))]
  transfers between devices with their start and end apart: 23 -> 21, of which waited for: 15 -> 15; matrix products, arithmetic and copies ran while one was open for 1% -> 1% of each run, Pallas kernels for 9% -> 7%
where the time goes in v4:
time: 155 us; the launch traced here: 154 us
  waiting for transfers between devices  47.7 us (31%)
  blocking collectives  41.5 us (27%)
  starting transfers between devices  31.3 us (20%)
  Pallas kernels  27 us (17%)
  local copies, waits for them, and re-layouts  5.14 us (3%)
    ppermute x20, waiting for transfers between devices, send(): return lax.ppermute(value, ('gx', 'gy'), flat_perm(place))  43 us
    all_to_all x2, blocking collectives, exchange(): return lax.all_to_all(value, ('gx', 'gy'), 0, 0, axis_index_groups=groups)  41.5 us
    ppermute x20, starting transfers between devices, send(): return lax.ppermute(value, ('gx', 'gy'), flat_perm(place))  26 us
    pallas_call x3, Pallas kernels, project(): pl.pallas_call(functools.partial(project_body, places), in_specs=[IN_SMEM...  8.93 us
    pallas_call x1, Pallas kernels, attend(): pl.pallas_call(attend_body, in_specs=[IN_SMEM, IN_VMEM, IN_HBM, IN_HBM],...  7.46 us
    all_to_all x1, starting transfers between devices, gather_and_project(): stat = lax.all_to_all(row_statistics(tok), 'gx', 0, 0)  5.31 us
    all_to_all x1, waiting for transfers between devices, gather_and_project(): stat = lax.all_to_all(row_statistics(tok), 'gx', 0, 0)  4.73 us
    unnamed x12, local copies, waits for them, and re-layouts  4.09 us
  transfers between devices with their start and end apart: 21, of which 15 were waited for; matrix products, arithmetic and copies ran while one was open for 1% of the time, Pallas kernels for 7%

profile of v4, /device:TPU:24, one launch (start us, length us, event | category | flops | bytes accessed | tf_op | source)
XLA Modules:
  0.0 154.1 jit_solution(3531971134520734959)
XLA Ops:
  0.0 1.1 copy-done.4
  1.1 0.9 row_statistics.1
  2.0 5.3 %all-to-all-start = ((f32[8,8,128]{2,1,0:T(8,128)}), f32[8,8,128]{2,1,0:T(8,128)S(1)}, u32[]{:S(2)}, u32[]{:S(2)}) async-start(f32[8,8,128]{2,1,0:T(8,128)} %row_statistics.1), calls=%async_computation | async-start | bytes 65536 | tf_op jit(solution)/shard_map/all_to_all | solution.py:458
  7.4 0.7 broadcast_in_dim.3.gain
  8.1 4.7 %all-to-all-done.tiles = f32[8,8,128]{2,1,0:T(8,128)S(1)} async-done(((f32[8,8,128]{2,1,0:T(8,128)}), f32[8,8,128]{2,1,0:T(8,128)S(1)}, u32[]{:S(2)}, u32[]{:S(2)}) %all-to-all-start) | async-done | bytes 32800 | tf_op jit(solution)/shard_map/all_to_all | solution.py:458
  12.8 1.0 copy-done.5
  13.8 0.4 normalise.1
  14.2 2.8 %collective-permute-start = (bf16[64,2304]{1,0:T(8,128)(2,1)S(1)}, bf16[64,2304]{1,0:T(8,128)(2,1)S(1)}, u32[]{:S(2)}, u32[]{:S(2)}) collective-permute-start(bf16[64,2304]{1,0:T(8,128)(2,1)S(1)} %normalise.1), channel_id=1, source_target_pairs={{0,3},{1,0},{2,1},{3,2},{4,7},{5,4},{6,5},{7,6},{8,11},{9,8},{10,9... | collective-permute-start | bytes 884744 | tf_op jit(solution)/shard_map/ppermute | solution.py:29
  17.0 0.0 collective-permute-start.2
  17.0 2.3 %collective-permute-start.1 = (bf16[64,2304]{1,0:T(8,128)(2,1)S(1)}, bf16[64,2304]{1,0:T(8,128)(2,1)S(1)}, u32[]{:S(2)}, u32[]{:S(2)}) collective-permute-start(bf16[64,2304]{1,0:T(8,128)(2,1)S(1)} %normalise.1), channel_id=1, source_target_pairs={{0,2},{1,3},{2,0},{3,1},{4,6},{5,7},{6,4},{7,5},{8,10},{9,11},{10,... | collective-permute-start | bytes 884744 | tf_op jit(solution)/shard_map/ppermute | solution.py:29
  19.3 1.9 %collective-permute-done = bf16[64,2304]{1,0:T(8,128)(2,1)S(1)} collective-permute-done((bf16[64,2304]{1,0:T(8,128)(2,1)S(1)}, bf16[64,2304]{1,0:T(8,128)(2,1)S(1)}, u32[]{:S(2)}, u32[]{:S(2)}) %collective-permute-start) | collective-permute-done | bytes 294944 | tf_op jit(solution)/shard_map/ppermute | solution.py:29
  21.3 6.8 %collective-permute-done.2 = bf16[64,2304]{1,0:T(8,128)(2,1)S(1)} collective-permute-done((bf16[64,2304]{1,0:T(8,128)(2,1)S(1)}, bf16[64,2304]{1,0:T(8,128)(2,1)S(1)}, u32[]{:S(2)}, u32[]{:S(2)}) %collective-permute-start.2) | collective-permute-done | bytes 294944 | tf_op jit(solution)/shard_map/ppermute | solution.py:29
  28.1 0.0 collective-permute-done.1
  28.2 0.3 collective-permute-start.3
  28.4 1.8 %collective-permute-start.5 = (bf16[128,2304]{1,0:T(8,128)(2,1)S(1)}, bf16[128,2304]{1,0:T(8,128)(2,1)}, u32[]{:S(2)}, u32[]{:S(2)}) collective-permute-start(bf16[128,2304]{1,0:T(8,128)(2,1)S(1)} %pad_maximum_fusion.1.refs_1_), channel_id=1, source_target_pairs={{0,12},{1,13},{2,14},{3,15},{4,0},{5,1},{6,2},{7,3},{8,4},{9,5},{1... | collective-permute-start | bytes 1769480 | tf_op jit(solution)/shard_map/ppermute | solution.py:29
  30.3 0.2 constant_dynamic-slice_fusion
  30.5 0.1 pad.4.refs_3_.refs_5_
  30.6 0.8 collective-permute-start.7
  31.4 2.5 %collective-permute-start.8 = (bf16[128,2304]{1,0:T(8,128)(2,1)S(1)}, bf16[128,2304]{1,0:T(8,128)(2,1)S(1)}, u32[]{:S(2)}, u32[]{:S(2)}) collective-permute-start(bf16[128,2304]{1,0:T(8,128)(2,1)S(1)} %pad_maximum_fusion.1.refs_1_), channel_id=1, source_target_pairs={{0,4},{1,5},{2,6},{3,7},{4,8},{5,9},{6,10},{7,11},{8,12},{9,13},{1... | collective-permute-start | bytes 1769480 | tf_op jit(solution)/shard_map/ppermute | solution.py:29
  33.9 0.1 pad_add_fusion.place
  34.0 2.0 %copy-done.1 = bf16[2304,768]{1,0:T(8,128)(2,1)S(1)} copy-done((bf16[2304,768]{1,0:T(8,128)(2,1)S(1)}, bf16[2304,768]{1,0:T(8,128)(2,1)}, u32[]{:S(2)}) %copy-start.1) | copy-done | bytes 3538968
  36.0 2.2 %project.3 = (f32[8,64,896]{2,1,0:T(8,128)S(1)}, f32[8,64,896]{2,1,0:T(8,128)S(1)}) custom-call(s32[4]{0:T(128)S(1)} %pad_add_fusion.place, bf16[128,2304]{1,0:T(8,128)(2,1)S(1)} %pad_maximum_fusion.refs_0_, bf16[128,2304]{1,0:T(8,128)(2,1)S(1)} %pad_maximum_fusion.1.refs_1_, bf16[2304,768]{1,0:T(8,128)(2,1)S(1)} %copy-done.1, ...), custom_call_target="tpu_custom_call" | custom-call | flops 1056964608 | bytes 6225920 | tf_op jit(solution)/shard_map/project/pallas_call | solution.py:186
  38.2 0.0 collective-permute-done.3.refs_2_
  38.2 1.4 collective-permute-done.5.refs_1_
  39.6 0.6 collective-permute-start.6
  40.2 2.6 %collective-permute-start.4 = (bf16[128,2304]{1,0:T(8,128)(2,1)}, bf16[128,2304]{1,0:T(8,128)(2,1)S(1)}, u32[]{:S(2)}, u32[]{:S(2)}) collective-permute-start(bf16[128,2304]{1,0:T(8,128)(2,1)} %collective-permute-done.3.refs_2_), channel_id=1, source_target_pairs={{0,4},{1,5},{2,6},{3,7},{4,8},{5,9},{6,10},{7,11},{8,12},{9,13},{1... | collective-permute-start | bytes 1769480 | tf_op jit(solution)/shard_map/ppermute | solution.py:29
  42.9 3.0 %collective-permute-done.7.refs_0_ = bf16[128,2304]{1,0:T(8,128)(2,1)S(1)} collective-permute-done((bf16[128,2304]{1,0:T(8,128)(2,1)S(1)}, bf16[128,2304]{1,0:T(8,128)(2,1)S(1)}, u32[]{:S(2)}, u32[]{:S(2)}) %collective-permute-start.7) | collective-permute-done | bytes 589856 | tf_op jit(solution)/shard_map/ppermute | solution.py:29
  45.9 0.0 collective-permute-done.8.refs_3_
  45.9 4.6 %project.4 = (f32[8,64,896]{2,1,0:T(8,128)S(1)}, f32[8,64,896]{2,1,0:T(8,128)S(1)}) custom-call(s32[4]{0:T(128)S(1)} %pad_add_fusion.place, bf16[128,2304]{1,0:T(8,128)(2,1)S(1)} %collective-permute-done.7.refs_0_, bf16[128,2304]{1,0:T(8,128)(2,1)} %collective-permute-done.5.refs_1_, ...), custom_call_target="tpu_custom_call", output_to_operand_aliasing={{0}: (7, {}), {1}: (8, {})} | custom-call | flops 2113929216 | bytes 8323072 | tf_op jit(solution)/shard_map/project/pallas_call | solution.py:186
  50.4 1.8 %collective-permute-done.6.refs_1_ = bf16[128,2304]{1,0:T(8,128)(2,1)S(1)} collective-permute-done((bf16[128,2304]{1,0:T(8,128)(2,1)}, bf16[128,2304]{1,0:T(8,128)(2,1)S(1)}, u32[]{:S(2)}, u32[]{:S(2)}) %collective-permute-start.6) | collective-permute-done | bytes 589856 | tf_op jit(solution)/shard_map/ppermute | solution.py:29
  52.2 2.2 %project.5 = (f32[8,64,896]{2,1,0:T(8,128)S(1)}, f32[8,64,896]{2,1,0:T(8,128)S(1)}) custom-call(s32[4]{0:T(128)S(1)} %pad_add_fusion.place, bf16[128,2304]{1,0:T(8,128)(2,1)S(1)} %collective-permute-done.4.refs_0_, bf16[128,2304]{1,0:T(8,128)(2,1)S(1)} %collective-permute-done.6.refs_1_, ...), custom_call_target="tpu_custom_call", output_to_operand_aliasing={{0}: (5, {}), {1}: (6, {})} | custom-call | flops 1056964608 | bytes 6225920 | tf_op jit(solution)/shard_map/project/pallas_call | solution.py:186
  54.4 0.1 collective-permute-start.9
  54.5 3.8 %collective-permute-done.9 = f32[8,64,896]{2,1,0:T(8,128)S(1)} collective-permute-done((f32[8,64,896]{2,1,0:T(8,128)S(1)}, f32[8,64,896]{2,1,0:T(8,128)S(1)}, u32[]{:S(2)}, u32[]{:S(2)}) %collective-permute-start.9) | collective-permute-done | bytes 1835040 | tf_op jit(solution)/shard_map/ppermute | solution.py:29
  58.2 0.3 multiply_convert_fusion
  58.6 21.3 %all_to_all.15 = f16[64,8,896]{2,1,0:T(8,128)(2,1)S(1)} all-to-all(f16[64,8,896]{2,1,0:T(8,128)(2,1)S(1)} %bitcast.15), channel_id=1, replica_groups={{0,1,2,3,4,5,6,7,8,9,10,11,12,13,14,15,32,33,34,35,36,37,38,39,40,41,42..., dimensions={0} | all-to-all | bytes 1835008 | tf_op jit(solution)/shard_map/all_to_all | solution.py:50
  79.8 0.1 convert_reduce_fusion
  79.9 0.7 multiply_convert_fusion.1.x
  80.7 7.5 %attend.1 = bf16[4,16,8,768]{3,2,1,0:T(8,128)(2,1)} custom-call(s32[4]{0:T(128)} %lens.1, bf16[16,8,896]{2,1,0:T(8,128)(2,1)} %multiply_convert_fusion.1.x, bf16[4,2048,256]{2,1,0:T(8,128)(2,1)} %keys_hbm.1, bf16[4,2048,256]{2,1,0:T(8,128)(2,1)} %values_hbm.1), custom_call_target="tpu_custom_call" | custom-call | flops 805306368 | bytes 8388608 | tf_op jit(solution)/shard_map/attend/pallas_call | solution.py:288
  88.1 20.2 %all_to_all.16 = bf16[64,8,768]{2,1,0:T(8,128)(2,1)S(1)} all-to-all(bf16[64,8,768]{2,1,0:T(8,128)(2,1)} %bitcast.16), channel_id=1, replica_groups={{0,1,2,3,4,5,6,7,8,9,10,11,12,13,14,15,32,33,34,35,36,37,38,39,40,41,42..., dimensions={0} | all-to-all | bytes 1572864 | tf_op jit(solution)/shard_map/all_to_all | solution.py:50
  108.4 2.3 %collective-permute-done.10.cross = bf16[4,16,8,768]{3,2,1,0:T(8,128)(2,1)S(1)} collective-permute-done((bf16[4,16,8,768]{3,2,1,0:T(8,128)(2,1)S(1)}, bf16[4,16,8,768]{3,2,1,0:T(8,128)(2,1)S(1)}, u32[]{:S(2)}, u32[]{:S(2)}) %collective-permute-start.10) | collective-permute-done | bytes 786464 | tf_op jit(solution)/shard_map/ppermute | solution.py:29
  110.7 1.7 %output_far.1 = (bf16[16,64,768]{2,1,0:T(8,128)(2,1)S(1)}, bf16[128,2304]{1,0:T(8,128)(2,1)S(1)}, bf16[128,2304]{1,0:T(8,128)(2,1)S(1)}) custom-call(s32[4]{0:T(128)S(1)} %pad_add_fusion.place, bf16[4,16,8,768]{3,2,1,0:T(8,128)(2,1)S(1)} %bitcast.11, bf16[4,16,8,768]{3,2,1,0:T(8,128)(2,1)S(1)} %collective-permute-done.10.cross, bf16[768,2304]{1,0:T(8,128)(2,1)S(1)} %copy-done.3), custom_call_target="tpu_custom_call" | custom-call | flops 905969664 | bytes 7864320 | tf_op jit(solution)/shard_map/output_far/pallas_call | solution.py:334
  112.4 2.9 %collective-permute-start.11 = (bf16[128,2304]{1,0:T(8,128)(2,1)S(1)}, bf16[128,2304]{1,0:T(8,128)(2,1)S(1)}, u32[]{:S(2)}, u32[]{:S(2)}) collective-permute-start(bf16[128,2304]{1,0:T(8,128)(2,1)S(1)} %get-tuple-element.44), channel_id=1, source_target_pairs={{0,4},{1,5},{2,6},{3,7},{4,8},{5,9},{6,10},{7,11},{8,12},{9,13},{1... | collective-permute-start | bytes 1769480 | tf_op jit(solution)/shard_map/ppermute | solution.py:29
  115.3 0.0 collective-permute-start.12
  115.3 2.6 %output_near.1 = (bf16[128,2304]{1,0:T(8,128)(2,1)S(1)}, bf16[128,2304]{1,0:T(8,128)(2,1)S(1)}, bf16[128,2304]{1,0:T(8,128)(2,1)S(1)}, bf16[128,2304]{1,0:T(8,128)(2,1)S(1)}) custom-call(s32[4]{0:T(128)S(1)} %pad_add_fusion.place, bf16[16,64,768]{2,1,0:T(8,128)(2,1)S(1)} %get-tuple-element.42.left, bf16[768,2304]{1,0:T(8,128)(2,1)S(1)} %copy-done.3), custom_call_target="tpu_custom_call" | custom-call | flops 1811939328 | bytes 7471104 | tf_op jit(solution)/shard_map/output_near/pallas_call | solution.py:352
  117.8 3.3 %collective-permute-start.14 = (bf16[128,2304]{1,0:T(8,128)(2,1)S(1)}, bf16[128,2304]{1,0:T(8,128)(2,1)S(1)}, u32[]{:S(2)}, u32[]{:S(2)}) collective-permute-start(bf16[128,2304]{1,0:T(8,128)(2,1)S(1)} %get-tuple-element.48), channel_id=1, source_target_pairs={{0,4},{1,5},{2,6},{3,7},{4,8},{5,9},{6,10},{7,11},{8,12},{9,13},{1... | collective-permute-start | bytes 1769480 | tf_op jit(solution)/shard_map/ppermute | solution.py:29
  121.1 0.0 collective-permute-start.15
  121.1 1.5 collective-permute-done.11.a1
  122.7 3.7 %collective-permute-done.12.b1 = bf16[128,2304]{1,0:T(8,128)(2,1)S(1)} collective-permute-done((bf16[128,2304]{1,0:T(8,128)(2,1)S(1)}, bf16[128,2304]{1,0:T(8,128)(2,1)S(1)}, u32[]{:S(2)}, u32[]{:S(2)}) %collective-permute-start.12) | collective-permute-done | bytes 589856 | tf_op jit(solution)/shard_map/ppermute | solution.py:29
  126.4 0.3 pair_add.1
  126.6 0.1 collective-permute-start.13
  126.7 2.0 %collective-permute-start.16 = (bf16[128,2304]{1,0:T(8,128)(2,1)S(1)}, bf16[128,2304]{1,0:T(8,128)(2,1)S(1)}, u32[]{:S(2)}, u32[]{:S(2)}) collective-permute-start(bf16[128,2304]{1,0:T(8,128)(2,1)S(1)} %get-tuple-element.50), channel_id=1, source_target_pairs={{0,12},{1,13},{2,14},{3,15},{4,0},{5,1},{6,2},{7,3},{8,4},{9,5},{1... | collective-permute-start | bytes 1769480 | tf_op jit(solution)/shard_map/ppermute | solution.py:29
  128.7 1.6 %output_own.1.a = bf16[256,2304]{1,0:T(8,128)(2,1)S(1)} custom-call(s32[4]{0:T(128)S(1)} %pad_add_fusion.place, bf16[16,64,768]{2,1,0:T(8,128)(2,1)S(1)} %get-tuple-element.42.left, bf16[768,2304]{1,0:T(8,128)(2,1)S(1)} %copy-done.3), custom_call_target="tpu_custom_call" | custom-call | flops 905969664 | bytes 6291456 | tf_op jit(solution)/shard_map/output_own/pallas_call | solution.py:369
  130.4 0.0 collective-permute-done.14.b1
  130.4 2.3 %collective-permute-done.15.c0 = bf16[128,2304]{1,0:T(8,128)(2,1)S(1)} collective-permute-done((bf16[128,2304]{1,0:T(8,128)(2,1)S(1)}, bf16[128,2304]{1,0:T(8,128)(2,1)S(1)}, u32[]{:S(2)}, u32[]{:S(2)}) %collective-permute-start.15) | collective-permute-done | bytes 589856 | tf_op jit(solution)/shard_map/ppermute | solution.py:29
  132.7 3.9 %collective-permute-done.13.b0 = bf16[128,2304]{1,0:T(8,128)(2,1)S(1)} collective-permute-done((bf16[128,2304]{1,0:T(8,128)(2,1)S(1)}, bf16[128,2304]{1,0:T(8,128)(2,1)S(1)}, u32[]{:S(2)}, u32[]{:S(2)}) %collective-permute-start.13) | collective-permute-done | bytes 589856 | tf_op jit(solution)/shard_map/ppermute | solution.py:29
  136.6 2.4 %collective-permute-done.16.c1 = bf16[128,2304]{1,0:T(8,128)(2,1)S(1)} collective-permute-done((bf16[128,2304]{1,0:T(8,128)(2,1)S(1)}, bf16[128,2304]{1,0:T(8,128)(2,1)S(1)}, u32[]{:S(2)}, u32[]{:S(2)}) %collective-permute-start.16) | collective-permute-done | bytes 589856 | tf_op jit(solution)/shard_map/ppermute | solution.py:29
  139.0 1.5 group_sum.1
  140.5 0.6 collective-permute-start.17
  141.2 1.8 %collective-permute-start.18 = (bf16[64,2304]{1,0:T(8,128)(2,1)S(1)}, bf16[64,2304]{1,0:T(8,128)(2,1)S(1)}, u32[]{:S(2)}, u32[]{:S(2)}) collective-permute-start(bf16[64,2304]{1,0:T(8,128)(2,1)S(1)} %get-tuple-element.53), channel_id=1, source_target_pairs={{0,2},{1,3},{2,0},{3,1},{4,6},{5,7},{6,4},{7,5},{8,10},{9,11},{10,... | collective-permute-start | bytes 884744 | tf_op jit(solution)/shard_map/ppermute | solution.py:29
  143.0 1.5 collective-permute-start.19
  144.5 7.2 %collective-permute-done.17.r1 = bf16[64,2304]{1,0:T(8,128)(2,1)S(1)} collective-permute-done((bf16[64,2304]{1,0:T(8,128)(2,1)S(1)}, bf16[64,2304]{1,0:T(8,128)(2,1)S(1)}, u32[]{:S(2)}, u32[]{:S(2)}) %collective-permute-start.17) | collective-permute-done | bytes 294944 | tf_op jit(solution)/shard_map/ppermute | solution.py:29
  151.7 0.0 collective-permute-done.18.r2
  151.7 0.9 collective-permute-done.19.r3
  152.6 1.6 %last_sum.1 = bf16[2,32,2304]{2,1,0:T(8,128)(2,1)} custom-call(s32[4]{0:T(128)S(1)} %pad_add_fusion.place, f32[64,2304]{1,0:T(8,128)S(1)} %get-tuple-element.51.own, bf16[64,2304]{1,0:T(8,128)(2,1)S(1)} %collective-permute-done.17.r1, bf16[64,2304]{1,0:T(8,128)(2,1)S(1)} %collective-permute-done.18.r2, bf16[64,2304]{1,0:T(8,128)(2,1)S(1)} %collective-permute-done.19.r3), custom_call_target="tpu_custom_call" | custom-call | flops 589824 | bytes 1769472 | tf_op jit(solution)/shard_map/last_sum/pallas_call | solution.py:442
  (13 shorter events, 0.1 us)
Async XLA Ops:
  0.0 30.3 %copy-start = (bf16[2304,512]{1,0:T(8,128)(2,1)S(1)}, bf16[2304,512]{1,0:T(8,128)(2,1)}, u32[]{:S(2)}) copy-start(bf16[2304,512]{1,0:T(8,128)(2,1)} %param.11) | copy-start | bytes 7077892
  0.0 1.1 copy-start.4
  2.0 10.8 %all-to-all-start = ((f32[8,8,128]{2,1,0:T(8,128)}), f32[8,8,128]{2,1,0:T(8,128)S(1)}, u32[]{:S(2)}, u32[]{:S(2)}) async-start(f32[8,8,128]{2,1,0:T(8,128)} %row_statistics.1), calls=%async_computation | async-start | bytes 65536 | tf_op jit(solution)/shard_map/all_to_all | solution.py:458
  12.8 1.0 copy-start.5
  14.2 7.1 %collective-permute-start = (bf16[64,2304]{1,0:T(8,128)(2,1)S(1)}, bf16[64,2304]{1,0:T(8,128)(2,1)S(1)}, u32[]{:S(2)}, u32[]{:S(2)}) collective-permute-start(bf16[64,2304]{1,0:T(8,128)(2,1)S(1)} %normalise.1), channel_id=1, source_target_pairs={{0,3},{1,0},{2,1},{3,2},{4,7},{5,4},{6,5},{7,6},{8,11},{9,8},{10,9... | collective-permute-start | bytes 884744 | tf_op jit(solution)/shard_map/ppermute | solution.py:29
  17.0 11.1 %collective-permute-start.2 = (bf16[64,2304]{1,0:T(8,128)(2,1)S(1)}, bf16[64,2304]{1,0:T(8,128)(2,1)S(1)}, u32[]{:S(2)}, u32[]{:S(2)}) collective-permute-start(bf16[64,2304]{1,0:T(8,128)(2,1)S(1)} %normalise.1), channel_id=1, source_target_pairs={{0,1},{1,2},{2,3},{3,0},{4,5},{5,6},{6,7},{7,4},{8,9},{9,10},{10,1... | collective-permute-start | bytes 884744 | tf_op jit(solution)/shard_map/ppermute | solution.py:29
  17.0 11.1 %collective-permute-start.1 = (bf16[64,2304]{1,0:T(8,128)(2,1)S(1)}, bf16[64,2304]{1,0:T(8,128)(2,1)S(1)}, u32[]{:S(2)}, u32[]{:S(2)}) collective-permute-start(bf16[64,2304]{1,0:T(8,128)(2,1)S(1)} %normalise.1), channel_id=1, source_target_pairs={{0,2},{1,3},{2,0},{3,1},{4,6},{5,7},{6,4},{7,5},{8,10},{9,11},{10,... | collective-permute-start | bytes 884744 | tf_op jit(solution)/shard_map/ppermute | solution.py:29
  28.2 10.1 %collective-permute-start.3 = (bf16[128,2304]{1,0:T(8,128)(2,1)S(1)}, bf16[128,2304]{1,0:T(8,128)(2,1)}, u32[]{:S(2)}, u32[]{:S(2)}) collective-permute-start(bf16[128,2304]{1,0:T(8,128)(2,1)S(1)} %pad_maximum_fusion.refs_0_), channel_id=1, source_target_pairs={{0,4},{1,5},{2,6},{3,7},{4,8},{5,9},{6,10},{7,11},{8,12},{9,13},{1... | collective-permute-start | bytes 1769480 | tf_op jit(solution)/shard_map/ppermute | solution.py:29
  28.4 11.2 %collective-permute-start.5 = (bf16[128,2304]{1,0:T(8,128)(2,1)S(1)}, bf16[128,2304]{1,0:T(8,128)(2,1)}, u32[]{:S(2)}, u32[]{:S(2)}) collective-permute-start(bf16[128,2304]{1,0:T(8,128)(2,1)S(1)} %pad_maximum_fusion.1.refs_1_), channel_id=1, source_target_pairs={{0,12},{1,13},{2,14},{3,15},{4,0},{5,1},{6,2},{7,3},{8,4},{9,5},{1... | collective-permute-start | bytes 1769480 | tf_op jit(solution)/shard_map/ppermute | solution.py:29
  30.6 15.3 %collective-permute-start.7 = (bf16[128,2304]{1,0:T(8,128)(2,1)S(1)}, bf16[128,2304]{1,0:T(8,128)(2,1)S(1)}, u32[]{:S(2)}, u32[]{:S(2)}) collective-permute-start(bf16[128,2304]{1,0:T(8,128)(2,1)S(1)} %pad_maximum_fusion.refs_0_), channel_id=1, source_target_pairs={{0,12},{1,13},{2,14},{3,15},{4,0},{5,1},{6,2},{7,3},{8,4},{9,5},{1... | collective-permute-start | bytes 1769480 | tf_op jit(solution)/shard_map/ppermute | solution.py:29
  31.4 14.4 %collective-permute-start.8 = (bf16[128,2304]{1,0:T(8,128)(2,1)S(1)}, bf16[128,2304]{1,0:T(8,128)(2,1)S(1)}, u32[]{:S(2)}, u32[]{:S(2)}) collective-permute-start(bf16[128,2304]{1,0:T(8,128)(2,1)S(1)} %pad_maximum_fusion.1.refs_1_), channel_id=1, source_target_pairs={{0,4},{1,5},{2,6},{3,7},{4,8},{5,9},{6,10},{7,11},{8,12},{9,13},{1... | collective-permute-start | bytes 1769480 | tf_op jit(solution)/shard_map/ppermute | solution.py:29
  34.0 2.0 %copy-start.1 = (bf16[2304,768]{1,0:T(8,128)(2,1)S(1)}, bf16[2304,768]{1,0:T(8,128)(2,1)}, u32[]{:S(2)}) copy-start(bf16[2304,768]{1,0:T(8,128)(2,1)} %refs_2_.3) | copy-start | bytes 10616836
  36.0 9.9 %copy-start.2 = (bf16[2304,768]{1,0:T(8,128)(2,1)S(1)}, bf16[2304,768]{1,0:T(8,128)(2,1)}, u32[]{:S(2)}) copy-start(bf16[2304,768]{1,0:T(8,128)(2,1)} %refs_2_.3) | copy-start | bytes 10616836
  39.6 12.5 %collective-permute-start.6 = (bf16[128,2304]{1,0:T(8,128)(2,1)}, bf16[128,2304]{1,0:T(8,128)(2,1)S(1)}, u32[]{:S(2)}, u32[]{:S(2)}) collective-permute-start(bf16[128,2304]{1,0:T(8,128)(2,1)} %collective-permute-done.5.refs_1_), channel_id=1, source_target_pairs={{0,12},{1,13},{2,14},{3,15},{4,0},{5,1},{6,2},{7,3},{8,4},{9,5},{1... | collective-permute-start | bytes 1769480 | tf_op jit(solution)/shard_map/ppermute | solution.py:29
  40.2 11.9 %collective-permute-start.4 = (bf16[128,2304]{1,0:T(8,128)(2,1)}, bf16[128,2304]{1,0:T(8,128)(2,1)S(1)}, u32[]{:S(2)}, u32[]{:S(2)}) collective-permute-start(bf16[128,2304]{1,0:T(8,128)(2,1)} %collective-permute-done.3.refs_2_), channel_id=1, source_target_pairs={{0,4},{1,5},{2,6},{3,7},{4,8},{5,9},{6,10},{7,11},{8,12},{9,13},{1... | collective-permute-start | bytes 1769480 | tf_op jit(solution)/shard_map/ppermute | solution.py:29
  54.4 3.9 %collective-permute-start.9 = (f32[8,64,896]{2,1,0:T(8,128)S(1)}, f32[8,64,896]{2,1,0:T(8,128)S(1)}, u32[]{:S(2)}, u32[]{:S(2)}) collective-permute-start(f32[8,64,896]{2,1,0:T(8,128)S(1)} %get-tuple-element.41), channel_id=1, source_target_pairs={{0,16},{1,17},{2,18},{3,19},{4,20},{5,21},{6,22},{7,23},{8,24},{9,... | collective-permute-start | bytes 5505032 | tf_op jit(solution)/shard_map/ppermute | solution.py:29
  80.7 30.0 %copy-start.3 = (bf16[768,2304]{1,0:T(8,128)(2,1)S(1)}, bf16[768,2304]{1,0:T(8,128)(2,1)}, u32[]{:S(2)}) copy-start(bf16[768,2304]{1,0:T(8,128)(2,1)} %w_out.5) | copy-start | bytes 10616836
  108.4 2.3 %collective-permute-start.10 = (bf16[4,16,8,768]{3,2,1,0:T(8,128)(2,1)S(1)}, bf16[4,16,8,768]{3,2,1,0:T(8,128)(2,1)S(1)}, u32[]{:S(2)}, u32[]{:S(2)}) collective-permute-start(bf16[4,16,8,768]{3,2,1,0:T(8,128)(2,1)S(1)} %bitcast.10), channel_id=1, source_target_pairs={{0,16},{1,17},{2,18},{3,19},{4,20},{5,21},{6,22},{7,23},{8,24},{9,... | collective-permute-start | bytes 2359304 | tf_op jit(solution)/shard_map/ppermute | solution.py:29
  112.4 10.3 %collective-permute-start.11 = (bf16[128,2304]{1,0:T(8,128)(2,1)S(1)}, bf16[128,2304]{1,0:T(8,128)(2,1)S(1)}, u32[]{:S(2)}, u32[]{:S(2)}) collective-permute-start(bf16[128,2304]{1,0:T(8,128)(2,1)S(1)} %get-tuple-element.44), channel_id=1, source_target_pairs={{0,4},{1,5},{2,6},{3,7},{4,8},{5,9},{6,10},{7,11},{8,12},{9,13},{1... | collective-permute-start | bytes 1769480 | tf_op jit(solution)/shard_map/ppermute | solution.py:29
  115.3 11.1 %collective-permute-start.12 = (bf16[128,2304]{1,0:T(8,128)(2,1)S(1)}, bf16[128,2304]{1,0:T(8,128)(2,1)S(1)}, u32[]{:S(2)}, u32[]{:S(2)}) collective-permute-start(bf16[128,2304]{1,0:T(8,128)(2,1)S(1)} %get-tuple-element.46), channel_id=1, source_target_pairs={{0,12},{1,13},{2,14},{3,15},{4,0},{5,1},{6,2},{7,3},{8,4},{9,5},{1... | collective-permute-start | bytes 1769480 | tf_op jit(solution)/shard_map/ppermute | solution.py:29
  117.8 12.5 %collective-permute-start.14 = (bf16[128,2304]{1,0:T(8,128)(2,1)S(1)}, bf16[128,2304]{1,0:T(8,128)(2,1)S(1)}, u32[]{:S(2)}, u32[]{:S(2)}) collective-permute-start(bf16[128,2304]{1,0:T(8,128)(2,1)S(1)} %get-tuple-element.48), channel_id=1, source_target_pairs={{0,4},{1,5},{2,6},{3,7},{4,8},{5,9},{6,10},{7,11},{8,12},{9,13},{1... | collective-permute-start | bytes 1769480 | tf_op jit(solution)/shard_map/ppermute | solution.py:29
  121.1 11.5 %collective-permute-start.15 = (bf16[128,2304]{1,0:T(8,128)(2,1)S(1)}, bf16[128,2304]{1,0:T(8,128)(2,1)S(1)}, u32[]{:S(2)}, u32[]{:S(2)}) collective-permute-start(bf16[128,2304]{1,0:T(8,128)(2,1)S(1)} %get-tuple-element.49), channel_id=1, source_target_pairs={{0,12},{1,13},{2,14},{3,15},{4,0},{5,1},{6,2},{7,3},{8,4},{9,5},{1... | collective-permute-start | bytes 1769480 | tf_op jit(solution)/shard_map/ppermute | solution.py:29
  126.6 10.0 %collective-permute-start.13 = (bf16[128,2304]{1,0:T(8,128)(2,1)S(1)}, bf16[128,2304]{1,0:T(8,128)(2,1)S(1)}, u32[]{:S(2)}, u32[]{:S(2)}) collective-permute-start(bf16[128,2304]{1,0:T(8,128)(2,1)S(1)} %get-tuple-element.47), channel_id=1, source_target_pairs={{0,4},{1,5},{2,6},{3,7},{4,8},{5,9},{6,10},{7,11},{8,12},{9,13},{1... | collective-permute-start | bytes 1769480 | tf_op jit(solution)/shard_map/ppermute | solution.py:29
  126.7 12.3 %collective-permute-start.16 = (bf16[128,2304]{1,0:T(8,128)(2,1)S(1)}, bf16[128,2304]{1,0:T(8,128)(2,1)S(1)}, u32[]{:S(2)}, u32[]{:S(2)}) collective-permute-start(bf16[128,2304]{1,0:T(8,128)(2,1)S(1)} %get-tuple-element.50), channel_id=1, source_target_pairs={{0,12},{1,13},{2,14},{3,15},{4,0},{5,1},{6,2},{7,3},{8,4},{9,5},{1... | collective-permute-start | bytes 1769480 | tf_op jit(solution)/shard_map/ppermute | solution.py:29
  140.5 11.2 %collective-permute-start.17 = (bf16[64,2304]{1,0:T(8,128)(2,1)S(1)}, bf16[64,2304]{1,0:T(8,128)(2,1)S(1)}, u32[]{:S(2)}, u32[]{:S(2)}) collective-permute-start(bf16[64,2304]{1,0:T(8,128)(2,1)S(1)} %get-tuple-element.52), channel_id=1, source_target_pairs={{0,1},{1,2},{2,3},{3,0},{4,5},{5,6},{6,7},{7,4},{8,9},{9,10},{10,1... | collective-permute-start | bytes 884744 | tf_op jit(solution)/shard_map/ppermute | solution.py:29
  141.2 10.5 %collective-permute-start.18 = (bf16[64,2304]{1,0:T(8,128)(2,1)S(1)}, bf16[64,2304]{1,0:T(8,128)(2,1)S(1)}, u32[]{:S(2)}, u32[]{:S(2)}) collective-permute-start(bf16[64,2304]{1,0:T(8,128)(2,1)S(1)} %get-tuple-element.53), channel_id=1, source_target_pairs={{0,2},{1,3},{2,0},{3,1},{4,6},{5,7},{6,4},{7,5},{8,10},{9,11},{10,... | collective-permute-start | bytes 884744 | tf_op jit(solution)/shard_map/ppermute | solution.py:29
  143.0 9.6 %collective-permute-start.19 = (bf16[64,2304]{1,0:T(8,128)(2,1)S(1)}, bf16[64,2304]{1,0:T(8,128)(2,1)S(1)}, u32[]{:S(2)}, u32[]{:S(2)}) collective-permute-start(bf16[64,2304]{1,0:T(8,128)(2,1)S(1)} %get-tuple-element.54), channel_id=1, source_target_pairs={{0,3},{1,0},{2,1},{3,2},{4,7},{5,4},{6,5},{7,6},{8,11},{9,8},{10,9... | collective-permute-start | bytes 884744 | tf_op jit(solution)/shard_map/ppermute | solution.py:29

commit v5 on v4

--- a/solution.py
+++ b/solution.py
@@ -50,30 +50,9 @@
     return lax.all_to_all(value, ("gx", "gy"), 0, 0, axis_index_groups=groups)
 
 
-def whole(shape):
-    return pl.BlockSpec(shape, lambda *_: (0,) * len(shape))
-
-
 IN_VMEM = pl.BlockSpec(memory_space=pltpu.VMEM)
 IN_SMEM = pl.BlockSpec(memory_space=pltpu.SMEM)
 IN_HBM = pl.BlockSpec(memory_space=pltpu.HBM)
-
-
-def kernel_call(body, grid, in_specs, out_specs, out_shape, scratch, flops, nbytes, name):
-    return pl.pallas_call(
-        body,
-        grid_spec=pltpu.PrefetchScalarGridSpec(
-            num_scalar_prefetch=1,
-            grid=grid,
-            in_specs=in_specs,
-            out_specs=out_specs,
-            scratch_shapes=scratch,
-        ),
-        out_shape=out_shape,
-        compiler_params=pltpu.CompilerParams(vmem_limit_bytes=VMEM_LIMIT),
-        cost_estimate=pl.CostEstimate(flops=flops, bytes_accessed=nbytes, transcendentals=0),
-        name=name,
-    )
 
 
 def one_step(body, in_specs, out_shape, scratch, flops, nbytes, name):
@@ -111,16 +90,14 @@
     lane = lax.broadcasted_iota(jnp.int32, (rows, 128), 1)
     cols = jnp.where(lane == 0, mean, jnp.where(lane == 1, squares, 0.0))
     cols = jnp.concatenate([cols, jnp.zeros((128 - rows, 128), F32)], axis=0)
-    tile = jnp.transpose(cols)[:8]
-    for k in range(8):
-        out[k] = tile
+    out[...] = jnp.transpose(cols)[:8]
 
 
 def row_statistics(tok):
     return one_step(
         row_statistics_body,
         [IN_VMEM],
-        jax.ShapeDtypeStruct((8, 8, 128), F32),
+        jax.ShapeDtypeStruct((8, 128), F32),
         [],
         6 * tok.size,
         tok.size * 2,
@@ -128,29 +105,57 @@
     )(tok)
 
 
-def normalise_body(tok, tiles, gain, out):
-    count = tok.shape[1]
-    held = [tiles[k] for k in range(8)]
-    mean = sum(h[0:1] for h in held) * (1.0 / 8)
-    squares = sum(h[1:2] + (h[0:1] - mean) * (h[0:1] - mean) * float(count) for h in held)
-    inverse = lax.rsqrt(squares * (1.0 / (8 * count)) + 1e-05)
-    cols = jnp.transpose(jnp.concatenate([mean, inverse, jnp.zeros((126, 128), F32)], axis=0))
-    value = tok[...].astype(F32)
-    value = ((value - cols[:64, 0:1]) * cols[:64, 1:2] * gain[...]).astype(BF)
+def join(tiles, count):
+    mean = sum(t[0:1] for t in tiles) * (1.0 / len(tiles))
+    squares = sum(t[1:2] + (t[0:1] - mean) * (t[0:1] - mean) * float(count) for t in tiles)
+    return mean, squares
+
+
+def chip_statistics(mine, other, count):
+    def body(a, b, out):
+        mean, squares = join([a[...], b[...]], count)
+        tile = jnp.concatenate([mean, squares, jnp.zeros((6, 128), F32)], axis=0)
+        for k in range(16):
+            out[k] = tile
+
+    return one_step(
+        body,
+        [IN_VMEM] * 2,
+        jax.ShapeDtypeStruct((16, 8, 128), F32),
+        [],
+        16 * 1024,
+        18 * 4096,
+        "chip_statistics",
+    )(mine, other)
+
+
+def normalise_body(place, b0, b1, b2, b3, tiles, gain, low, high):
+    me = jnp.where(place[3] == 0, place[0], place[1])
+    count = b0.shape[1]
     order = one_hot(64, 64, lambda o: ((o >> 2) & 1) * 32 + (o >> 3) * 4 + (o & 3))
-    out[...] = jnp.dot(order, value, preferred_element_type=F32).astype(BF)
-
-
-def normalise(tok, tiles, gain):
+    for k, block in enumerate((b0, b1, b2, b3)):
+        mean, squares = join([tiles[4 * z + ((me + k) & 3)] for z in range(4)], 2 * count)
+        inverse = lax.rsqrt(squares * (1.0 / (8 * count)) + 1e-05)
+        cols = jnp.transpose(
+            jnp.concatenate([mean, inverse, jnp.zeros((126, 128), F32)], axis=0)
+        )
+        value = block[...].astype(F32)
+        value = ((value - cols[:64, 0:1]) * cols[:64, 1:2] * gain[...]).astype(BF)
+        value = jnp.dot(order, value, preferred_element_type=F32).astype(BF)
+        (low, high)[k // 2][(k % 2) * 64 : (k % 2) * 64 + 64] = value
+
+
+def normalise(place, blocks, tiles, gain):
+    width = blocks[0].shape[1]
     return one_step(
         normalise_body,
-        [IN_VMEM] * 3,
-        jax.ShapeDtypeStruct(tok.shape, BF),
-        [],
-        tok.size * 6,
-        tok.size * 4,
+        [IN_SMEM] + [IN_VMEM] * 6,
+        [jax.ShapeDtypeStruct((128, width), BF)] * 2,
+        [],
+        256 * width * 6,
+        256 * width * 4,
         "normalise",
-    )(tok, tiles, gain)
+    )(place, *blocks, tiles, gain)
 
 
 def project_body(places, place, *refs):
@@ -395,33 +400,21 @@
 
 
 def group_sum_body(place, a, b0, b1, c0, c1, own, s1, s2, s3):
-    step = pl.program_id(0)
-    low = ((jnp.where(place[3] == 0, place[0], place[1]) + step) & 3) < 2
-    value = a[...].astype(F32)
-    value = value + jnp.where(low, b0[...], b1[...]).astype(F32)
-    value = value + jnp.where(low, c0[...], c1[...]).astype(F32)
-
-    @pl.when(step == 0)
-    def _():
-        own[...] = value
-
-    for d, ref in ((1, s1), (2, s2), (3, s3)):
-
-        @pl.when(step == d)
-        def _(ref=ref):
-            ref[...] = value.astype(BF)
+    me = jnp.where(place[3] == 0, place[0], place[1])
+    for d, out in enumerate((own, s1, s2, s3)):
+        at = (me + d) & 3
+        half = pl.ds(pl.multiple_of((at & 1) * 64, 64), 64)
+        value = a[pl.ds(pl.multiple_of(at * 64, 64), 64)].astype(F32)
+        value = value + jnp.where(at < 2, b0[half], b1[half]).astype(F32)
+        value = value + jnp.where(at < 2, c0[half], c1[half]).astype(F32)
+        out[...] = value.astype(out.dtype)
 
 
 def group_sum(place, own, halves):
     width = own.shape[-1]
-    mine = lambda d, p: (jnp.where(p[3] == 0, p[0], p[1]) + d) & 3
-    block = pl.BlockSpec((64, width), lambda d, p: (mine(d, p), 0))
-    half = pl.BlockSpec((64, width), lambda d, p: (mine(d, p) & 1, 0))
-    return kernel_call(
+    return one_step(
         group_sum_body,
-        (4,),
-        [block] + [half] * 4,
-        [whole((64, width))] * 4,
+        [IN_SMEM] + [IN_VMEM] * 5,
         [jax.ShapeDtypeStruct((64, width), F32)] + [jax.ShapeDtypeStruct((64, width), BF)] * 3,
         [],
         1024 * width,
@@ -455,12 +448,16 @@
 
 
 def gather_and_project(place, tok, gain, wq, wkv):
-    stat = lax.all_to_all(row_statistics(tok), "gx", 0, 0)
-    tok = normalise(tok, stat, gain)
-    b1, b2, b3 = [send(tok, first_axis(d)) for d in (-1, 2, 1)]
-    low = jnp.concatenate([tok, b1], axis=0)
-    high = jnp.concatenate([b2, b3], axis=0)
-    low, high = after(low, high)
+    stat = row_statistics(tok)
+    b1, b3, b2 = [send(tok, first_axis(d)) for d in (-1, 1, 2)]
+    blocks = [tok, b1, b2, b3]
+    stat = chip_statistics(stat, send(stat, other_core), tok.shape[1])
+    groups = [[2 * z * 16 + 4 * i + j for z in range(4) for j in range(4)] for i in range(4)]
+    groups += [
+        [(2 * z + 1) * 16 + 4 * j + i for z in range(4) for j in range(4)] for i in range(4)
+    ]
+    tiles = lax.all_to_all(stat, ("gx", "gy"), 0, 0, axis_index_groups=groups)
+    low, high = normalise(place, blocks, tiles, gain)
     minus_low = send(low, second_axis(1))
     plus_high = send(high, second_axis(-1))
     minus_high = send(high, second_axis(1))
@@ -512,7 +509,7 @@
     own, s1, s2, s3 = group_sum(
         place, own, [from_minus_a, from_minus_b, from_plus_a, from_plus_b]
     )
-    got = [send(s1, first_axis(1)), send(s2, first_axis(2)), send(s3, first_axis(-1))]
+    got = [send(s2, first_axis(2)), send(s1, first_axis(1)), send(s3, first_axis(-1))]
     return last_sum(place, own, got)
 
 

time: 155 us -> 152 us (0.981)
  waiting for transfers between devices: 47.7 us -> 42.5 us
  Pallas kernels: 27 us -> 28.6 us
    ppermute x20 -> x21, waiting for transfers between devices: 43 us -> 34.9 us  [send(): return lax.ppermute(value, ('gx', 'gy'), flat_perm(place))]
    all_to_all x1, waiting for transfers between devices: 4.73 us -> 7.59 us  [gather_and_project(): tiles = lax.all_to_all(stat, ('gx', 'gy'), 0, 0, axis_index_groups=groups)]
    pallas_call x3 -> x4, Pallas kernels: 2.86 us -> 4.28 us  [the longest x1 2.29 us: normalise(): one_step(normalise_body, [IN_SMEM] + [IN_VMEM] * 6, [jax.ShapeDtypeStruct...]
    ppermute x20 -> x21, starting transfers between devices: 26 us -> 27.2 us  [send(): return lax.ppermute(value, ('gx', 'gy'), flat_perm(place))]
  transfers between devices with their start and end apart: 21 -> 22, of which waited for: 15 -> 14; matrix products, arithmetic and copies ran while one was open for 1% -> 1% of each run, Pallas kernels for 7% -> 8%
where the time goes in v5:
time: 152 us
  waiting for transfers between devices  42.5 us (28%)
  blocking collectives  41.7 us (27%)
  starting transfers between devices  32.7 us (22%)
  Pallas kernels  28.6 us (19%)
  local copies, waits for them, and re-layouts  5.02 us (3%)
    all_to_all x2, blocking collectives, exchange(): return lax.all_to_all(value, ('gx', 'gy'), 0, 0, axis_index_groups=groups)  41.7 us
    ppermute x21, waiting for transfers between devices, send(): return lax.ppermute(value, ('gx', 'gy'), flat_perm(place))  34.9 us
    ppermute x21, starting transfers between devices, send(): return lax.ppermute(value, ('gx', 'gy'), flat_perm(place))  27.2 us
    pallas_call x3, Pallas kernels, project(): pl.pallas_call(functools.partial(project_body, places), in_specs=[IN_SMEM...  9.09 us
    all_to_all x1, waiting for transfers between devices, gather_and_project(): tiles = lax.all_to_all(stat, ('gx', 'gy'), 0, 0, axis_index_groups=groups)  7.59 us
    pallas_call x1, Pallas kernels, attend(): pl.pallas_call(attend_body, in_specs=[IN_SMEM, IN_VMEM, IN_HBM, IN_HBM],...  7.48 us
    all_to_all x1, starting transfers between devices, gather_and_project(): tiles = lax.all_to_all(stat, ('gx', 'gy'), 0, 0, axis_index_groups=groups)  5.45 us
    unnamed x12, local copies, waits for them, and re-layouts  3.96 us
  transfers between devices with their start and end apart: 22, of which 14 were waited for; matrix products, arithmetic and copies ran while one was open for 1% of the time, Pallas kernels for 8%

profile of v5, /device:TPU:24, one launch (start us, length us, event | category | flops | bytes accessed | tf_op | source)
XLA Modules:
  0.0 151.9 jit_solution(207092378845995754)
XLA Ops:
  0.0 1.5 collective-permute-start.2
  1.5 2.7 %collective-permute-start.1 = (bf16[64,2304]{1,0:T(8,128)(2,1)}, bf16[64,2304]{1,0:T(8,128)(2,1)S(1)}, u32[]{:S(2)}, u32[]{:S(2)}) collective-permute-start(bf16[64,2304]{1,0:T(8,128)(2,1)} %bitcast.13), channel_id=1, source_target_pairs={{0,2},{1,3},{2,0},{3,1},{4,6},{5,7},{6,4},{7,5},{8,10},{9,11},{10,... | collective-permute-start | bytes 884744 | tf_op jit(solution)/shard_map/ppermute | solution.py:29
  4.2 1.4 collective-permute-start
  5.7 1.0 copy-done.4
  6.7 0.3 row_statistics.1.a
  7.0 0.0 collective-permute-start.3
  7.0 0.7 broadcast_in_dim.3.gain
  7.7 0.4 collective-permute-done.3.b
  8.1 0.6 chip_statistics.1
  8.8 5.4 %all-to-all-start = ((f32[16,8,128]{2,1,0:T(8,128)}), f32[16,8,128]{2,1,0:T(8,128)S(1)}, u32[]{:S(2)}, u32[]{:S(2)}) async-start(f32[16,8,128]{2,1,0:T(8,128)} %chip_statistics.1), calls=%async_computation | async-start | bytes 131072 | tf_op jit(solution)/shard_map/all_to_all | solution.py:459
  14.2 0.1 pad_add_fusion.place
  14.3 7.6 %all-to-all-done.tiles = f32[16,8,128]{2,1,0:T(8,128)S(1)} async-done(((f32[16,8,128]{2,1,0:T(8,128)}), f32[16,8,128]{2,1,0:T(8,128)S(1)}, u32[]{:S(2)}, u32[]{:S(2)}) %all-to-all-start) | async-done | bytes 65568 | tf_op jit(solution)/shard_map/all_to_all | solution.py:459
  21.9 0.0 collective-permute-done.2.b3
  21.9 0.0 collective-permute-done.1.b2
  21.9 0.0 collective-permute-done.b1
  21.9 0.0 copy-start.5
  21.9 1.0 copy-done.5
  22.9 2.3 %normalise.1 = (bf16[128,2304]{1,0:T(8,128)(2,1)}, bf16[128,2304]{1,0:T(8,128)(2,1)}) custom-call(s32[4]{0:T(128)S(1)} %pad_add_fusion.place, bf16[64,2304]{1,0:T(8,128)(2,1)S(1)} %bitcast.16, bf16[64,2304]{1,0:T(8,128)(2,1)S(1)} %collective-permute-done.b1, bf16[64,2304]{1,0:T(8,128)(2,1)S(1)} %collective-permute-done.1.b2, ...), custom_call_target="tpu_custom_call" | custom-call | flops 3538944 | bytes 2359296 | tf_op jit(solution)/shard_map/normalise/pallas_call | solution.py:150
  25.2 1.5 collective-permute-start.4
  26.7 0.5 collective-permute-start.6
  27.2 0.7 collective-permute-start.8
  27.9 2.5 %collective-permute-start.9 = (bf16[128,2304]{1,0:T(8,128)(2,1)}, bf16[128,2304]{1,0:T(8,128)(2,1)S(1)}, u32[]{:S(2)}, u32[]{:S(2)}) collective-permute-start(bf16[128,2304]{1,0:T(8,128)(2,1)} %get-tuple-element.31.refs_1_), channel_id=1, source_target_pairs={{0,4},{1,5},{2,6},{3,7},{4,8},{5,9},{6,10},{7,11},{8,12},{9,13},{1... | collective-permute-start | bytes 1769480 | tf_op jit(solution)/shard_map/ppermute | solution.py:29
  30.4 0.2 constant_dynamic-slice_fusion
  30.7 0.1 pad.4.refs_3_.refs_5_
  30.8 0.0 copy-start.1
  30.8 2.0 %copy-done.1 = bf16[2304,768]{1,0:T(8,128)(2,1)S(1)} copy-done((bf16[2304,768]{1,0:T(8,128)(2,1)S(1)}, bf16[2304,768]{1,0:T(8,128)(2,1)}, u32[]{:S(2)}) %copy-start.1) | copy-done | bytes 3538968
  32.8 3.1 %project.3 = (f32[8,64,896]{2,1,0:T(8,128)S(1)}, f32[8,64,896]{2,1,0:T(8,128)S(1)}) custom-call(s32[4]{0:T(128)S(1)} %pad_add_fusion.place, bf16[128,2304]{1,0:T(8,128)(2,1)} %get-tuple-element.30.refs_0_, bf16[128,2304]{1,0:T(8,128)(2,1)} %get-tuple-element.31.refs_1_, bf16[2304,768]{1,0:T(8,128)(2,1)S(1)} %copy-done.1, ...), custom_call_target="tpu_custom_call" | custom-call | flops 1056964608 | bytes 6225920 | tf_op jit(solution)/shard_map/project/pallas_call | solution.py:191
  35.9 0.0 collective-permute-done.4.refs_2_
  35.9 2.1 %collective-permute-done.6.refs_1_ = bf16[128,2304]{1,0:T(8,128)(2,1)S(1)} collective-permute-done((bf16[128,2304]{1,0:T(8,128)(2,1)}, bf16[128,2304]{1,0:T(8,128)(2,1)S(1)}, u32[]{:S(2)}, u32[]{:S(2)}) %collective-permute-start.6) | collective-permute-done | bytes 589856 | tf_op jit(solution)/shard_map/ppermute | solution.py:29
  38.0 0.0 collective-permute-start.7
  38.0 3.2 %collective-permute-start.5 = (bf16[128,2304]{1,0:T(8,128)(2,1)S(1)}, bf16[128,2304]{1,0:T(8,128)(2,1)S(1)}, u32[]{:S(2)}, u32[]{:S(2)}) collective-permute-start(bf16[128,2304]{1,0:T(8,128)(2,1)S(1)} %collective-permute-done.4.refs_2_), channel_id=1, source_target_pairs={{0,4},{1,5},{2,6},{3,7},{4,8},{5,9},{6,10},{7,11},{8,12},{9,13},{1... | collective-permute-start | bytes 1769480 | tf_op jit(solution)/shard_map/ppermute | solution.py:29
  41.2 3.1 %collective-permute-done.8.refs_0_ = bf16[128,2304]{1,0:T(8,128)(2,1)S(1)} collective-permute-done((bf16[128,2304]{1,0:T(8,128)(2,1)}, bf16[128,2304]{1,0:T(8,128)(2,1)S(1)}, u32[]{:S(2)}, u32[]{:S(2)}) %collective-permute-start.8) | collective-permute-done | bytes 589856 | tf_op jit(solution)/shard_map/ppermute | solution.py:29
  44.3 3.8 %project.4 = (f32[8,64,896]{2,1,0:T(8,128)S(1)}, f32[8,64,896]{2,1,0:T(8,128)S(1)}) custom-call(s32[4]{0:T(128)S(1)} %pad_add_fusion.place, bf16[128,2304]{1,0:T(8,128)(2,1)S(1)} %collective-permute-done.8.refs_0_, bf16[128,2304]{1,0:T(8,128)(2,1)S(1)} %collective-permute-done.6.refs_1_, ...), custom_call_target="tpu_custom_call", output_to_operand_aliasing={{0}: (7, {}), {1}: (8, {})} | custom-call | flops 2113929216 | bytes 8323072 | tf_op jit(solution)/shard_map/project/pallas_call | solution.py:191
  48.2 2.5 %collective-permute-done.7.refs_1_ = bf16[128,2304]{1,0:T(8,128)(2,1)S(1)} collective-permute-done((bf16[128,2304]{1,0:T(8,128)(2,1)S(1)}, bf16[128,2304]{1,0:T(8,128)(2,1)S(1)}, u32[]{:S(2)}, u32[]{:S(2)}) %collective-permute-start.7) | collective-permute-done | bytes 589856 | tf_op jit(solution)/shard_map/ppermute | solution.py:29
  50.6 2.2 %project.5 = (f32[8,64,896]{2,1,0:T(8,128)S(1)}, f32[8,64,896]{2,1,0:T(8,128)S(1)}) custom-call(s32[4]{0:T(128)S(1)} %pad_add_fusion.place, bf16[128,2304]{1,0:T(8,128)(2,1)S(1)} %collective-permute-done.5.refs_0_, bf16[128,2304]{1,0:T(8,128)(2,1)S(1)} %collective-permute-done.7.refs_1_, ...), custom_call_target="tpu_custom_call", output_to_operand_aliasing={{0}: (5, {}), {1}: (6, {})} | custom-call | flops 1056964608 | bytes 6225920 | tf_op jit(solution)/shard_map/project/pallas_call | solution.py:191
  52.8 0.3 collective-permute-start.10
  53.1 3.8 %collective-permute-done.10 = f32[8,64,896]{2,1,0:T(8,128)S(1)} collective-permute-done((f32[8,64,896]{2,1,0:T(8,128)S(1)}, f32[8,64,896]{2,1,0:T(8,128)S(1)}, u32[]{:S(2)}, u32[]{:S(2)}) %collective-permute-start.10) | collective-permute-done | bytes 1835040 | tf_op jit(solution)/shard_map/ppermute | solution.py:29
  56.9 0.3 multiply_convert_fusion
  57.2 21.7 %all_to_all.15 = f16[64,8,896]{2,1,0:T(8,128)(2,1)S(1)} all-to-all(f16[64,8,896]{2,1,0:T(8,128)(2,1)S(1)} %bitcast.18), channel_id=1, replica_groups={{0,1,2,3,4,5,6,7,8,9,10,11,12,13,14,15,32,33,34,35,36,37,38,39,40,41,42..., dimensions={0} | all-to-all | bytes 1835008 | tf_op jit(solution)/shard_map/all_to_all | solution.py:50
  78.8 0.1 convert_reduce_fusion
  79.0 0.7 multiply_convert_fusion.1.x
  79.7 7.5 %attend.1 = bf16[4,16,8,768]{3,2,1,0:T(8,128)(2,1)} custom-call(s32[4]{0:T(128)} %lens.1, bf16[16,8,896]{2,1,0:T(8,128)(2,1)} %multiply_convert_fusion.1.x, bf16[4,2048,256]{2,1,0:T(8,128)(2,1)} %keys_hbm.1, bf16[4,2048,256]{2,1,0:T(8,128)(2,1)} %values_hbm.1), custom_call_target="tpu_custom_call" | custom-call | flops 805306368 | bytes 8388608 | tf_op jit(solution)/shard_map/attend/pallas_call | solution.py:293
  87.2 20.0 %all_to_all.16 = bf16[64,8,768]{2,1,0:T(8,128)(2,1)S(1)} all-to-all(bf16[64,8,768]{2,1,0:T(8,128)(2,1)} %bitcast.19), channel_id=1, replica_groups={{0,1,2,3,4,5,6,7,8,9,10,11,12,13,14,15,32,33,34,35,36,37,38,39,40,41,42..., dimensions={0} | all-to-all | bytes 1572864 | tf_op jit(solution)/shard_map/all_to_all | solution.py:50
  107.2 2.3 %collective-permute-done.11.cross = bf16[4,16,8,768]{3,2,1,0:T(8,128)(2,1)S(1)} collective-permute-done((bf16[4,16,8,768]{3,2,1,0:T(8,128)(2,1)S(1)}, bf16[4,16,8,768]{3,2,1,0:T(8,128)(2,1)S(1)}, u32[]{:S(2)}, u32[]{:S(2)}) %collective-permute-start.11) | collective-permute-done | bytes 786464 | tf_op jit(solution)/shard_map/ppermute | solution.py:29
  109.5 1.7 %output_far.1 = (bf16[16,64,768]{2,1,0:T(8,128)(2,1)S(1)}, bf16[128,2304]{1,0:T(8,128)(2,1)S(1)}, bf16[128,2304]{1,0:T(8,128)(2,1)S(1)}) custom-call(s32[4]{0:T(128)S(1)} %pad_add_fusion.place, bf16[4,16,8,768]{3,2,1,0:T(8,128)(2,1)S(1)} %bitcast.11, bf16[4,16,8,768]{3,2,1,0:T(8,128)(2,1)S(1)} %collective-permute-done.11.cross, bf16[768,2304]{1,0:T(8,128)(2,1)S(1)} %copy-done.3), custom_call_target="tpu_custom_call" | custom-call | flops 905969664 | bytes 7864320 | tf_op jit(solution)/shard_map/output_far/pallas_call | solution.py:339
  111.2 2.9 %collective-permute-start.12 = (bf16[128,2304]{1,0:T(8,128)(2,1)S(1)}, bf16[128,2304]{1,0:T(8,128)(2,1)S(1)}, u32[]{:S(2)}, u32[]{:S(2)}) collective-permute-start(bf16[128,2304]{1,0:T(8,128)(2,1)S(1)} %get-tuple-element.44), channel_id=1, source_target_pairs={{0,4},{1,5},{2,6},{3,7},{4,8},{5,9},{6,10},{7,11},{8,12},{9,13},{1... | collective-permute-start | bytes 1769480 | tf_op jit(solution)/shard_map/ppermute | solution.py:29
  114.1 2.6 %output_near.1 = (bf16[128,2304]{1,0:T(8,128)(2,1)S(1)}, bf16[128,2304]{1,0:T(8,128)(2,1)S(1)}, bf16[128,2304]{1,0:T(8,128)(2,1)S(1)}, bf16[128,2304]{1,0:T(8,128)(2,1)S(1)}) custom-call(s32[4]{0:T(128)S(1)} %pad_add_fusion.place, bf16[16,64,768]{2,1,0:T(8,128)(2,1)S(1)} %get-tuple-element.42.left, bf16[768,2304]{1,0:T(8,128)(2,1)S(1)} %copy-done.3), custom_call_target="tpu_custom_call" | custom-call | flops 1811939328 | bytes 7471104 | tf_op jit(solution)/shard_map/output_near/pallas_call | solution.py:357
  116.6 3.3 %collective-permute-start.15 = (bf16[128,2304]{1,0:T(8,128)(2,1)S(1)}, bf16[128,2304]{1,0:T(8,128)(2,1)S(1)}, u32[]{:S(2)}, u32[]{:S(2)}) collective-permute-start(bf16[128,2304]{1,0:T(8,128)(2,1)S(1)} %get-tuple-element.48), channel_id=1, source_target_pairs={{0,4},{1,5},{2,6},{3,7},{4,8},{5,9},{6,10},{7,11},{8,12},{9,13},{1... | collective-permute-start | bytes 1769480 | tf_op jit(solution)/shard_map/ppermute | solution.py:29
  119.9 1.5 %collective-permute-done.12.a1 = bf16[128,2304]{1,0:T(8,128)(2,1)S(1)} collective-permute-done((bf16[128,2304]{1,0:T(8,128)(2,1)S(1)}, bf16[128,2304]{1,0:T(8,128)(2,1)S(1)}, u32[]{:S(2)}, u32[]{:S(2)}) %collective-permute-start.12) | collective-permute-done | bytes 589856 | tf_op jit(solution)/shard_map/ppermute | solution.py:29
  121.5 3.7 %collective-permute-done.13.b1 = bf16[128,2304]{1,0:T(8,128)(2,1)S(1)} collective-permute-done((bf16[128,2304]{1,0:T(8,128)(2,1)S(1)}, bf16[128,2304]{1,0:T(8,128)(2,1)S(1)}, u32[]{:S(2)}, u32[]{:S(2)}) %collective-permute-start.13) | collective-permute-done | bytes 589856 | tf_op jit(solution)/shard_map/ppermute | solution.py:29
  125.2 0.3 pair_add.1
  125.4 0.1 collective-permute-start.14
  125.5 2.0 %collective-permute-start.17 = (bf16[128,2304]{1,0:T(8,128)(2,1)S(1)}, bf16[128,2304]{1,0:T(8,128)(2,1)S(1)}, u32[]{:S(2)}, u32[]{:S(2)}) collective-permute-start(bf16[128,2304]{1,0:T(8,128)(2,1)S(1)} %get-tuple-element.50), channel_id=1, source_target_pairs={{0,12},{1,13},{2,14},{3,15},{4,0},{5,1},{6,2},{7,3},{8,4},{9,5},{1... | collective-permute-start | bytes 1769480 | tf_op jit(solution)/shard_map/ppermute | solution.py:29
  127.5 1.6 %output_own.1.a = bf16[256,2304]{1,0:T(8,128)(2,1)S(1)} custom-call(s32[4]{0:T(128)S(1)} %pad_add_fusion.place, bf16[16,64,768]{2,1,0:T(8,128)(2,1)S(1)} %get-tuple-element.42.left, bf16[768,2304]{1,0:T(8,128)(2,1)S(1)} %copy-done.3), custom_call_target="tpu_custom_call" | custom-call | flops 905969664 | bytes 6291456 | tf_op jit(solution)/shard_map/output_own/pallas_call | solution.py:374
  129.2 2.3 %collective-permute-done.16.c0 = bf16[128,2304]{1,0:T(8,128)(2,1)S(1)} collective-permute-done((bf16[128,2304]{1,0:T(8,128)(2,1)S(1)}, bf16[128,2304]{1,0:T(8,128)(2,1)S(1)}, u32[]{:S(2)}, u32[]{:S(2)}) %collective-permute-start.16) | collective-permute-done | bytes 589856 | tf_op jit(solution)/shard_map/ppermute | solution.py:29
  131.5 3.9 %collective-permute-done.14.b0 = bf16[128,2304]{1,0:T(8,128)(2,1)S(1)} collective-permute-done((bf16[128,2304]{1,0:T(8,128)(2,1)S(1)}, bf16[128,2304]{1,0:T(8,128)(2,1)S(1)}, u32[]{:S(2)}, u32[]{:S(2)}) %collective-permute-start.14) | collective-permute-done | bytes 589856 | tf_op jit(solution)/shard_map/ppermute | solution.py:29
  135.4 2.4 %collective-permute-done.17.c1 = bf16[128,2304]{1,0:T(8,128)(2,1)S(1)} collective-permute-done((bf16[128,2304]{1,0:T(8,128)(2,1)S(1)}, bf16[128,2304]{1,0:T(8,128)(2,1)S(1)}, u32[]{:S(2)}, u32[]{:S(2)}) %collective-permute-start.17) | collective-permute-done | bytes 589856 | tf_op jit(solution)/shard_map/ppermute | solution.py:29
  137.8 1.0 group_sum.1
  138.8 1.3 collective-permute-start.18
  140.1 0.5 collective-permute-start.19
  140.7 2.7 %collective-permute-start.20 = (bf16[64,2304]{1,0:T(8,128)(2,1)S(1)}, bf16[64,2304]{1,0:T(8,128)(2,1)S(1)}, u32[]{:S(2)}, u32[]{:S(2)}) collective-permute-start(bf16[64,2304]{1,0:T(8,128)(2,1)S(1)} %get-tuple-element.54), channel_id=1, source_target_pairs={{0,3},{1,0},{2,1},{3,2},{4,7},{5,4},{6,5},{7,6},{8,11},{9,8},{10,9... | collective-permute-start | bytes 884744 | tf_op jit(solution)/shard_map/ppermute | solution.py:29
  143.4 3.9 %collective-permute-done.18.r1 = bf16[64,2304]{1,0:T(8,128)(2,1)S(1)} collective-permute-done((bf16[64,2304]{1,0:T(8,128)(2,1)S(1)}, bf16[64,2304]{1,0:T(8,128)(2,1)S(1)}, u32[]{:S(2)}, u32[]{:S(2)}) %collective-permute-start.18) | collective-permute-done | bytes 294944 | tf_op jit(solution)/shard_map/ppermute | solution.py:29
  147.3 3.1 %collective-permute-done.19.r2 = bf16[64,2304]{1,0:T(8,128)(2,1)S(1)} collective-permute-done((bf16[64,2304]{1,0:T(8,128)(2,1)S(1)}, bf16[64,2304]{1,0:T(8,128)(2,1)S(1)}, u32[]{:S(2)}, u32[]{:S(2)}) %collective-permute-start.19) | collective-permute-done | bytes 294944 | tf_op jit(solution)/shard_map/ppermute | solution.py:29
  150.3 1.6 %last_sum.1 = bf16[2,32,2304]{2,1,0:T(8,128)(2,1)} custom-call(s32[4]{0:T(128)S(1)} %pad_add_fusion.place, f32[64,2304]{1,0:T(8,128)S(1)} %get-tuple-element.51.own, bf16[64,2304]{1,0:T(8,128)(2,1)S(1)} %collective-permute-done.18.r1, bf16[64,2304]{1,0:T(8,128)(2,1)S(1)} %collective-permute-done.19.r2, bf16[64,2304]{1,0:T(8,128)(2,1)S(1)} %collective-permute-done.20.r3), custom_call_target="tpu_custom_call" | custom-call | flops 589824 | bytes 1769472 | tf_op jit(solution)/shard_map/last_sum/pallas_call | solution.py:435
  (14 shorter events, 0.0 us)
Async XLA Ops:
  0.0 30.4 %copy-start = (bf16[2304,512]{1,0:T(8,128)(2,1)S(1)}, bf16[2304,512]{1,0:T(8,128)(2,1)}, u32[]{:S(2)}) copy-start(bf16[2304,512]{1,0:T(8,128)(2,1)} %param.11) | copy-start | bytes 7077892
  0.0 21.9 %collective-permute-start.2 = (bf16[64,2304]{1,0:T(8,128)(2,1)}, bf16[64,2304]{1,0:T(8,128)(2,1)S(1)}, u32[]{:S(2)}, u32[]{:S(2)}) collective-permute-start(bf16[64,2304]{1,0:T(8,128)(2,1)} %bitcast.12), channel_id=1, source_target_pairs={{0,1},{1,2},{2,3},{3,0},{4,5},{5,6},{6,7},{7,4},{8,9},{9,10},{10,1... | collective-permute-start | bytes 884744 | tf_op jit(solution)/shard_map/ppermute | solution.py:29
  1.5 20.4 %collective-permute-start.1 = (bf16[64,2304]{1,0:T(8,128)(2,1)}, bf16[64,2304]{1,0:T(8,128)(2,1)S(1)}, u32[]{:S(2)}, u32[]{:S(2)}) collective-permute-start(bf16[64,2304]{1,0:T(8,128)(2,1)} %bitcast.13), channel_id=1, source_target_pairs={{0,2},{1,3},{2,0},{3,1},{4,6},{5,7},{6,4},{7,5},{8,10},{9,11},{10,... | collective-permute-start | bytes 884744 | tf_op jit(solution)/shard_map/ppermute | solution.py:29
  4.2 17.7 %collective-permute-start = (bf16[64,2304]{1,0:T(8,128)(2,1)}, bf16[64,2304]{1,0:T(8,128)(2,1)S(1)}, u32[]{:S(2)}, u32[]{:S(2)}) collective-permute-start(bf16[64,2304]{1,0:T(8,128)(2,1)} %bitcast.14), channel_id=1, source_target_pairs={{0,3},{1,0},{2,1},{3,2},{4,7},{5,4},{6,5},{7,6},{8,11},{9,8},{10,9... | collective-permute-start | bytes 884744 | tf_op jit(solution)/shard_map/ppermute | solution.py:29
  5.7 1.0 copy-start.4
  7.0 1.2 collective-permute-start.3
  8.8 13.1 %all-to-all-start = ((f32[16,8,128]{2,1,0:T(8,128)}), f32[16,8,128]{2,1,0:T(8,128)S(1)}, u32[]{:S(2)}, u32[]{:S(2)}) async-start(f32[16,8,128]{2,1,0:T(8,128)} %chip_statistics.1), calls=%async_computation | async-start | bytes 131072 | tf_op jit(solution)/shard_map/all_to_all | solution.py:459
  21.9 1.0 copy-start.5
  25.2 10.7 %collective-permute-start.4 = (bf16[128,2304]{1,0:T(8,128)(2,1)}, bf16[128,2304]{1,0:T(8,128)(2,1)S(1)}, u32[]{:S(2)}, u32[]{:S(2)}) collective-permute-start(bf16[128,2304]{1,0:T(8,128)(2,1)} %get-tuple-element.30.refs_0_), channel_id=1, source_target_pairs={{0,4},{1,5},{2,6},{3,7},{4,8},{5,9},{6,10},{7,11},{8,12},{9,13},{1... | collective-permute-start | bytes 1769480 | tf_op jit(solution)/shard_map/ppermute | solution.py:29
  26.7 11.3 %collective-permute-start.6 = (bf16[128,2304]{1,0:T(8,128)(2,1)}, bf16[128,2304]{1,0:T(8,128)(2,1)S(1)}, u32[]{:S(2)}, u32[]{:S(2)}) collective-permute-start(bf16[128,2304]{1,0:T(8,128)(2,1)} %get-tuple-element.31.refs_1_), channel_id=1, source_target_pairs={{0,12},{1,13},{2,14},{3,15},{4,0},{5,1},{6,2},{7,3},{8,4},{9,5},{1... | collective-permute-start | bytes 1769480 | tf_op jit(solution)/shard_map/ppermute | solution.py:29
  27.2 17.1 %collective-permute-start.8 = (bf16[128,2304]{1,0:T(8,128)(2,1)}, bf16[128,2304]{1,0:T(8,128)(2,1)S(1)}, u32[]{:S(2)}, u32[]{:S(2)}) collective-permute-start(bf16[128,2304]{1,0:T(8,128)(2,1)} %get-tuple-element.30.refs_0_), channel_id=1, source_target_pairs={{0,12},{1,13},{2,14},{3,15},{4,0},{5,1},{6,2},{7,3},{8,4},{9,5},{1... | collective-permute-start | bytes 1769480 | tf_op jit(solution)/shard_map/ppermute | solution.py:29
  27.9 16.4 %collective-permute-start.9 = (bf16[128,2304]{1,0:T(8,128)(2,1)}, bf16[128,2304]{1,0:T(8,128)(2,1)S(1)}, u32[]{:S(2)}, u32[]{:S(2)}) collective-permute-start(bf16[128,2304]{1,0:T(8,128)(2,1)} %get-tuple-element.31.refs_1_), channel_id=1, source_target_pairs={{0,4},{1,5},{2,6},{3,7},{4,8},{5,9},{6,10},{7,11},{8,12},{9,13},{1... | collective-permute-start | bytes 1769480 | tf_op jit(solution)/shard_map/ppermute | solution.py:29
  30.8 2.0 %copy-start.1 = (bf16[2304,768]{1,0:T(8,128)(2,1)S(1)}, bf16[2304,768]{1,0:T(8,128)(2,1)}, u32[]{:S(2)}) copy-start(bf16[2304,768]{1,0:T(8,128)(2,1)} %refs_2_.3) | copy-start | bytes 10616836
  32.8 11.5 %copy-start.2 = (bf16[2304,768]{1,0:T(8,128)(2,1)S(1)}, bf16[2304,768]{1,0:T(8,128)(2,1)}, u32[]{:S(2)}) copy-start(bf16[2304,768]{1,0:T(8,128)(2,1)} %refs_2_.3) | copy-start | bytes 10616836
  38.0 12.6 %collective-permute-start.7 = (bf16[128,2304]{1,0:T(8,128)(2,1)S(1)}, bf16[128,2304]{1,0:T(8,128)(2,1)S(1)}, u32[]{:S(2)}, u32[]{:S(2)}) collective-permute-start(bf16[128,2304]{1,0:T(8,128)(2,1)S(1)} %collective-permute-done.6.refs_1_), channel_id=1, source_target_pairs={{0,12},{1,13},{2,14},{3,15},{4,0},{5,1},{6,2},{7,3},{8,4},{9,5},{1... | collective-permute-start | bytes 1769480 | tf_op jit(solution)/shard_map/ppermute | solution.py:29
  38.0 12.6 %collective-permute-start.5 = (bf16[128,2304]{1,0:T(8,128)(2,1)S(1)}, bf16[128,2304]{1,0:T(8,128)(2,1)S(1)}, u32[]{:S(2)}, u32[]{:S(2)}) collective-permute-start(bf16[128,2304]{1,0:T(8,128)(2,1)S(1)} %collective-permute-done.4.refs_2_), channel_id=1, source_target_pairs={{0,4},{1,5},{2,6},{3,7},{4,8},{5,9},{6,10},{7,11},{8,12},{9,13},{1... | collective-permute-start | bytes 1769480 | tf_op jit(solution)/shard_map/ppermute | solution.py:29
  52.8 4.0 %collective-permute-start.10 = (f32[8,64,896]{2,1,0:T(8,128)S(1)}, f32[8,64,896]{2,1,0:T(8,128)S(1)}, u32[]{:S(2)}, u32[]{:S(2)}) collective-permute-start(f32[8,64,896]{2,1,0:T(8,128)S(1)} %get-tuple-element.41), channel_id=1, source_target_pairs={{0,16},{1,17},{2,18},{3,19},{4,20},{5,21},{6,22},{7,23},{8,24},{9,... | collective-permute-start | bytes 5505032 | tf_op jit(solution)/shard_map/ppermute | solution.py:29
  79.7 29.8 %copy-start.3 = (bf16[768,2304]{1,0:T(8,128)(2,1)S(1)}, bf16[768,2304]{1,0:T(8,128)(2,1)}, u32[]{:S(2)}) copy-start(bf16[768,2304]{1,0:T(8,128)(2,1)} %w_out.5) | copy-start | bytes 10616836
  107.2 2.3 %collective-permute-start.11 = (bf16[4,16,8,768]{3,2,1,0:T(8,128)(2,1)S(1)}, bf16[4,16,8,768]{3,2,1,0:T(8,128)(2,1)S(1)}, u32[]{:S(2)}, u32[]{:S(2)}) collective-permute-start(bf16[4,16,8,768]{3,2,1,0:T(8,128)(2,1)S(1)} %bitcast.10), channel_id=1, source_target_pairs={{0,16},{1,17},{2,18},{3,19},{4,20},{5,21},{6,22},{7,23},{8,24},{9,... | collective-permute-start | bytes 2359304 | tf_op jit(solution)/shard_map/ppermute | solution.py:29
  111.2 10.3 %collective-permute-start.12 = (bf16[128,2304]{1,0:T(8,128)(2,1)S(1)}, bf16[128,2304]{1,0:T(8,128)(2,1)S(1)}, u32[]{:S(2)}, u32[]{:S(2)}) collective-permute-start(bf16[128,2304]{1,0:T(8,128)(2,1)S(1)} %get-tuple-element.44), channel_id=1, source_target_pairs={{0,4},{1,5},{2,6},{3,7},{4,8},{5,9},{6,10},{7,11},{8,12},{9,13},{1... | collective-permute-start | bytes 1769480 | tf_op jit(solution)/shard_map/ppermute | solution.py:29
  114.1 11.1 %collective-permute-start.13 = (bf16[128,2304]{1,0:T(8,128)(2,1)S(1)}, bf16[128,2304]{1,0:T(8,128)(2,1)S(1)}, u32[]{:S(2)}, u32[]{:S(2)}) collective-permute-start(bf16[128,2304]{1,0:T(8,128)(2,1)S(1)} %get-tuple-element.46), channel_id=1, source_target_pairs={{0,12},{1,13},{2,14},{3,15},{4,0},{5,1},{6,2},{7,3},{8,4},{9,5},{1... | collective-permute-start | bytes 1769480 | tf_op jit(solution)/shard_map/ppermute | solution.py:29
  116.6 12.5 %collective-permute-start.15 = (bf16[128,2304]{1,0:T(8,128)(2,1)S(1)}, bf16[128,2304]{1,0:T(8,128)(2,1)S(1)}, u32[]{:S(2)}, u32[]{:S(2)}) collective-permute-start(bf16[128,2304]{1,0:T(8,128)(2,1)S(1)} %get-tuple-element.48), channel_id=1, source_target_pairs={{0,4},{1,5},{2,6},{3,7},{4,8},{5,9},{6,10},{7,11},{8,12},{9,13},{1... | collective-permute-start | bytes 1769480 | tf_op jit(solution)/shard_map/ppermute | solution.py:29
  119.9 11.5 %collective-permute-start.16 = (bf16[128,2304]{1,0:T(8,128)(2,1)S(1)}, bf16[128,2304]{1,0:T(8,128)(2,1)S(1)}, u32[]{:S(2)}, u32[]{:S(2)}) collective-permute-start(bf16[128,2304]{1,0:T(8,128)(2,1)S(1)} %get-tuple-element.49), channel_id=1, source_target_pairs={{0,12},{1,13},{2,14},{3,15},{4,0},{5,1},{6,2},{7,3},{8,4},{9,5},{1... | collective-permute-start | bytes 1769480 | tf_op jit(solution)/shard_map/ppermute | solution.py:29
  125.4 10.0 %collective-permute-start.14 = (bf16[128,2304]{1,0:T(8,128)(2,1)S(1)}, bf16[128,2304]{1,0:T(8,128)(2,1)S(1)}, u32[]{:S(2)}, u32[]{:S(2)}) collective-permute-start(bf16[128,2304]{1,0:T(8,128)(2,1)S(1)} %get-tuple-element.47), channel_id=1, source_target_pairs={{0,4},{1,5},{2,6},{3,7},{4,8},{5,9},{6,10},{7,11},{8,12},{9,13},{1... | collective-permute-start | bytes 1769480 | tf_op jit(solution)/shard_map/ppermute | solution.py:29
  125.5 12.3 %collective-permute-start.17 = (bf16[128,2304]{1,0:T(8,128)(2,1)S(1)}, bf16[128,2304]{1,0:T(8,128)(2,1)S(1)}, u32[]{:S(2)}, u32[]{:S(2)}) collective-permute-start(bf16[128,2304]{1,0:T(8,128)(2,1)S(1)} %get-tuple-element.50), channel_id=1, source_target_pairs={{0,12},{1,13},{2,14},{3,15},{4,0},{5,1},{6,2},{7,3},{8,4},{9,5},{1... | collective-permute-start | bytes 1769480 | tf_op jit(solution)/shard_map/ppermute | solution.py:29
  138.8 8.4 %collective-permute-start.18 = (bf16[64,2304]{1,0:T(8,128)(2,1)S(1)}, bf16[64,2304]{1,0:T(8,128)(2,1)S(1)}, u32[]{:S(2)}, u32[]{:S(2)}) collective-permute-start(bf16[64,2304]{1,0:T(8,128)(2,1)S(1)} %get-tuple-element.52), channel_id=1, source_target_pairs={{0,2},{1,3},{2,0},{3,1},{4,6},{5,7},{6,4},{7,5},{8,10},{9,11},{10,... | collective-permute-start | bytes 884744 | tf_op jit(solution)/shard_map/ppermute | solution.py:29
  140.1 10.2 %collective-permute-start.19 = (bf16[64,2304]{1,0:T(8,128)(2,1)S(1)}, bf16[64,2304]{1,0:T(8,128)(2,1)S(1)}, u32[]{:S(2)}, u32[]{:S(2)}) collective-permute-start(bf16[64,2304]{1,0:T(8,128)(2,1)S(1)} %get-tuple-element.53), channel_id=1, source_target_pairs={{0,1},{1,2},{2,3},{3,0},{4,5},{5,6},{6,7},{7,4},{8,9},{9,10},{10,1... | collective-permute-start | bytes 884744 | tf_op jit(solution)/shard_map/ppermute | solution.py:29
  140.7 9.6 %collective-permute-start.20 = (bf16[64,2304]{1,0:T(8,128)(2,1)S(1)}, bf16[64,2304]{1,0:T(8,128)(2,1)S(1)}, u32[]{:S(2)}, u32[]{:S(2)}) collective-permute-start(bf16[64,2304]{1,0:T(8,128)(2,1)S(1)} %get-tuple-element.54), channel_id=1, source_target_pairs={{0,3},{1,0},{2,1},{3,2},{4,7},{5,4},{6,5},{7,6},{8,11},{9,8},{10,9... | collective-permute-start | bytes 884744 | tf_op jit(solution)/shard_map/ppermute | solution.py:29

commit v6 on v5

--- a/solution.py
+++ b/solution.py
@@ -202,6 +202,53 @@
         ),
         name="project",
     )(place, *halves, wq, wkv, *held)
+
+
+def project_last_body(low, high, wq, wkv, out):
+    nq = wq.shape[1]
+    for k, ref in enumerate((low, high)):
+        q = jnp.dot(ref[...], wq[...], preferred_element_type=F32)
+        kv = jnp.dot(ref[...], wkv[...], preferred_element_type=F32)
+        out[2 * k : 2 * k + 2, :, :nq] = q.reshape(2, 64, nq)
+        out[2 * k : 2 * k + 2, :, nq:] = kv.reshape(2, 64, kv.shape[1])
+
+
+def project_last(low, high, wq, wkv):
+    width, nq = wq.shape
+    n = nq + wkv.shape[1]
+    return one_step(
+        project_last_body,
+        [IN_VMEM] * 4,
+        jax.ShapeDtypeStruct((4, 64, n), F32),
+        [],
+        2 * 256 * width * n,
+        256 * width * 2 + width * n * 2 + 256 * n * 4,
+        "project_last",
+    )(low, high, wq, wkv)
+
+
+def chip_sums_body(place, near, far, late, far_late, out):
+    x, y, c = place[0], place[1], place[3]
+    for slot in range(8):
+        dx = (2 * c + slot % 2 - x) & 3
+        dy = (slot // 2 - y) & 3
+        mine = jnp.where(jnp.where(c == 0, dy, dx) == 2, late[jnp.where(c == 0, dx, dy)], near[slot])
+        other = jnp.where(
+            jnp.where(c == 0, dx, dy) == 2, far_late[jnp.where(c == 0, dy, dx)], far[slot]
+        )
+        out[slot] = (mine + other) * PARTIAL_SCALE
+
+
+def chip_sums(place, near, far, late, far_late):
+    return one_step(
+        chip_sums_body,
+        [IN_SMEM] + [IN_VMEM] * 4,
+        jax.ShapeDtypeStruct(near.shape, F32),
+        [],
+        2 * near.size,
+        near.size * 16,
+        "chip_sums",
+    )(place, near, far, late, far_late)
 
 
 def attend_body(lens, x, keys_hbm, values_hbm, out, keys, values, sems):
@@ -469,8 +516,11 @@
     twice_high = send(plus_high, second_axis(-1))
     held = (held[0], near)
     halves = (plus_low, plus_high, minus_low, minus_high)
-    held = project((1, 3), place, halves, wq, wkv, held)
-    return project((2,), place, (twice_low, twice_high), wq, wkv, held)
+    far, near = project((1, 3), place, halves, wq, wkv, held)
+    near, twice_low = after(near, twice_low)
+    near, twice_high = after(near, twice_high)
+    late = project_last(twice_low, twice_high, wq, wkv)
+    return chip_sums(place, near, send(far, other_core), late, send(late, other_core))
 
 
 def per_device(tokens, norm_gain, w_query, w_kv, w_out, cache_keys, cache_values, lengths):
@@ -484,12 +534,11 @@
     wkv = lax.dynamic_slice_in_dim(w_kv, gy * piece, piece, 1)
     wkv = jnp.pad(wkv, ((0, 0), (0, 128 - piece)))
 
-    far, near = gather_and_project(
+    partial = gather_and_project(
         place, tokens.reshape(64, width), gain, w_query, wkv
     )
-    n = near.shape[-1]
-
-    partial = (near + send(far, other_core)) * PARTIAL_SCALE
+    n = partial.shape[-1]
+
     partial = exchange(partial.astype(jnp.float16).reshape(64, 8, n))
     query = jnp.sum(partial.astype(F32).reshape(4, 16, 8, n), axis=0) * (1.0 / PARTIAL_SCALE)
     mixed = attend(lengths, query.astype(BF), cache_keys, cache_values, nq)

time: 152 us -> 162 us (1.066)
  waiting for transfers between devices: 42.5 us -> 51.2 us
    ppermute x21 -> x22, waiting for transfers between devices: 34.9 us -> 43.6 us  [send(): return lax.ppermute(value, ('gx', 'gy'), flat_perm(place))]
    pallas_call x0 -> x2, Pallas kernels: none -> 2.26 us  [the longest x1 1.39 us: project_last(): one_step(project_last_body, [IN_VMEM] * 4, jax.ShapeDtypeStruct((4, 64, n...]
    pallas_call x3 -> x2, Pallas kernels: 9.09 us -> 7.66 us  [project(): pl.pallas_call(functools.partial(project_body, places), in_specs=[IN_SMEM...]
    ppermute x21 -> x22, starting transfers between devices: 27.2 us -> 26.2 us  [send(): return lax.ppermute(value, ('gx', 'gy'), flat_perm(place))]
  transfers between devices with their start and end apart: 22 -> 23, of which waited for: 14 -> 15; matrix products, arithmetic and copies ran while one was open for 1% -> 1% of each run, Pallas kernels for 8% -> 6%
where the time goes in v6:
time: 162 us; the launch traced here: 161 us
  waiting for transfers between devices  51.2 us (32%)
  blocking collectives  42.6 us (26%)
  starting transfers between devices  31.6 us (20%)
  Pallas kernels  29.4 us (18%)
  local copies, waits for them, and re-layouts  5.02 us (3%)
    ppermute x22, waiting for transfers between devices, send(): return lax.ppermute(value, ('gx', 'gy'), flat_perm(place))  43.6 us
    all_to_all x2, blocking collectives, exchange(): return lax.all_to_all(value, ('gx', 'gy'), 0, 0, axis_index_groups=groups)  42.6 us
    ppermute x22, starting transfers between devices, send(): return lax.ppermute(value, ('gx', 'gy'), flat_perm(place))  26.2 us
    pallas_call x2, Pallas kernels, project(): pl.pallas_call(functools.partial(project_body, places), in_specs=[IN_SMEM...  7.66 us
    all_to_all x1, waiting for transfers between devices, gather_and_project(): tiles = lax.all_to_all(stat, ('gx', 'gy'), 0, 0, axis_index_groups=groups)  7.59 us
    pallas_call x1, Pallas kernels, attend(): pl.pallas_call(attend_body, in_specs=[IN_SMEM, IN_VMEM, IN_HBM, IN_HBM],...  7.47 us
    all_to_all x1, starting transfers between devices, gather_and_project(): tiles = lax.all_to_all(stat, ('gx', 'gy'), 0, 0, axis_index_groups=groups)  5.45 us
    unnamed x12, local copies, waits for them, and re-layouts  3.96 us
  transfers between devices with their start and end apart: 23, of which 15 were waited for; matrix products, arithmetic and copies ran while one was open for 1% of the time, Pallas kernels for 6%

profile of v6, /device:TPU:24, one launch (start us, length us, event | category | flops | bytes accessed | tf_op | source)
XLA Modules:
  0.0 161.1 jit_solution(16376756117717138345)
XLA Ops:
  0.0 1.5 collective-permute-start.2
  1.5 2.7 %collective-permute-start.1 = (bf16[64,2304]{1,0:T(8,128)(2,1)}, bf16[64,2304]{1,0:T(8,128)(2,1)S(1)}, u32[]{:S(2)}, u32[]{:S(2)}) collective-permute-start(bf16[64,2304]{1,0:T(8,128)(2,1)} %bitcast.13), channel_id=1, source_target_pairs={{0,2},{1,3},{2,0},{3,1},{4,6},{5,7},{6,4},{7,5},{8,10},{9,11},{10,... | collective-permute-start | bytes 884744 | tf_op jit(solution)/shard_map/ppermute | solution.py:29
  4.2 1.4 collective-permute-start
  5.7 1.0 copy-done.4
  6.7 0.3 row_statistics.1.a
  7.0 0.0 collective-permute-start.3
  7.0 0.7 broadcast_in_dim.3.gain
  7.7 0.4 collective-permute-done.3.b
  8.1 0.6 chip_statistics.1
  8.8 5.4 %all-to-all-start = ((f32[16,8,128]{2,1,0:T(8,128)}), f32[16,8,128]{2,1,0:T(8,128)S(1)}, u32[]{:S(2)}, u32[]{:S(2)}) async-start(f32[16,8,128]{2,1,0:T(8,128)} %chip_statistics.1), calls=%async_computation | async-start | bytes 131072 | tf_op jit(solution)/shard_map/all_to_all | solution.py:506
  14.2 0.1 pad_add_fusion.place
  14.3 7.6 %all-to-all-done.tiles = f32[16,8,128]{2,1,0:T(8,128)S(1)} async-done(((f32[16,8,128]{2,1,0:T(8,128)}), f32[16,8,128]{2,1,0:T(8,128)S(1)}, u32[]{:S(2)}, u32[]{:S(2)}) %all-to-all-start) | async-done | bytes 65568 | tf_op jit(solution)/shard_map/all_to_all | solution.py:506
  21.9 0.0 collective-permute-done.2.b3
  21.9 0.0 copy-start.5
  21.9 1.0 copy-done.5
  22.9 2.3 %normalise.1 = (bf16[128,2304]{1,0:T(8,128)(2,1)}, bf16[128,2304]{1,0:T(8,128)(2,1)}) custom-call(s32[4]{0:T(128)S(1)} %pad_add_fusion.place, bf16[64,2304]{1,0:T(8,128)(2,1)S(1)} %bitcast.16, bf16[64,2304]{1,0:T(8,128)(2,1)S(1)} %collective-permute-done.b1, bf16[64,2304]{1,0:T(8,128)(2,1)S(1)} %collective-permute-done.1.b2, ...), custom_call_target="tpu_custom_call" | custom-call | flops 3538944 | bytes 2359296 | tf_op jit(solution)/shard_map/normalise/pallas_call | solution.py:150
  25.2 1.5 collective-permute-start.5
  26.7 0.5 collective-permute-start.6
  27.2 0.7 collective-permute-start.4
  27.9 2.5 %collective-permute-start.7 = (bf16[128,2304]{1,0:T(8,128)(2,1)}, bf16[128,2304]{1,0:T(8,128)(2,1)}, u32[]{:S(2)}, u32[]{:S(2)}) collective-permute-start(bf16[128,2304]{1,0:T(8,128)(2,1)} %get-tuple-element.33.refs_1_), channel_id=1, source_target_pairs={{0,4},{1,5},{2,6},{3,7},{4,8},{5,9},{6,10},{7,11},{8,12},{9,13},{1... | collective-permute-start | bytes 1769480 | tf_op jit(solution)/shard_map/ppermute | solution.py:29
  30.4 0.2 constant_dynamic-slice_fusion
  30.7 0.1 pad.4.refs_3_.refs_5_.wkv
  30.8 0.0 copy-start.1
  30.8 2.0 %copy-done.1 = bf16[2304,768]{1,0:T(8,128)(2,1)S(1)} copy-done((bf16[2304,768]{1,0:T(8,128)(2,1)S(1)}, bf16[2304,768]{1,0:T(8,128)(2,1)}, u32[]{:S(2)}) %copy-start.1) | copy-done | bytes 3538968
  32.8 3.1 %project.2 = (f32[8,64,896]{2,1,0:T(8,128)S(1)}, f32[8,64,896]{2,1,0:T(8,128)S(1)}) custom-call(s32[4]{0:T(128)S(1)} %pad_add_fusion.place, bf16[128,2304]{1,0:T(8,128)(2,1)} %get-tuple-element.32.refs_0_, bf16[128,2304]{1,0:T(8,128)(2,1)} %get-tuple-element.33.refs_1_, bf16[2304,768]{1,0:T(8,128)(2,1)S(1)} %copy-done.1, ...), custom_call_target="tpu_custom_call" | custom-call | flops 1056964608 | bytes 6225920 | tf_op jit(solution)/shard_map/project/pallas_call | solution.py:191
  35.9 2.1 %collective-permute-done.6.refs_1_ = bf16[128,2304]{1,0:T(8,128)(2,1)S(1)} collective-permute-done((bf16[128,2304]{1,0:T(8,128)(2,1)}, bf16[128,2304]{1,0:T(8,128)(2,1)S(1)}, u32[]{:S(2)}, u32[]{:S(2)}) %collective-permute-start.6) | collective-permute-done | bytes 589856 | tf_op jit(solution)/shard_map/ppermute | solution.py:29
  38.0 6.4 %collective-permute-done.4.refs_0_ = bf16[128,2304]{1,0:T(8,128)(2,1)} collective-permute-done((bf16[128,2304]{1,0:T(8,128)(2,1)}, bf16[128,2304]{1,0:T(8,128)(2,1)}, u32[]{:S(2)}, u32[]{:S(2)}) %collective-permute-start.4) | collective-permute-done | bytes 589856 | tf_op jit(solution)/shard_map/ppermute | solution.py:29
  44.4 4.6 %project.3 = (f32[8,64,896]{2,1,0:T(8,128)S(1)}, f32[8,64,896]{2,1,0:T(8,128)S(1)}) custom-call(s32[4]{0:T(128)S(1)} %pad_add_fusion.place, bf16[128,2304]{1,0:T(8,128)(2,1)} %collective-permute-done.4.refs_0_, bf16[128,2304]{1,0:T(8,128)(2,1)S(1)} %collective-permute-done.6.refs_1_, ...), custom_call_target="tpu_custom_call", output_to_operand_aliasing={{0}: (7, {}), {1}: (8, {})} | custom-call | flops 2113929216 | bytes 8323072 | tf_op jit(solution)/shard_map/project/pallas_call | solution.py:191
  49.0 0.1 collective-permute-start.10
  49.1 0.1 collective-permute-start.8
  49.2 2.0 %collective-permute-start.9 = (bf16[128,2304]{1,0:T(8,128)(2,1)S(1)}, bf16[128,2304]{1,0:T(8,128)(2,1)S(1)}, u32[]{:S(2)}, u32[]{:S(2)}) collective-permute-start(bf16[128,2304]{1,0:T(8,128)(2,1)S(1)} %collective-permute-done.6.refs_1_), channel_id=1, source_target_pairs={{0,12},{1,13},{2,14},{3,15},{4,0},{5,1},{6,2},{7,3},{8,4},{9,5},{1... | collective-permute-start | bytes 1769480 | tf_op jit(solution)/shard_map/ppermute | solution.py:29
  51.2 7.9 %collective-permute-done.8.low = bf16[128,2304]{1,0:T(8,128)(2,1)S(1)} collective-permute-done((bf16[128,2304]{1,0:T(8,128)(2,1)S(1)}, bf16[128,2304]{1,0:T(8,128)(2,1)S(1)}, u32[]{:S(2)}, u32[]{:S(2)}) %collective-permute-start.8) | collective-permute-done | bytes 589856 | tf_op jit(solution)/shard_map/ppermute | solution.py:29
  59.1 1.3 collective-permute-done.9.high
  60.4 1.4 project_last.1.late
  61.8 0.3 collective-permute-start.11
  62.0 2.5 %collective-permute-done.11.far_late = f32[4,64,896]{2,1,0:T(8,128)S(1)} collective-permute-done((f32[4,64,896]{2,1,0:T(8,128)S(1)}, f32[4,64,896]{2,1,0:T(8,128)S(1)}, u32[]{:S(2)}, u32[]{:S(2)}) %collective-permute-start.11) | collective-permute-done | bytes 917536 | tf_op jit(solution)/shard_map/ppermute | solution.py:29
  64.5 0.9 chip_sums.1
  65.4 0.1 convert_element_type.9
  65.5 22.4 %all_to_all.15 = f16[64,8,896]{2,1,0:T(8,128)(2,1)S(1)} all-to-all(f16[64,8,896]{2,1,0:T(8,128)(2,1)S(1)} %bitcast.18), channel_id=1, replica_groups={{0,1,2,3,4,5,6,7,8,9,10,11,12,13,14,15,32,33,34,35,36,37,38,39,40,41,42..., dimensions={0} | all-to-all | bytes 1835008 | tf_op jit(solution)/shard_map/all_to_all | solution.py:50
  87.9 0.1 convert_reduce_fusion
  88.0 0.7 multiply_convert_fusion.x
  88.8 7.5 %attend.1 = bf16[4,16,8,768]{3,2,1,0:T(8,128)(2,1)} custom-call(s32[4]{0:T(128)} %lens.1, bf16[16,8,896]{2,1,0:T(8,128)(2,1)} %multiply_convert_fusion.x, bf16[4,2048,256]{2,1,0:T(8,128)(2,1)} %keys_hbm.1, bf16[4,2048,256]{2,1,0:T(8,128)(2,1)} %values_hbm.1), custom_call_target="tpu_custom_call" | custom-call | flops 805306368 | bytes 8388608 | tf_op jit(solution)/shard_map/attend/pallas_call | solution.py:340
  96.2 20.2 %all_to_all.16 = bf16[64,8,768]{2,1,0:T(8,128)(2,1)S(1)} all-to-all(bf16[64,8,768]{2,1,0:T(8,128)(2,1)} %bitcast.19), channel_id=1, replica_groups={{0,1,2,3,4,5,6,7,8,9,10,11,12,13,14,15,32,33,34,35,36,37,38,39,40,41,42..., dimensions={0} | all-to-all | bytes 1572864 | tf_op jit(solution)/shard_map/all_to_all | solution.py:50
  116.4 2.3 %collective-permute-done.12.cross = bf16[4,16,8,768]{3,2,1,0:T(8,128)(2,1)S(1)} collective-permute-done((bf16[4,16,8,768]{3,2,1,0:T(8,128)(2,1)S(1)}, bf16[4,16,8,768]{3,2,1,0:T(8,128)(2,1)S(1)}, u32[]{:S(2)}, u32[]{:S(2)}) %collective-permute-start.12) | collective-permute-done | bytes 786464 | tf_op jit(solution)/shard_map/ppermute | solution.py:29
  118.7 1.7 %output_far.1 = (bf16[16,64,768]{2,1,0:T(8,128)(2,1)S(1)}, bf16[128,2304]{1,0:T(8,128)(2,1)S(1)}, bf16[128,2304]{1,0:T(8,128)(2,1)S(1)}) custom-call(s32[4]{0:T(128)S(1)} %pad_add_fusion.place, bf16[4,16,8,768]{3,2,1,0:T(8,128)(2,1)S(1)} %bitcast.11, bf16[4,16,8,768]{3,2,1,0:T(8,128)(2,1)S(1)} %collective-permute-done.12.cross, bf16[768,2304]{1,0:T(8,128)(2,1)S(1)} %copy-done.3), custom_call_target="tpu_custom_call" | custom-call | flops 905969664 | bytes 7864320 | tf_op jit(solution)/shard_map/output_far/pallas_call | solution.py:386
  120.5 2.9 %collective-permute-start.13 = (bf16[128,2304]{1,0:T(8,128)(2,1)S(1)}, bf16[128,2304]{1,0:T(8,128)(2,1)S(1)}, u32[]{:S(2)}, u32[]{:S(2)}) collective-permute-start(bf16[128,2304]{1,0:T(8,128)(2,1)S(1)} %get-tuple-element.48), channel_id=1, source_target_pairs={{0,4},{1,5},{2,6},{3,7},{4,8},{5,9},{6,10},{7,11},{8,12},{9,13},{1... | collective-permute-start | bytes 1769480 | tf_op jit(solution)/shard_map/ppermute | solution.py:29
  123.3 2.6 %output_near.1 = (bf16[128,2304]{1,0:T(8,128)(2,1)S(1)}, bf16[128,2304]{1,0:T(8,128)(2,1)S(1)}, bf16[128,2304]{1,0:T(8,128)(2,1)S(1)}, bf16[128,2304]{1,0:T(8,128)(2,1)S(1)}) custom-call(s32[4]{0:T(128)S(1)} %pad_add_fusion.place, bf16[16,64,768]{2,1,0:T(8,128)(2,1)S(1)} %get-tuple-element.46.left, bf16[768,2304]{1,0:T(8,128)(2,1)S(1)} %copy-done.3), custom_call_target="tpu_custom_call" | custom-call | flops 1811939328 | bytes 7471104 | tf_op jit(solution)/shard_map/output_near/pallas_call | solution.py:404
  125.9 3.3 %collective-permute-start.16 = (bf16[128,2304]{1,0:T(8,128)(2,1)S(1)}, bf16[128,2304]{1,0:T(8,128)(2,1)S(1)}, u32[]{:S(2)}, u32[]{:S(2)}) collective-permute-start(bf16[128,2304]{1,0:T(8,128)(2,1)S(1)} %get-tuple-element.52), channel_id=1, source_target_pairs={{0,4},{1,5},{2,6},{3,7},{4,8},{5,9},{6,10},{7,11},{8,12},{9,13},{1... | collective-permute-start | bytes 1769480 | tf_op jit(solution)/shard_map/ppermute | solution.py:29
  129.2 1.5 collective-permute-done.13.a1
  130.7 3.7 %collective-permute-done.14.b1 = bf16[128,2304]{1,0:T(8,128)(2,1)S(1)} collective-permute-done((bf16[128,2304]{1,0:T(8,128)(2,1)S(1)}, bf16[128,2304]{1,0:T(8,128)(2,1)S(1)}, u32[]{:S(2)}, u32[]{:S(2)}) %collective-permute-start.14) | collective-permute-done | bytes 589856 | tf_op jit(solution)/shard_map/ppermute | solution.py:29
  134.4 0.3 pair_add.1
  134.7 0.1 collective-permute-start.15
  134.8 2.0 %collective-permute-start.18 = (bf16[128,2304]{1,0:T(8,128)(2,1)S(1)}, bf16[128,2304]{1,0:T(8,128)(2,1)S(1)}, u32[]{:S(2)}, u32[]{:S(2)}) collective-permute-start(bf16[128,2304]{1,0:T(8,128)(2,1)S(1)} %get-tuple-element.54), channel_id=1, source_target_pairs={{0,12},{1,13},{2,14},{3,15},{4,0},{5,1},{6,2},{7,3},{8,4},{9,5},{1... | collective-permute-start | bytes 1769480 | tf_op jit(solution)/shard_map/ppermute | solution.py:29
  136.8 1.6 %output_own.1.a = bf16[256,2304]{1,0:T(8,128)(2,1)S(1)} custom-call(s32[4]{0:T(128)S(1)} %pad_add_fusion.place, bf16[16,64,768]{2,1,0:T(8,128)(2,1)S(1)} %get-tuple-element.46.left, bf16[768,2304]{1,0:T(8,128)(2,1)S(1)} %copy-done.3), custom_call_target="tpu_custom_call" | custom-call | flops 905969664 | bytes 6291456 | tf_op jit(solution)/shard_map/output_own/pallas_call | solution.py:421
  138.4 2.3 %collective-permute-done.17.c0 = bf16[128,2304]{1,0:T(8,128)(2,1)S(1)} collective-permute-done((bf16[128,2304]{1,0:T(8,128)(2,1)S(1)}, bf16[128,2304]{1,0:T(8,128)(2,1)S(1)}, u32[]{:S(2)}, u32[]{:S(2)}) %collective-permute-start.17) | collective-permute-done | bytes 589856 | tf_op jit(solution)/shard_map/ppermute | solution.py:29
  140.7 3.9 %collective-permute-done.15.b0 = bf16[128,2304]{1,0:T(8,128)(2,1)S(1)} collective-permute-done((bf16[128,2304]{1,0:T(8,128)(2,1)S(1)}, bf16[128,2304]{1,0:T(8,128)(2,1)S(1)}, u32[]{:S(2)}, u32[]{:S(2)}) %collective-permute-start.15) | collective-permute-done | bytes 589856 | tf_op jit(solution)/shard_map/ppermute | solution.py:29
  144.6 2.4 %collective-permute-done.18.c1 = bf16[128,2304]{1,0:T(8,128)(2,1)S(1)} collective-permute-done((bf16[128,2304]{1,0:T(8,128)(2,1)S(1)}, bf16[128,2304]{1,0:T(8,128)(2,1)S(1)}, u32[]{:S(2)}, u32[]{:S(2)}) %collective-permute-start.18) | collective-permute-done | bytes 589856 | tf_op jit(solution)/shard_map/ppermute | solution.py:29
  147.1 1.0 group_sum.1
  148.1 1.3 collective-permute-start.19
  149.4 0.5 collective-permute-start.20
  149.9 2.7 %collective-permute-start.21 = (bf16[64,2304]{1,0:T(8,128)(2,1)S(1)}, bf16[64,2304]{1,0:T(8,128)(2,1)S(1)}, u32[]{:S(2)}, u32[]{:S(2)}) collective-permute-start(bf16[64,2304]{1,0:T(8,128)(2,1)S(1)} %get-tuple-element.58), channel_id=1, source_target_pairs={{0,3},{1,0},{2,1},{3,2},{4,7},{5,4},{6,5},{7,6},{8,11},{9,8},{10,9... | collective-permute-start | bytes 884744 | tf_op jit(solution)/shard_map/ppermute | solution.py:29
  152.6 3.9 %collective-permute-done.19.r1 = bf16[64,2304]{1,0:T(8,128)(2,1)S(1)} collective-permute-done((bf16[64,2304]{1,0:T(8,128)(2,1)S(1)}, bf16[64,2304]{1,0:T(8,128)(2,1)S(1)}, u32[]{:S(2)}, u32[]{:S(2)}) %collective-permute-start.19) | collective-permute-done | bytes 294944 | tf_op jit(solution)/shard_map/ppermute | solution.py:29
  156.5 3.1 %collective-permute-done.20.r2 = bf16[64,2304]{1,0:T(8,128)(2,1)S(1)} collective-permute-done((bf16[64,2304]{1,0:T(8,128)(2,1)S(1)}, bf16[64,2304]{1,0:T(8,128)(2,1)S(1)}, u32[]{:S(2)}, u32[]{:S(2)}) %collective-permute-start.20) | collective-permute-done | bytes 294944 | tf_op jit(solution)/shard_map/ppermute | solution.py:29
  159.6 1.6 last_sum.1
  (17 shorter events, 0.0 us)
Async XLA Ops:
  0.0 30.4 %copy-start = (bf16[2304,512]{1,0:T(8,128)(2,1)S(1)}, bf16[2304,512]{1,0:T(8,128)(2,1)}, u32[]{:S(2)}) copy-start(bf16[2304,512]{1,0:T(8,128)(2,1)} %param.11) | copy-start | bytes 7077892
  0.0 21.9 %collective-permute-start.2 = (bf16[64,2304]{1,0:T(8,128)(2,1)}, bf16[64,2304]{1,0:T(8,128)(2,1)S(1)}, u32[]{:S(2)}, u32[]{:S(2)}) collective-permute-start(bf16[64,2304]{1,0:T(8,128)(2,1)} %bitcast.12), channel_id=1, source_target_pairs={{0,1},{1,2},{2,3},{3,0},{4,5},{5,6},{6,7},{7,4},{8,9},{9,10},{10,1... | collective-permute-start | bytes 884744 | tf_op jit(solution)/shard_map/ppermute | solution.py:29
  1.5 20.4 %collective-permute-start.1 = (bf16[64,2304]{1,0:T(8,128)(2,1)}, bf16[64,2304]{1,0:T(8,128)(2,1)S(1)}, u32[]{:S(2)}, u32[]{:S(2)}) collective-permute-start(bf16[64,2304]{1,0:T(8,128)(2,1)} %bitcast.13), channel_id=1, source_target_pairs={{0,2},{1,3},{2,0},{3,1},{4,6},{5,7},{6,4},{7,5},{8,10},{9,11},{10,... | collective-permute-start | bytes 884744 | tf_op jit(solution)/shard_map/ppermute | solution.py:29
  4.2 17.7 %collective-permute-start = (bf16[64,2304]{1,0:T(8,128)(2,1)}, bf16[64,2304]{1,0:T(8,128)(2,1)S(1)}, u32[]{:S(2)}, u32[]{:S(2)}) collective-permute-start(bf16[64,2304]{1,0:T(8,128)(2,1)} %bitcast.14), channel_id=1, source_target_pairs={{0,3},{1,0},{2,1},{3,2},{4,7},{5,4},{6,5},{7,6},{8,11},{9,8},{10,9... | collective-permute-start | bytes 884744 | tf_op jit(solution)/shard_map/ppermute | solution.py:29
  5.7 1.0 copy-start.4
  7.0 1.2 collective-permute-start.3
  8.8 13.1 %all-to-all-start = ((f32[16,8,128]{2,1,0:T(8,128)}), f32[16,8,128]{2,1,0:T(8,128)S(1)}, u32[]{:S(2)}, u32[]{:S(2)}) async-start(f32[16,8,128]{2,1,0:T(8,128)} %chip_statistics.1), calls=%async_computation | async-start | bytes 131072 | tf_op jit(solution)/shard_map/all_to_all | solution.py:506
  21.9 1.0 copy-start.5
  25.2 10.7 %collective-permute-start.5 = (bf16[128,2304]{1,0:T(8,128)(2,1)}, bf16[128,2304]{1,0:T(8,128)(2,1)S(1)}, u32[]{:S(2)}, u32[]{:S(2)}) collective-permute-start(bf16[128,2304]{1,0:T(8,128)(2,1)} %get-tuple-element.32.refs_0_), channel_id=1, source_target_pairs={{0,4},{1,5},{2,6},{3,7},{4,8},{5,9},{6,10},{7,11},{8,12},{9,13},{1... | collective-permute-start | bytes 1769480 | tf_op jit(solution)/shard_map/ppermute | solution.py:29
  26.7 11.3 %collective-permute-start.6 = (bf16[128,2304]{1,0:T(8,128)(2,1)}, bf16[128,2304]{1,0:T(8,128)(2,1)S(1)}, u32[]{:S(2)}, u32[]{:S(2)}) collective-permute-start(bf16[128,2304]{1,0:T(8,128)(2,1)} %get-tuple-element.33.refs_1_), channel_id=1, source_target_pairs={{0,12},{1,13},{2,14},{3,15},{4,0},{5,1},{6,2},{7,3},{8,4},{9,5},{1... | collective-permute-start | bytes 1769480 | tf_op jit(solution)/shard_map/ppermute | solution.py:29
  27.2 17.2 %collective-permute-start.4 = (bf16[128,2304]{1,0:T(8,128)(2,1)}, bf16[128,2304]{1,0:T(8,128)(2,1)}, u32[]{:S(2)}, u32[]{:S(2)}) collective-permute-start(bf16[128,2304]{1,0:T(8,128)(2,1)} %get-tuple-element.32.refs_0_), channel_id=1, source_target_pairs={{0,12},{1,13},{2,14},{3,15},{4,0},{5,1},{6,2},{7,3},{8,4},{9,5},{1... | collective-permute-start | bytes 1769480 | tf_op jit(solution)/shard_map/ppermute | solution.py:29
  27.9 16.5 %collective-permute-start.7 = (bf16[128,2304]{1,0:T(8,128)(2,1)}, bf16[128,2304]{1,0:T(8,128)(2,1)}, u32[]{:S(2)}, u32[]{:S(2)}) collective-permute-start(bf16[128,2304]{1,0:T(8,128)(2,1)} %get-tuple-element.33.refs_1_), channel_id=1, source_target_pairs={{0,4},{1,5},{2,6},{3,7},{4,8},{5,9},{6,10},{7,11},{8,12},{9,13},{1... | collective-permute-start | bytes 1769480 | tf_op jit(solution)/shard_map/ppermute | solution.py:29
  30.8 2.0 %copy-start.1 = (bf16[2304,768]{1,0:T(8,128)(2,1)S(1)}, bf16[2304,768]{1,0:T(8,128)(2,1)}, u32[]{:S(2)}) copy-start(bf16[2304,768]{1,0:T(8,128)(2,1)} %wq.1) | copy-start | bytes 10616836
  32.8 11.6 %copy-start.2 = (bf16[2304,768]{1,0:T(8,128)(2,1)S(1)}, bf16[2304,768]{1,0:T(8,128)(2,1)}, u32[]{:S(2)}) copy-start(bf16[2304,768]{1,0:T(8,128)(2,1)} %wq.1) | copy-start | bytes 10616836
  49.0 15.5 %collective-permute-start.10 = (f32[8,64,896]{2,1,0:T(8,128)S(1)}, f32[8,64,896]{2,1,0:T(8,128)S(1)}, u32[]{:S(2)}, u32[]{:S(2)}) collective-permute-start(f32[8,64,896]{2,1,0:T(8,128)S(1)} %get-tuple-element.43), channel_id=1, source_target_pairs={{0,16},{1,17},{2,18},{3,19},{4,20},{5,21},{6,22},{7,23},{8,24},{9,... | collective-permute-start | bytes 5505032 | tf_op jit(solution)/shard_map/ppermute | solution.py:29
  49.1 10.0 %collective-permute-start.8 = (bf16[128,2304]{1,0:T(8,128)(2,1)S(1)}, bf16[128,2304]{1,0:T(8,128)(2,1)S(1)}, u32[]{:S(2)}, u32[]{:S(2)}) collective-permute-start(bf16[128,2304]{1,0:T(8,128)(2,1)S(1)} %collective-permute-done.5.refs_2_), channel_id=1, source_target_pairs={{0,4},{1,5},{2,6},{3,7},{4,8},{5,9},{6,10},{7,11},{8,12},{9,13},{1... | collective-permute-start | bytes 1769480 | tf_op jit(solution)/shard_map/ppermute | solution.py:29
  49.2 11.2 %collective-permute-start.9 = (bf16[128,2304]{1,0:T(8,128)(2,1)S(1)}, bf16[128,2304]{1,0:T(8,128)(2,1)S(1)}, u32[]{:S(2)}, u32[]{:S(2)}) collective-permute-start(bf16[128,2304]{1,0:T(8,128)(2,1)S(1)} %collective-permute-done.6.refs_1_), channel_id=1, source_target_pairs={{0,12},{1,13},{2,14},{3,15},{4,0},{5,1},{6,2},{7,3},{8,4},{9,5},{1... | collective-permute-start | bytes 1769480 | tf_op jit(solution)/shard_map/ppermute | solution.py:29
  61.8 2.7 %collective-permute-start.11 = (f32[4,64,896]{2,1,0:T(8,128)S(1)}, f32[4,64,896]{2,1,0:T(8,128)S(1)}, u32[]{:S(2)}, u32[]{:S(2)}) collective-permute-start(f32[4,64,896]{2,1,0:T(8,128)S(1)} %project_last.1.late), channel_id=1, source_target_pairs={{0,16},{1,17},{2,18},{3,19},{4,20},{5,21},{6,22},{7,23},{8,24},{9,... | collective-permute-start | bytes 2752520 | tf_op jit(solution)/shard_map/ppermute | solution.py:29
  88.8 30.0 %copy-start.3 = (bf16[768,2304]{1,0:T(8,128)(2,1)S(1)}, bf16[768,2304]{1,0:T(8,128)(2,1)}, u32[]{:S(2)}) copy-start(bf16[768,2304]{1,0:T(8,128)(2,1)} %w_out.5) | copy-start | bytes 10616836
  116.4 2.3 %collective-permute-start.12 = (bf16[4,16,8,768]{3,2,1,0:T(8,128)(2,1)S(1)}, bf16[4,16,8,768]{3,2,1,0:T(8,128)(2,1)S(1)}, u32[]{:S(2)}, u32[]{:S(2)}) collective-permute-start(bf16[4,16,8,768]{3,2,1,0:T(8,128)(2,1)S(1)} %bitcast.10), channel_id=1, source_target_pairs={{0,16},{1,17},{2,18},{3,19},{4,20},{5,21},{6,22},{7,23},{8,24},{9,... | collective-permute-start | bytes 2359304 | tf_op jit(solution)/shard_map/ppermute | solution.py:29
  120.5 10.3 %collective-permute-start.13 = (bf16[128,2304]{1,0:T(8,128)(2,1)S(1)}, bf16[128,2304]{1,0:T(8,128)(2,1)S(1)}, u32[]{:S(2)}, u32[]{:S(2)}) collective-permute-start(bf16[128,2304]{1,0:T(8,128)(2,1)S(1)} %get-tuple-element.48), channel_id=1, source_target_pairs={{0,4},{1,5},{2,6},{3,7},{4,8},{5,9},{6,10},{7,11},{8,12},{9,13},{1... | collective-permute-start | bytes 1769480 | tf_op jit(solution)/shard_map/ppermute | solution.py:29
  123.3 11.1 %collective-permute-start.14 = (bf16[128,2304]{1,0:T(8,128)(2,1)S(1)}, bf16[128,2304]{1,0:T(8,128)(2,1)S(1)}, u32[]{:S(2)}, u32[]{:S(2)}) collective-permute-start(bf16[128,2304]{1,0:T(8,128)(2,1)S(1)} %get-tuple-element.50), channel_id=1, source_target_pairs={{0,12},{1,13},{2,14},{3,15},{4,0},{5,1},{6,2},{7,3},{8,4},{9,5},{1... | collective-permute-start | bytes 1769480 | tf_op jit(solution)/shard_map/ppermute | solution.py:29
  125.9 12.5 %collective-permute-start.16 = (bf16[128,2304]{1,0:T(8,128)(2,1)S(1)}, bf16[128,2304]{1,0:T(8,128)(2,1)S(1)}, u32[]{:S(2)}, u32[]{:S(2)}) collective-permute-start(bf16[128,2304]{1,0:T(8,128)(2,1)S(1)} %get-tuple-element.52), channel_id=1, source_target_pairs={{0,4},{1,5},{2,6},{3,7},{4,8},{5,9},{6,10},{7,11},{8,12},{9,13},{1... | collective-permute-start | bytes 1769480 | tf_op jit(solution)/shard_map/ppermute | solution.py:29
  129.2 11.5 %collective-permute-start.17 = (bf16[128,2304]{1,0:T(8,128)(2,1)S(1)}, bf16[128,2304]{1,0:T(8,128)(2,1)S(1)}, u32[]{:S(2)}, u32[]{:S(2)}) collective-permute-start(bf16[128,2304]{1,0:T(8,128)(2,1)S(1)} %get-tuple-element.53), channel_id=1, source_target_pairs={{0,12},{1,13},{2,14},{3,15},{4,0},{5,1},{6,2},{7,3},{8,4},{9,5},{1... | collective-permute-start | bytes 1769480 | tf_op jit(solution)/shard_map/ppermute | solution.py:29
  134.7 10.0 %collective-permute-start.15 = (bf16[128,2304]{1,0:T(8,128)(2,1)S(1)}, bf16[128,2304]{1,0:T(8,128)(2,1)S(1)}, u32[]{:S(2)}, u32[]{:S(2)}) collective-permute-start(bf16[128,2304]{1,0:T(8,128)(2,1)S(1)} %get-tuple-element.51), channel_id=1, source_target_pairs={{0,4},{1,5},{2,6},{3,7},{4,8},{5,9},{6,10},{7,11},{8,12},{9,13},{1... | collective-permute-start | bytes 1769480 | tf_op jit(solution)/shard_map/ppermute | solution.py:29
  134.8 12.3 %collective-permute-start.18 = (bf16[128,2304]{1,0:T(8,128)(2,1)S(1)}, bf16[128,2304]{1,0:T(8,128)(2,1)S(1)}, u32[]{:S(2)}, u32[]{:S(2)}) collective-permute-start(bf16[128,2304]{1,0:T(8,128)(2,1)S(1)} %get-tuple-element.54), channel_id=1, source_target_pairs={{0,12},{1,13},{2,14},{3,15},{4,0},{5,1},{6,2},{7,3},{8,4},{9,5},{1... | collective-permute-start | bytes 1769480 | tf_op jit(solution)/shard_map/ppermute | solution.py:29
  148.1 8.4 %collective-permute-start.19 = (bf16[64,2304]{1,0:T(8,128)(2,1)S(1)}, bf16[64,2304]{1,0:T(8,128)(2,1)S(1)}, u32[]{:S(2)}, u32[]{:S(2)}) collective-permute-start(bf16[64,2304]{1,0:T(8,128)(2,1)S(1)} %get-tuple-element.56), channel_id=1, source_target_pairs={{0,2},{1,3},{2,0},{3,1},{4,6},{5,7},{6,4},{7,5},{8,10},{9,11},{10,... | collective-permute-start | bytes 884744 | tf_op jit(solution)/shard_map/ppermute | solution.py:29
  149.4 10.2 %collective-permute-start.20 = (bf16[64,2304]{1,0:T(8,128)(2,1)S(1)}, bf16[64,2304]{1,0:T(8,128)(2,1)S(1)}, u32[]{:S(2)}, u32[]{:S(2)}) collective-permute-start(bf16[64,2304]{1,0:T(8,128)(2,1)S(1)} %get-tuple-element.57), channel_id=1, source_target_pairs={{0,1},{1,2},{2,3},{3,0},{4,5},{5,6},{6,7},{7,4},{8,9},{9,10},{10,1... | collective-permute-start | bytes 884744 | tf_op jit(solution)/shard_map/ppermute | solution.py:29
  149.9 9.6 %collective-permute-start.21 = (bf16[64,2304]{1,0:T(8,128)(2,1)S(1)}, bf16[64,2304]{1,0:T(8,128)(2,1)S(1)}, u32[]{:S(2)}, u32[]{:S(2)}) collective-permute-start(bf16[64,2304]{1,0:T(8,128)(2,1)S(1)} %get-tuple-element.58), channel_id=1, source_target_pairs={{0,3},{1,0},{2,1},{3,2},{4,7},{5,4},{6,5},{7,6},{8,11},{9,8},{10,9... | collective-permute-start | bytes 884744 | tf_op jit(solution)/shard_map/ppermute | solution.py:29
